TPU v7x, 32 devices: a whole 2x2x4 slice. The times are simulated.
32 devices in a mesh: dp: 8 (over z, x), fsdp: 4 (over y, core).
Axes of the slice: x: 2, y: 2, z: 4, core: 2. Of those that a mesh axis runs over, the one named last changes fastest.
Arguments:
- hidden_states: bfloat16 [4096, 8192], P(('dp', 'fsdp')), may hold values from -450 to 450
- gain: float32 [8192], replicated, may hold values from 0.1 to 1.9
- key_weight: bfloat16 [8192, 512], P('fsdp'), may hold values from -0.0625 to 0.0625
- key_cotangent: bfloat16 [4096, 512], P(('dp', 'fsdp')), may hold values from -18 to 18
- bucket: int32 [5, 32768], P(None, 'fsdp'), may hold values from 0 to 255
- sign_bits: int32 [5, 32768], P(None, 'fsdp'), may hold values from 0 to 1
- momentum: float32 [4, 5, 32768], P('fsdp', None, 'dp'), may hold values from -12 to 12
- error: float32 [4, 5, 32768], P('fsdp', None, 'dp'), may hold values from -12 to 12
Outputs:
- hidden_grad: bfloat16 [4096, 8192], P(('dp', 'fsdp'))
- momentum_new: float32 [4, 5, 32768], P('fsdp', None, 'dp')
- error_new: float32 [4, 5, 32768], P('fsdp', None, 'dp')
- update: float32 [8192, 512], P('fsdp')
All inputs are finite; a program needn't handle non-finite values.
Results may differ from a plain program's by a relative error of at most 0.0095.
Values may be sent and summed in bfloat16 or wider, within the bound.
No kernel may reach another device: no remote copies, remote signals or barrier semaphores. Data moves between devices by JAX's collectives and lax.ppermute only.
A program may use at most 128 MiB of HBM per device.

v0:
```python
import math

import jax
import jax.numpy as jnp
from jax import lax
from jax.sharding import PartitionSpec as P

ROWS = 5
NBB = 256
BLOCK = 128


EPS = 1e-05
DECAY = 0.9
THRESHOLD = 1.0


def normalize(states, gain):
    values = states.astype(jnp.float32)
    inverse_rms = lax.rsqrt(jnp.mean(values * values, axis=1, keepdims=True) + EPS)
    normed = values * inverse_rms
    return (normed, inverse_rms, (normed * gain).astype(jnp.bfloat16))


def norm_backward(input_grad, gain, normed, inverse_rms):
    scaled = input_grad.astype(jnp.float32) * gain
    mean_term = jnp.mean(scaled * normed, axis=1, keepdims=True)
    return (inverse_rms * (scaled - normed * mean_term)).astype(jnp.bfloat16)


def split_product(selector, values, numbers):
    upper = values.astype(jnp.bfloat16)
    lower = (values - upper.astype(jnp.float32)).astype(jnp.bfloat16)
    first = lax.dot_general(selector, upper, numbers, preferred_element_type=jnp.float32)
    return first + lax.dot_general(selector, lower, numbers, preferred_element_type=jnp.float32)


def middle_three(first, second, third):
    return jnp.maximum(jnp.minimum(first, second), jnp.minimum(jnp.maximum(first, second), third))


def middle_five(items):
    upper_pair = jnp.minimum(jnp.maximum(items[0], items[1]), jnp.maximum(items[2], items[3]))
    lower_pair = jnp.maximum(jnp.minimum(items[0], items[1]), jnp.minimum(items[2], items[3]))
    return middle_three(items[4], upper_pair, lower_pair)


def on_device(hidden_states, gain, key_weight, key_cotangent, bucket, sign_bits, momentum, error):
    normed, inverse_rms, inputs = normalize(hidden_states, gain)
    fsdp_count = lax.axis_size("fsdp")
    dp_count = lax.axis_size("dp")
    local_rows = key_weight.shape[0]
    grad_scale = 1.0 / math.sqrt(inputs.shape[0] * fsdp_count)
    contract_last = (((1,), (1,)), ((), ()))
    contract_first = (((0,), (0,)), ((), ()))
    contract_plain = (((1,), (0,)), ((), ()))
    all_cotangents = lax.all_gather(key_cotangent, "fsdp", axis=0, tiled=True)
    input_cols = lax.all_to_all(inputs, "fsdp", split_axis=1, concat_axis=0, tiled=True)
    weight_grad = lax.dot_general(
        input_cols, all_cotangents, contract_first, preferred_element_type=jnp.float32
    )
    grad_part = lax.dot_general(
        all_cotangents, key_weight, contract_last, preferred_element_type=jnp.float32
    ).astype(jnp.bfloat16)
    input_grad = lax.all_to_all(grad_part, "fsdp", split_axis=0, concat_axis=1, tiled=True)
    hidden_grad = norm_backward(input_grad, gain, normed, inverse_rms)
    blocks = (weight_grad * grad_scale).reshape(-1, BLOCK)
    signs = (2 * sign_bits - 1).astype(jnp.bfloat16)
    sign_values = (2 * sign_bits - 1).astype(jnp.float32)
    zero_sel = jnp.zeros((), jnp.bfloat16)
    bucket_ids = lax.broadcasted_iota(jnp.int32, (NBB, 1), 0)
    local_table = jnp.stack(
        [
            split_product(
                jnp.where(
                    bucket[row_index][None, :] == bucket_ids, signs[row_index][None, :], zero_sel
                ),
                blocks,
                contract_plain,
            )
            for row_index in range(ROWS)
        ]
    ).reshape(1, ROWS, NBB * BLOCK)
    share = momentum.shape[2]
    offset = lax.axis_index("dp") * share
    total = lax.psum(local_table, "dp")
    momentum_all, error_all = (
        lax.all_gather(momentum, "dp", axis=2, tiled=True),
        lax.all_gather(error, "dp", axis=2, tiled=True),
    )
    momentum_all = DECAY * momentum_all + total / dp_count
    error_all = error_all + momentum_all
    momentum_new = lax.dynamic_slice_in_dim(momentum_all, offset, share, 2)
    error_mid = lax.dynamic_slice_in_dim(error_all, offset, share, 2)
    error_rows = error_all.reshape(ROWS, NBB, BLOCK)
    reads = [
        error_rows[row_index][bucket[row_index]] * sign_values[row_index][:, None]
        for row_index in range(ROWS)
    ]
    estimate = middle_five(reads)
    update = estimate - jnp.clip(estimate, -THRESHOLD, THRESHOLD)
    share_buckets = share // BLOCK
    share_ids = bucket_ids[:share_buckets] + lax.axis_index("dp") * share_buckets
    sketched = jnp.stack(
        [
            split_product(
                jnp.where(
                    bucket[row_index][None, :] == share_ids, signs[row_index][None, :], zero_sel
                ),
                update,
                contract_plain,
            )
            for row_index in range(ROWS)
        ]
    ).reshape(1, ROWS, share)
    error_new = error_mid - sketched
    return (hidden_grad, momentum_new, error_new, update.reshape(local_rows, -1))


def solution(mesh):
    in_specs = (
        P(("dp", "fsdp"), None),
        P(),
        P("fsdp", None),
        P(("dp", "fsdp"), None),
        P(None, "fsdp"),
        P(None, "fsdp"),
        P("fsdp", None, "dp"),
        P("fsdp", None, "dp"),
    )
    out_specs = (
        P(("dp", "fsdp"), None),
        P("fsdp", None, "dp"),
        P("fsdp", None, "dp"),
        P("fsdp", None),
    )
    return jax.shard_map(
        on_device, mesh=mesh, in_specs=in_specs, out_specs=out_specs, check_vma=False
    )
```

profile of v0, /device:TPU:0, one launch (start us, length us, event | category | flops | bytes accessed | tf_op | source)
XLA Modules:
  0.0 444.7 jit_solution(9080943481307150394)
XLA Ops:
  7.2 9.0 %all_gather.9 = bf16[512,512]{1,0:T(8,128)(2,1)S(1)} all-gather(bf16[128,512]{1,0:T(8,128)(2,1)} %param.11), channel_id=1, replica_groups=mesh['dp'=8,'fsdp'=4] {'fsdp'}, dimensions={0}, use_global_device_ids=true | all-gather | bytes 655360 | tf_op jit(solution)/shard_map/all_gather | solution.py:57
  16.2 2.7 convolution_convert_fusion
  18.8 4.6 %all-to-all-start = ((bf16[4,128,2048]{2,1,0:T(8,128)(2,1)}), bf16[4,128,2048]{2,1,0:T(8,128)(2,1)}, u32[]{:S(2)}, u32[]{:S(2)}) async-start(bf16[4,128,2048]{2,1,0:T(8,128)(2,1)} %bitcast.136), calls=%async_computation | async-start | bytes 4194304 | tf_op jit(solution)/shard_map/all_to_all | solution.py:65
  23.4 3.2 copy.34
  26.7 1.0 slice_reduce_fusion
  27.8 0.8 compare_select_fusion.19
  28.6 1.5 slice_reduce_fusion.7
  30.1 1.8 mul.191
  31.9 2.8 mul.203
  34.7 2.8 mul.207
  37.6 2.9 mul.195
  40.5 2.9 mul.199
  43.4 1.1 fusion.33
  45.0 1.4 broadcast_clamp_fusion
  49.2 4.1 convert_bitcast_fusion
  53.3 5.4 %copy.35 = f32[128,4,2048]{0,2,1:T(8,128)} copy(f32[128,4,2048]{2,0,1:T(8,128)} %convert_bitcast_fusion) | data formatting | bytes 8388608 | tf_op jit(solution)/shard_map/convert_element_type | solution.py:26
  58.7 3.0 fusion.28
  62.2 4.6 %fusion.32 = (bf16[128,8192]{0,1:T(8,128)(2,1)}, bf16[128,8192]{0,1:T(8,128)(2,1)}) fusion(bf16[128,8192]{0,1:T(8,128)(2,1)S(1)} %copy.34, f32[8192]{0:T(1024)S(1)} %copy-done.18, f32[128]{0:T(128)S(1)} %copy-done.32, f32[128]{0:T(128)S(1)} %broadcast_multiply_fusion, f32[128,4,2048]{0,2,1:T(8,128)S(1)} %copy-done.2), kind=kLoop, calls=%fused_computation.36 | loop fusion | flops 9437184 | bytes 10519552 | tf_op jit(solution)/shard_map/convert_element_type | solution.py:22
  66.7 3.6 all-to-all-start.1
  70.4 0.7 fusion.149
  71.1 24.9 %all-to-all-done.1 = bf16[128,4,2048]{0,2,1:T(8,128)(2,1)S(1)} async-done(((bf16[128,4,2048]{0,2,1:T(8,128)(2,1)}), bf16[128,4,2048]{0,2,1:T(8,128)(2,1)S(1)}, u32[]{:S(2)}, u32[]{:S(2)}) %all-to-all-start.1) | async-done | bytes 2097184 | tf_op jit(solution)/shard_map/all_to_all | solution.py:58
  96.0 1.3 copy-done.3
  97.3 2.9 copy.36
  100.3 4.3 convolution_multiply_fusion
  104.6 5.0 %reshape.231 = f32[8192,128]{1,0:T(8,128)} reshape(f32[2048,512]{1,0:T(8,128)} %convolution_multiply_fusion) | data formatting | bytes 8388608 | tf_op jit(solution)/shard_map/reshape | solution.py:67
  109.6 4.0 subtract_convert_fusion.1
  113.6 1.2 fusion.21
  114.9 1.3 fusion.64
  116.2 0.7 constant_dynamic-update-slice_fusion.4
  116.8 1.2 fusion.17
  118.1 1.3 fusion.67
  119.4 1.2 fusion.13
  120.6 1.2 fusion.70
  121.9 1.2 fusion.9
  123.1 1.2 fusion.73
  124.4 1.2 fusion.5
  125.7 10.6 %fusion.76 = f32[256,128]{1,0:T(8,128)S(1)} fusion(f32[256,128]{1,0:T(8,128)S(1)} %fusion.5, bf16[8192,128]{1,0:T(8,128)(2,1)S(1)} %get-tuple-element.23, s32[8192]{0:T(1024)S(1)} %bitcast.138, bf16[8192]{0:T(1024)(128)(2,1)S(1)} %get-tuple-element.13), kind=kOutput, calls=%fused_computation.83 | convolution fusion | flops 541097984 | bytes 2408448 | tf_op jit(solution)/shard_map/dot_general | solution.py:34
  136.2 0.7 constant_dynamic-update-slice_fusion.3
  136.9 0.7 constant_dynamic-update-slice_fusion.2
  137.6 0.7 constant_dynamic-update-slice_fusion.1
  139.4 35.1 %all_gather.11 = f32[1,5,32768]{2,0,1:T(1,128)} all-gather(f32[1,5,4096]{2,0,1:T(1,128)} %param.15), channel_id=1, replica_groups=mesh['dp'=8,'fsdp'=4] {'dp'}, dimensions={2}, use_global_device_ids=true | all-gather | bytes 737280 | tf_op jit(solution)/shard_map/all_gather | solution.py:89
  174.5 34.3 %all_gather.10 = f32[1,5,32768]{2,0,1:T(1,128)} all-gather(f32[1,5,4096]{2,0,1:T(1,128)} %param.14), channel_id=1, replica_groups=mesh['dp'=8,'fsdp'=4] {'dp'}, dimensions={2}, use_global_device_ids=true | all-gather | bytes 737280 | tf_op jit(solution)/shard_map/all_gather | solution.py:88
  208.8 2.9 copy.47
  211.7 4.5 %all-reduce.2.cloned.1.call-done = f32[1,5,32768]{2,0,1:T(1,128)} async-done(((f32[1,5,32768]{2,0,1:T(1,128)}), f32[1,5,32768]{2,0,1:T(1,128)}) %all-reduce.2.cloned.1.call-update) | async-done | bytes 655376 | tf_op jit(solution)/shard_map/psum | solution.py:86
  216.2 3.9 fusion.147
  220.2 28.0 %gather_fusion.4 = f32[8192,128]{1,0:T(8,128)} fusion(f32[256,128]{1,0:T(8,128)S(1)} %bitcast.127, s32[8192]{0:T(1024)S(1)} %copy-done.28), kind=kCustom, calls=%fused_computation.4 | custom fusion | bytes 8421376 | tf_op jit(solution)/shard_map/gather | solution.py:97
  248.2 27.9 %gather_fusion.3 = f32[8192,128]{1,0:T(8,128)} fusion(f32[256,128]{1,0:T(8,128)S(1)} %bitcast.126, s32[8192]{0:T(1024)S(1)} %copy-done.27), kind=kCustom, calls=%fused_computation.3 | custom fusion | bytes 8421376 | tf_op jit(solution)/shard_map/gather | solution.py:97
  276.1 27.9 %gather_fusion.2 = f32[8192,128]{1,0:T(8,128)} fusion(f32[256,128]{1,0:T(8,128)S(1)} %bitcast.125, s32[8192]{0:T(1024)S(1)} %copy-done.26), kind=kCustom, calls=%fused_computation.2 | custom fusion | bytes 8421376 | tf_op jit(solution)/shard_map/gather | solution.py:97
  304.0 27.8 %gather_fusion.1 = f32[8192,128]{1,0:T(8,128)} fusion(f32[256,128]{1,0:T(8,128)S(1)} %bitcast.124, s32[8192]{0:T(1024)S(1)} %copy-done.25), kind=kCustom, calls=%fused_computation.1 | custom fusion | bytes 8421376 | tf_op jit(solution)/shard_map/gather | solution.py:97
  331.9 27.8 %gather_fusion = f32[8192,128]{1,0:T(8,128)} fusion(f32[256,128]{1,0:T(8,128)S(1)} %bitcast.123, s32[8192]{0:T(1024)S(1)} %copy-done.24), kind=kCustom, calls=%fused_computation | custom fusion | bytes 8421376 | tf_op jit(solution)/shard_map/gather | solution.py:97
  359.8 8.9 %subtract_convert_fusion = (bf16[8192,128]{1,0:T(8,128)(2,1)S(1)}, bf16[8192,128]{1,0:T(8,128)(2,1)S(1)}) fusion(f32[8192,128]{1,0:T(8,128)} %gather_fusion.4, f32[8192]{0:T(1024)S(1)} %bitcast.157, f32[8192,128]{1,0:T(8,128)} %gather_fusion.3, f32[8192]{0:T(1024)S(1)} %bitcast.158, f32[8192,128]{1,0:T(8,128)} %gather_fusion.2, f32[8192]{0:T(1024)S(1)} %bitcast.159, ...), kind=kLoop, calls=%fused_computation.45 | loop fusion | flops 22020096 | bytes 25329664 | tf_op jit(solution)/shard_map/convert_element_type | solution.py:33
  371.0 4.9 %gather.30 = f32[2048,512]{1,0:T(8,128)} reshape(f32[8192,128]{1,0:T(8,128)} %gather_fusion) | data formatting | bytes 8388608 | tf_op jit(solution)/shard_map/gather | solution.py:97
  376.0 4.9 %gather.33 = f32[2048,512]{1,0:T(8,128)} reshape(f32[8192,128]{1,0:T(8,128)} %gather_fusion.3) | data formatting | bytes 8388608 | tf_op jit(solution)/shard_map/gather | solution.py:97
  380.9 4.9 %gather.34 = f32[2048,512]{1,0:T(8,128)} reshape(f32[8192,128]{1,0:T(8,128)} %gather_fusion.4) | data formatting | bytes 8388608 | tf_op jit(solution)/shard_map/gather | solution.py:97
  385.9 4.9 %gather.31 = f32[2048,512]{1,0:T(8,128)} reshape(f32[8192,128]{1,0:T(8,128)} %gather_fusion.1) | data formatting | bytes 8388608 | tf_op jit(solution)/shard_map/gather | solution.py:97
  390.8 4.9 %gather.32 = f32[2048,512]{1,0:T(8,128)} reshape(f32[8192,128]{1,0:T(8,128)} %gather_fusion.2) | data formatting | bytes 8388608 | tf_op jit(solution)/shard_map/gather | solution.py:97
  396.2 1.1 convolution_add_fusion.3
  398.8 1.7 dynamic-slice_subtract_fusion
  400.5 4.6 %mul.192 = f32[2048,4,128]{2,1,0:T(4,128)S(1)} broadcast(f32[2048,4]{1,0:T(8,128)S(1)} %mul.191), dimensions={0,1} | broadcast | bytes 4227072 | tf_op jit(solution)/shard_map/mul | solution.py:97
  405.2 3.8 mul.204
  409.0 3.8 mul.208
  412.8 3.9 mul.196
  416.7 3.9 mul.200
  420.6 17.1 %clamp_subtract_fusion = f32[2048,512]{1,0:T(8,128)} fusion(f32[2048,512]{1,0:T(8,128)} %gather.30, f32[256,8,4,128]{3,2,1,0:T(4,128)S(1)} %bitcast.128, f32[2048,512]{1,0:T(8,128)} %gather.33, f32[256,8,4,128]{3,2,1,0:T(4,128)} %bitcast.129, f32[2048,512]{1,0:T(8,128)} %gather.34, f32[256,8,4,128]{3,2,1,0:T(4,128)} %bitcast.130, f32[2048,512]{1,0:T(8,128)} %gather.31, ...), kind=kLoop, calls=%fused_computation.15 | loop fusion | flops 17825792 | bytes 46137344 | tf_op jit(solution)/shard_map/sub | solution.py:101
  (92 shorter events, 9.5 us)
Async XLA Ops:
  7.2 9.0 %copy-start = (bf16[2048,512]{1,0:T(8,128)(2,1)S(1)}, bf16[2048,512]{1,0:T(8,128)(2,1)}, u32[]{:S(2)}) copy-start(bf16[2048,512]{1,0:T(8,128)(2,1)} %param.10) | copy-start | bytes 6291460
  16.2 2.7 copy-start.10
  18.8 7.8 %copy-start.13 = (s32[5,8192]{1,0:T(8,128)S(1)}, s32[5,8192]{1,0:T(8,128)}, u32[]{:S(2)}) copy-start(s32[5,8192]{1,0:T(8,128)} %param.13) | copy-start | bytes 491524
  18.8 8.9 %copy-start.11 = (s32[5,8192]{1,0:T(8,128)S(1)}, s32[5,8192]{1,0:T(8,128)}, u32[]{:S(2)}) copy-start(s32[5,8192]{1,0:T(8,128)} %param.12) | copy-start | bytes 491524
  18.8 30.4 %all-to-all-start = ((bf16[4,128,2048]{2,1,0:T(8,128)(2,1)}), bf16[4,128,2048]{2,1,0:T(8,128)(2,1)}, u32[]{:S(2)}, u32[]{:S(2)}) async-start(bf16[4,128,2048]{2,1,0:T(8,128)(2,1)} %bitcast.136), calls=%async_computation | async-start | bytes 4194304 | tf_op jit(solution)/shard_map/all_to_all | solution.py:65
  53.3 5.4 %copy-start.18 = (f32[8192]{0:T(1024)S(1)}, f32[8192]{0:T(1024)}, u32[]{:S(2)}) copy-start(f32[8192]{0:T(1024)} %param.9) | copy-start | bytes 98308
  53.3 5.4 %copy-start.32 = (f32[128]{0:T(128)S(1)}, f32[128]{0:T(128)}, u32[]{:S(2)}) copy-start(f32[128]{0:T(128)} %add_rsqrt_fusion) | copy-start | bytes 1540
  58.7 3.5 copy-start.2
  66.7 29.3 %all-to-all-start.1 = ((bf16[128,4,2048]{0,2,1:T(8,128)(2,1)}), bf16[128,4,2048]{0,2,1:T(8,128)(2,1)S(1)}, u32[]{:S(2)}, u32[]{:S(2)}) async-start(bf16[128,4,2048]{0,2,1:T(8,128)(2,1)} %bitcast.135), calls=%async_computation.1 | async-start | bytes 4194304 | tf_op jit(solution)/shard_map/all_to_all | solution.py:58
  70.3 145.9 %all-reduce.2.cloned.1.call-start = ((), (), s32[]{:S(2)}) async-start(), calls=%async_computation.2 | async-start | bytes 1310720 | tf_op jit(solution)/shard_map/psum | solution.py:86
  96.0 1.3 copy-start.3
  109.6 4.0 copy-start.12
  109.6 4.0 copy-start.17
  114.9 1.9 copy-start.16
  118.1 1.3 copy-start.15
  120.6 1.3 copy-start.14
  125.6 83.2 %copy-start.4 = (bf16[128,8192]{0,1:T(8,128)(2,1)S(1)}, bf16[128,8192]{0,1:T(8,128)(2,1)}, u32[]{:S(2)}) copy-start(bf16[128,8192]{0,1:T(8,128)(2,1)} %get-tuple-element.25) | copy-start | bytes 6291460
  208.8 11.4 %copy-start.28 = (s32[8192]{0:T(1024)S(1)}, s32[8192]{0:T(1024)}, u32[]{:S(2)}) copy-start(s32[8192]{0:T(1024)} %broadcast_clamp_fusion) | copy-start | bytes 98308
  220.1 28.0 %copy-start.9 = (f32[1,5,32768]{2,0,1:T(1,128)}, f32[1,5,32768]{2,0,1:T(1,128)S(1)}, u32[]{:S(2)}) copy-start(f32[1,5,32768]{2,0,1:T(1,128)S(1)} %get-tuple-element.20) | copy-start | bytes 1966084
  220.2 28.0 %copy-start.27 = (s32[8192]{0:T(1024)S(1)}, s32[8192]{0:T(1024)}, u32[]{:S(2)}) copy-start(s32[8192]{0:T(1024)} %broadcast_clamp_fusion.1) | copy-start | bytes 98308
  248.2 27.9 %copy-start.26 = (s32[8192]{0:T(1024)S(1)}, s32[8192]{0:T(1024)}, u32[]{:S(2)}) copy-start(s32[8192]{0:T(1024)} %broadcast_clamp_fusion.2) | copy-start | bytes 98308
  276.1 27.9 %copy-start.25 = (s32[8192]{0:T(1024)S(1)}, s32[8192]{0:T(1024)}, u32[]{:S(2)}) copy-start(s32[8192]{0:T(1024)} %broadcast_clamp_fusion.3) | copy-start | bytes 98308
  304.0 27.8 %copy-start.24 = (s32[8192]{0:T(1024)S(1)}, s32[8192]{0:T(1024)}, u32[]{:S(2)}) copy-start(s32[8192]{0:T(1024)} %broadcast_clamp_fusion.4) | copy-start | bytes 98308
  331.8 27.9 %copy-start.19 = (f32[1,8192]{1,0:T(1,128)S(1)}, f32[1,8192]{1,0:T(1,128)}, u32[]{:S(2)}) copy-start(f32[1,8192]{1,0:T(1,128)} %get-tuple-element.31) | copy-start | bytes 98308
  331.8 27.9 %copy-start.20 = (f32[1,8192]{1,0:T(1,128)S(1)}, f32[1,8192]{1,0:T(1,128)}, u32[]{:S(2)}) copy-start(f32[1,8192]{1,0:T(1,128)} %get-tuple-element.32) | copy-start | bytes 98308
  331.8 27.9 %copy-start.21 = (f32[1,8192]{1,0:T(1,128)S(1)}, f32[1,8192]{1,0:T(1,128)}, u32[]{:S(2)}) copy-start(f32[1,8192]{1,0:T(1,128)} %get-tuple-element.33) | copy-start | bytes 98308
  331.8 27.9 %copy-start.22 = (f32[1,8192]{1,0:T(1,128)S(1)}, f32[1,8192]{1,0:T(1,128)}, u32[]{:S(2)}) copy-start(f32[1,8192]{1,0:T(1,128)} %get-tuple-element.34) | copy-start | bytes 98308
  331.9 27.9 %copy-start.23 = (f32[1,8192]{1,0:T(1,128)S(1)}, f32[1,8192]{1,0:T(1,128)}, u32[]{:S(2)}) copy-start(f32[1,8192]{1,0:T(1,128)} %get-tuple-element.35) | copy-start | bytes 98308
  359.7 8.9 %copy-start.29 = (s32[32]{0:T(128)S(1)}, s32[32]{0:T(128)}, u32[]{:S(2)}) copy-start(s32[32]{0:T(128)} %fusion.126) | copy-start | bytes 388
  390.8 4.9 %copy-start.30 = (s32[32]{0:T(128)S(1)}, s32[32]{0:T(128)}, u32[]{:S(2)}) copy-start(s32[32]{0:T(128)} %fusion.126) | copy-start | bytes 388
  395.7 1.6 copy-start.31
  398.3 6.9 %copy-start.5 = (f32[2048,4]{1,0:T(8,128)S(1)}, f32[2048,4]{1,0:T(8,128)}, u32[]{:S(2)}) copy-start(f32[2048,4]{1,0:T(8,128)} %mul.203) | copy-start | bytes 98308
  400.5 8.5 %copy-start.6 = (f32[2048,4]{1,0:T(8,128)S(1)}, f32[2048,4]{1,0:T(8,128)}, u32[]{:S(2)}) copy-start(f32[2048,4]{1,0:T(8,128)} %mul.207) | copy-start | bytes 98308
  405.2 7.7 %copy-start.7 = (f32[2048,4]{1,0:T(8,128)S(1)}, f32[2048,4]{1,0:T(8,128)}, u32[]{:S(2)}) copy-start(f32[2048,4]{1,0:T(8,128)} %mul.195) | copy-start | bytes 98308
  409.0 7.7 %copy-start.8 = (f32[2048,4]{1,0:T(8,128)S(1)}, f32[2048,4]{1,0:T(8,128)}, u32[]{:S(2)}) copy-start(f32[2048,4]{1,0:T(8,128)} %mul.199) | copy-start | bytes 98308
  420.6 17.1 %copy-start.1 = (bf16[2048,512]{1,0:T(8,128)(2,1)S(1)}, bf16[2048,512]{1,0:T(8,128)(2,1)}, u32[]{:S(2)}) copy-start(bf16[2048,512]{1,0:T(8,128)(2,1)} %param.10) | copy-start | bytes 6291460
Sparse Core Ops, SparseCore 0:
  139.0 77.1 all-reduce.1
where the time goes:
time: 450 us; the launch traced here: 445 us
  local copies, waits for them, and re-layouts  225 us (50%)
  blocking collectives  78.3 us (17%)
  other arithmetic  54.1 us (12%)
  matrix products  34.1 us (8%)
  waiting for transfers between devices  29.9 us (7%)
  between operations  14.8 us (3%)
  starting transfers between devices  8.24 us (2%)
    gather x10, local copies, waits for them, and re-layouts, on_device(): error_rows[row_index][bucket[row_index]] * sign_values[row_index][:, None]  164 us
    all_gather x1, blocking collectives, on_device(): lax.all_gather(error, 'dp', axis=2, tiled=True)  35.1 us
    all_gather x1, blocking collectives, on_device(): lax.all_gather(momentum, 'dp', axis=2, tiled=True)  34.3 us
    mul x10, local copies, waits for them, and re-layouts, on_device(): error_rows[row_index][bucket[row_index]] * sign_values[row_index][:, None]  33.3 us
    all_to_all x1, waiting for transfers between devices, on_device(): lax.all_to_all(inputs, 'fsdp', split_axis=1, concat_axis=0, tiled=True)  24.9 us
    dot_general x10, matrix products, split_product(): lax.dot_general(selector, upper, numbers, preferred_element_type=jnp.floa...  17.9 us
    sub x1, other arithmetic, on_device(): update = estimate - jnp.clip(estimate, -THRESHOLD, THRESHOLD)  17.1 us
    convert_element_type x2, other arithmetic, split_product(): lower = (values - upper.astype(jnp.float32)).astype(jnp.bfloat16)  12.9 us
  transfers between devices with their start and end apart: 3, of which 3 were waited for; matrix products, arithmetic and copies ran while one was open for 7% of the time, Pallas kernels for 0%

commit v1 on v0

v1 whole, which is shorter than its diff:
```python
import functools
import math

import jax
import jax.numpy as jnp
from jax import lax
from jax.experimental import pallas as pl
from jax.experimental.pallas import tpu as pltpu
from jax.sharding import PartitionSpec as P

ROWS = 5
NBB = 256
BLOCK = 128
PAD = 8

EPS = 1e-05
DECAY = 0.9
THRESHOLD = 1.0
MIB = 1024 * 1024


def params(limit=48):
    return pltpu.CompilerParams(vmem_limit_bytes=limit * MIB)


def middle_three(first, second, third):
    return jnp.maximum(jnp.minimum(first, second), jnp.minimum(jnp.maximum(first, second), third))


def middle_five(items):
    upper_pair = jnp.minimum(jnp.maximum(items[0], items[1]), jnp.maximum(items[2], items[3]))
    lower_pair = jnp.maximum(jnp.minimum(items[0], items[1]), jnp.minimum(items[2], items[3]))
    return middle_three(items[4], upper_pair, lower_pair)


def partner(index, step, count):
    if count & (count - 1) == 0:
        return index ^ step
    return (index + step) % count


def turn(index, step, count):
    return (index + step) % count


def prep_kernel(where, bucket_ref, sign_ref, rows_ref, cols_ref, stacked):
    share, count = where[1], where[2]
    quads = rows_ref.shape[0]
    width = quads * BLOCK
    groups = bucket_ref.shape[1] // width
    bucket = bucket_ref[...]
    bucket = jnp.where(count == 1, bucket ^ share, lax.rem(bucket + (NBB - share), NBB))
    code = ((bucket + 1) * (2 * sign_ref[...] - 1)).astype(jnp.float32)
    stacked[...] = jnp.zeros_like(stacked)
    for group in range(groups):
        stacked[group * PAD : group * PAD + ROWS, :] = code[:, group * width : (group + 1) * width]
    source = lax.broadcasted_iota(jnp.int32, (width, width), 0)
    target = lax.broadcasted_iota(jnp.int32, (width, width), 1)
    chosen = source == quads * (target % BLOCK) + target // BLOCK
    order = jnp.where(chosen, 1.0, 0.0).astype(jnp.bfloat16)
    moved = jnp.dot(stacked[...].astype(jnp.bfloat16), order, preferred_element_type=jnp.float32)
    for group in range(groups):
        for quad in range(quads):
            rows_ref[quad, :, group * BLOCK : (group + 1) * BLOCK] = moved[
                group * PAD : (group + 1) * PAD, quad * BLOCK : (quad + 1) * BLOCK
            ].astype(rows_ref.dtype)
    for quad in range(quads):
        cols_ref[:, quad * PAD : (quad + 1) * PAD] = (
            rows_ref[quad].astype(jnp.float32).T
        )


def prep(where, bucket, sign_bits, quads):
    blocks = bucket.shape[1]
    features = blocks // quads
    vmem = pl.BlockSpec(memory_space=pltpu.VMEM)
    return pl.pallas_call(
        prep_kernel,
        out_shape=(
            jax.ShapeDtypeStruct((quads, PAD, features), jnp.bfloat16),
            jax.ShapeDtypeStruct((features, quads * PAD), jnp.float32),
        ),
        in_specs=[pl.BlockSpec(memory_space=pltpu.SMEM), vmem, vmem],
        out_specs=(vmem, vmem),
        scratch_shapes=[pltpu.VMEM((features // BLOCK * PAD, quads * BLOCK), jnp.float32)],
        compiler_params=params(),
        name="codes",
    )(where, bucket, sign_bits)


def norm_kernel(pair, turns, where, hidden_ref, gain_ref, *out_refs):
    core, place = where[3], where[4]
    features = out_refs[0].shape[2]
    values = hidden_ref[...].astype(jnp.float32)
    inverse_rms = lax.rsqrt(jnp.mean(values * values, axis=1, keepdims=True) + EPS)
    for other in range(pair):
        for step in range(turns):
            slab = lax.rem(place + step, turns) * pair + (core ^ other)
            span = pl.ds(pl.multiple_of(slab * features, BLOCK), features)
            normed = hidden_ref[:, span].astype(jnp.float32) * inverse_rms
            out_refs[other][step] = (normed * gain_ref[:, span]).astype(jnp.bfloat16)


def norm(where, hidden, gain, pair, turns):
    tokens, width = hidden.shape
    features = width // (pair * turns)
    tile = min(tokens, 32)
    out = jax.ShapeDtypeStruct((turns, tokens, features), jnp.bfloat16)
    return pl.pallas_call(
        functools.partial(norm_kernel, pair, turns),
        out_shape=(out,) * pair,
        grid=(tokens // tile,),
        in_specs=[
            pl.BlockSpec(memory_space=pltpu.SMEM),
            pl.BlockSpec((tile, width), lambda i: (i, 0)),
            pl.BlockSpec((1, width), lambda i: (0, 0)),
        ],
        out_specs=(pl.BlockSpec((turns, tile, features), lambda i: (0, i, 0)),) * pair,
        compiler_params=params(),
        name="normed",
    )(where, hidden, gain)


def sketch_kernel(scale, count, pair, *refs):
    inputs_refs, cot_refs, rows_ref = refs[:pair], refs[pair : 2 * pair], refs[2 * pair]
    table_ref, total = refs[2 * pair + 1 :]
    step = pl.program_id(0)
    contract = (((0,), (0,)), ((), ()))
    inputs = jnp.concatenate([ref[0] for ref in inputs_refs], axis=0)
    cots = jnp.concatenate([ref[...] for ref in cot_refs], axis=0)
    grad = lax.dot_general(inputs, cots, contract, preferred_element_type=jnp.float32) * scale
    quads = rows_ref.shape[0]
    upper = grad.astype(jnp.bfloat16)
    lower = (grad - upper.astype(jnp.float32)).astype(jnp.bfloat16)
    both = jnp.concatenate(
        [
            jnp.concatenate(
                [part[:, quad * BLOCK : (quad + 1) * BLOCK] for part in (upper, lower)], axis=1
            )
            for quad in range(quads)
        ],
        axis=0,
    )
    features = rows_ref.shape[2]
    numbers = lax.broadcasted_iota(jnp.int32, (NBB, features), 0).astype(jnp.bfloat16) + 1

    @pl.when(step == 0)
    def _():
        total[...] = jnp.zeros_like(total)

    for row in range(ROWS):
        picks = []
        for quad in range(quads):
            code = rows_ref[quad, row : row + 1, :]
            sign = jnp.where(code < 0, -1.0, 1.0).astype(jnp.bfloat16)
            picks.append(jnp.where(jnp.abs(code) == numbers, sign, jnp.zeros((), jnp.bfloat16)))
        pick = jnp.concatenate(picks, axis=1)
        total[row] += jnp.dot(pick, both, preferred_element_type=jnp.float32)

    @pl.when(step == pl.num_programs(0) - 1)
    def _():
        share = NBB // count
        for row in range(ROWS):
            table = total[row, :, :BLOCK] + total[row, :, BLOCK:]
            for part in range(count):
                table_ref[part, row] = table[part * share : (part + 1) * share, :].astype(
                    table_ref.dtype
                )


def sketch(inputs, cots, rows, which, scale, count, tile=512):
    tokens, features = inputs[0].shape[1:]
    quads = rows.shape[0]
    tile = min(tile, features)
    pair = len(inputs)
    return pl.pallas_call(
        functools.partial(sketch_kernel, scale, count, pair),
        out_shape=jax.ShapeDtypeStruct((count, ROWS, NBB // count, BLOCK), jnp.bfloat16),
        grid=(features // tile,),
        in_specs=[pl.BlockSpec((1, tokens, tile), lambda i: (which, 0, i))] * pair
        + [pl.BlockSpec(cots[0].shape, lambda i: (0, 0))] * pair
        + [pl.BlockSpec((quads, PAD, tile), lambda i: (0, 0, i))],
        out_specs=pl.BlockSpec((count, ROWS, NBB // count, BLOCK), lambda i: (0, 0, 0, 0)),
        scratch_shapes=[pltpu.VMEM((ROWS, NBB, 2 * BLOCK), jnp.float32)],
        compiler_params=params(),
        name="sketch",
    )(*inputs, *cots, rows)


def grads_kernel(turns, pair, *refs):
    cot_refs, weight_refs, out_refs = refs[:turns], refs[turns : turns + pair], refs[turns + pair :]
    cots = jnp.concatenate([ref[...] for ref in cot_refs], axis=0)
    tokens = cot_refs[0].shape[0]
    for other in range(pair):
        grad = lax.dot_general(
            cots,
            weight_refs[other][...],
            (((1,), (1,)), ((), ())),
            preferred_element_type=jnp.float32,
        ).astype(jnp.bfloat16)
        for step in range(turns):
            out_refs[step][other] = grad[step * tokens : (step + 1) * tokens]


def grads(cots, weights, tile=512):
    turns, pair = len(cots), len(weights)
    tokens, width = cots[0].shape
    features = weights[0].shape[0]
    tile = min(tile, features)
    return pl.pallas_call(
        functools.partial(grads_kernel, turns, pair),
        out_shape=(jax.ShapeDtypeStruct((pair, tokens, features), jnp.bfloat16),) * turns,
        grid=(features // tile,),
        in_specs=[pl.BlockSpec((tokens, width), lambda i: (0, 0))] * turns
        + [pl.BlockSpec((tile, width), lambda i: (i, 0))] * pair,
        out_specs=(pl.BlockSpec((pair, tokens, tile), lambda i: (0, 0, i)),) * turns,
        compiler_params=params(),
        name="input_grad",
    )(*cots, *weights)


def backward_kernel(turns, pair, where, hidden_ref, gain_ref, *refs):
    grad_refs, out_ref = refs[:turns], refs[turns]
    core, place = where[3], where[4]
    features = grad_refs[0].shape[2]
    width = hidden_ref.shape[1]
    values = hidden_ref[...].astype(jnp.float32)
    inverse_rms = lax.rsqrt(jnp.mean(values * values, axis=1, keepdims=True) + EPS)
    spans = []
    total = jnp.zeros((hidden_ref.shape[0], 1), jnp.float32)
    for step in range(turns):
        for other in range(pair):
            slab = lax.rem(place + step, turns) * pair + (core ^ other)
            span = pl.ds(pl.multiple_of(slab * features, BLOCK), features)
            spans.append((step, other, span))
            scaled = grad_refs[step][other].astype(jnp.float32) * gain_ref[:, span]
            normed = hidden_ref[:, span].astype(jnp.float32) * inverse_rms
            total += jnp.sum(scaled * normed, axis=1, keepdims=True)
    mean_term = total / width
    for step, other, span in spans:
        scaled = grad_refs[step][other].astype(jnp.float32) * gain_ref[:, span]
        normed = hidden_ref[:, span].astype(jnp.float32) * inverse_rms
        out_ref[:, span] = (inverse_rms * (scaled - normed * mean_term)).astype(jnp.bfloat16)


def backward(where, hidden, gain, grad_parts):
    tokens, width = hidden.shape
    turns, pair = len(grad_parts), grad_parts[0].shape[0]
    features = grad_parts[0].shape[2]
    tile = min(tokens, 32)
    return pl.pallas_call(
        functools.partial(backward_kernel, turns, pair),
        out_shape=jax.ShapeDtypeStruct((tokens, width), jnp.bfloat16),
        grid=(tokens // tile,),
        in_specs=[
            pl.BlockSpec(memory_space=pltpu.SMEM),
            pl.BlockSpec((tile, width), lambda i: (i, 0)),
            pl.BlockSpec((1, width), lambda i: (0, 0)),
        ]
        + [pl.BlockSpec((pair, tile, features), lambda i: (0, i, 0))] * turns,
        out_specs=pl.BlockSpec((tile, width), lambda i: (i, 0)),
        compiler_params=params(),
        name="hidden_grad",
    )(where, hidden, gain, *grad_parts)


def unsketch_kernel(count, *refs):
    part_refs, cols_ref, rows_ref, error_ref = refs[:count], *refs[count : count + 3]
    update_ref, error_new_ref, total = refs[count + 3 :]
    step = pl.program_id(0)
    quads = rows_ref.shape[0]
    share = NBB // count
    tile = cols_ref.shape[0]
    tables = [jnp.concatenate([ref[row] for ref in part_refs], axis=0) for row in range(ROWS)]
    lanes = (lax.broadcasted_iota(jnp.int32, (tile, NBB), 1) + 1).astype(jnp.float32)
    numbers = lax.broadcasted_iota(jnp.int32, (share, tile), 0).astype(jnp.bfloat16) + 1

    @pl.when(step == 0)
    def _():
        total[...] = jnp.zeros_like(total)

    for quad in range(quads):
        reads = []
        for row in range(ROWS):
            code = cols_ref[:, quad * PAD + row : quad * PAD + row + 1]
            pick = jnp.where(jnp.abs(code) == lanes, 1.0, 0.0).astype(jnp.bfloat16)
            read = jnp.dot(pick, tables[row], preferred_element_type=jnp.float32)
            reads.append(jnp.where(code < 0, -read, read))
        estimate = middle_five(reads)
        update = estimate - jnp.clip(estimate, -THRESHOLD, THRESHOLD)
        update_ref[:, quad * BLOCK : (quad + 1) * BLOCK] = update
        upper = update.astype(jnp.bfloat16)
        lower = (update - upper.astype(jnp.float32)).astype(jnp.bfloat16)
        both = jnp.concatenate([upper, lower], axis=1)
        picks = []
        for row in range(ROWS):
            code = rows_ref[quad, row : row + 1, :]
            sign = jnp.where(code < 0, -1.0, 1.0).astype(jnp.bfloat16)
            picks.append(jnp.where(jnp.abs(code) == numbers, sign, jnp.zeros((), jnp.bfloat16)))
        pick = jnp.concatenate(picks, axis=0)
        total[...] += jnp.dot(pick, both, preferred_element_type=jnp.float32)

    @pl.when(step == pl.num_programs(0) - 1)
    def _():
        for row in range(ROWS):
            rows = slice(row * share, (row + 1) * share)
            error_new_ref[row] = error_ref[row] - (total[rows, :BLOCK] + total[rows, BLOCK:])


def unsketch(parts, cols, rows, error_mid, tile=512):
    count = len(parts)
    features = cols.shape[0]
    quads = rows.shape[0]
    share = NBB // count
    tile = min(tile, features)
    table_spec = pl.BlockSpec((ROWS, share, BLOCK), lambda i: (0, 0, 0))
    return pl.pallas_call(
        functools.partial(unsketch_kernel, count),
        out_shape=(
            jax.ShapeDtypeStruct((features, quads * BLOCK), jnp.float32),
            jax.ShapeDtypeStruct((ROWS, share, BLOCK), jnp.float32),
        ),
        grid=(features // tile,),
        in_specs=[table_spec] * count
        + [
            pl.BlockSpec((tile, quads * PAD), lambda i: (i, 0)),
            pl.BlockSpec((quads, PAD, tile), lambda i: (0, 0, i)),
            table_spec,
        ],
        out_specs=(pl.BlockSpec((tile, quads * BLOCK), lambda i: (i, 0)), table_spec),
        scratch_shapes=[pltpu.VMEM((ROWS * share, 2 * BLOCK), jnp.float32)],
        compiler_params=params(),
        name="unsketch",
    )(*parts, cols, rows, error_mid)


def on_device(hidden_states, gain, key_weight, key_cotangent, bucket, sign_bits, momentum, error):
    fsdp_count = lax.axis_size("fsdp")
    dp_count = lax.axis_size("dp")
    pair = 2 if fsdp_count % 2 == 0 else 1
    turns = fsdp_count // pair
    tokens, width = hidden_states.shape
    quads = key_cotangent.shape[1] // BLOCK
    share = NBB // dp_count
    scale = 1.0 / math.sqrt(tokens * fsdp_count)
    dp_at, fsdp_at = lax.axis_index("dp"), lax.axis_index("fsdp")
    core, place = fsdp_at % pair, fsdp_at // pair
    power = 1 if dp_count & (dp_count - 1) == 0 else 0
    where = jnp.stack([jnp.int32(0), dp_at * share, jnp.int32(power), core, place]).astype(jnp.int32)
    gain = gain.reshape(1, width)

    def across(value):
        return lax.ppermute(value, "fsdp", [(i, i ^ 1) for i in range(fsdp_count)])

    def from_turn(value, step):
        pairs = [
            (((i // pair + step) % turns) * pair + i % pair, i) for i in range(fsdp_count)
        ]
        return lax.ppermute(value, "fsdp", pairs)

    def to_turn(value, step):
        return from_turn(value, turns - step)

    def to_share(value, step):
        return lax.ppermute(value, "dp", [(i, partner(i, step, dp_count)) for i in range(dp_count)])

    def from_share(value, step):
        return lax.ppermute(value, "dp", [(partner(i, step, dp_count), i) for i in range(dp_count)])

    rows, cols = prep(where, bucket, sign_bits, quads)
    rows_at = [rows] + [from_turn(rows, step) for step in range(1, turns)]
    inputs = list(norm(where, hidden_states, gain, pair, turns))
    cots = [key_cotangent]
    if pair == 2:
        inputs[1] = across(inputs[1])
        cots.append(across(key_cotangent))
    received = []
    for step in range(1, turns):
        table = sketch(inputs, cots, rows_at[step], step, scale, dp_count)
        received.append(to_turn(table, step))
    table = sketch(inputs, cots, rows, 0, scale, dp_count).astype(jnp.float32)
    for other in received:
        table = table + other.astype(jnp.float32)

    weights = [key_weight] + ([across(key_weight)] if pair == 2 else [])
    turn_cots = [key_cotangent] + [from_turn(key_cotangent, step) for step in range(1, turns)]
    grad_parts = grads(turn_cots, weights)
    grad_parts = [grad_parts[0]] + [
        from_turn(grad_parts[turns - step], step) for step in range(1, turns)
    ]
    hidden_grad = backward(where, hidden_states, gain, grad_parts)

    sent = table.astype(jnp.bfloat16)
    total = table[0]
    order = sorted(range(1, dp_count), key=lambda step: -bin(step).count("1") * 100 - step)
    arrived = [to_share(sent[step], step) for step in order]
    for part in arrived:
        total = total + part.astype(jnp.float32)
    momentum_new = DECAY * momentum.reshape(ROWS, share, BLOCK) + total / dp_count
    error_mid = error.reshape(ROWS, share, BLOCK) + momentum_new
    error_sent = error_mid.astype(jnp.bfloat16)
    gathered = {step: from_share(error_sent, step) for step in order}
    parts = [error_sent] + [gathered[step] for step in range(1, dp_count)]
    update, error_new = unsketch(parts, cols, rows, error_mid)
    return (
        hidden_grad,
        momentum_new.reshape(momentum.shape),
        error_new.reshape(error.shape),
        update,
    )


def solution(mesh):
    in_specs = (
        P(("dp", "fsdp"), None),
        P(),
        P("fsdp", None),
        P(("dp", "fsdp"), None),
        P(None, "fsdp"),
        P(None, "fsdp"),
        P("fsdp", None, "dp"),
        P("fsdp", None, "dp"),
    )
    out_specs = (
        P(("dp", "fsdp"), None),
        P("fsdp", None, "dp"),
        P("fsdp", None, "dp"),
        P("fsdp", None),
    )
    return jax.shard_map(
        on_device, mesh=mesh, in_specs=in_specs, out_specs=out_specs, check_vma=False
    )
```

time: 450 us -> 89.3 us (0.20); the launches traced: 445 us -> 89 us
  local copies, waits for them, and re-layouts: 225 us -> 2.5 us
  blocking collectives: 78.3 us -> 0 us
  other arithmetic: 54.1 us -> 0.9 us
  Pallas kernels: 0 us -> 43.2 us
  matrix products: 34.1 us -> 0 us
  starting transfers between devices: 8.24 us -> 30.6 us
  waiting for transfers between devices: 29.9 us -> 11 us
  between operations: 14.8 us -> 0.79 us
    gather x10 -> x0, local copies, waits for them, and re-layouts: 164 us -> none  [on_device(): error_rows[row_index][bucket[row_index]] * sign_values[row_index][:, None]]
    all_gather x3 -> x0, blocking collectives: 78.3 us -> none  [the longest x1 35.1 us: on_device(): lax.all_gather(error, 'dp', axis=2, tiled=True)]
    pallas_call x0 -> x7, Pallas kernels: none -> 43.2 us  [the longest x2 17.5 us: sketch(): pl.pallas_call(functools.partial(sketch_kernel, scale, count, pair), out_...]
    dot_general x22 -> x0, matrix products: 34.1 us -> none  [the longest x10 17.9 us: split_product(): lax.dot_general(selector, upper, numbers, preferred_element_type=jnp.floa...]
    mul x10 -> x0, local copies, waits for them, and re-layouts: 33.3 us -> none  [on_device(): error_rows[row_index][bucket[row_index]] * sign_values[row_index][:, None]]
    ppermute x0 -> x21, starting transfers between devices: none -> 30.6 us  [the longest x7 12.1 us: to_share(): lax.ppermute(value, 'dp', [(i, partner(i, step, dp_count)) for i in range...]
    all_to_all x2 -> x0, waiting for transfers between devices: 25.3 us -> none  [the longest x1 24.9 us: on_device(): lax.all_to_all(inputs, 'fsdp', split_axis=1, concat_axis=0, tiled=True)]
    convert_element_type x5 -> x1, other arithmetic: 21.6 us -> 0.7 us  [on_device(): error_sent = error_mid.astype(jnp.bfloat16)]
  transfers between devices with their start and end apart: 3 -> 21, of which waited for: 3 -> 6; matrix products, arithmetic and copies ran while one was open for 7% -> 1% of each run, Pallas kernels for 0% -> 44%
where the time goes in v1:
time: 89.3 us; the launch traced here: 89 us
  Pallas kernels  43.2 us (48%)
  starting transfers between devices  30.6 us (34%)
  waiting for transfers between devices  11 us (12%)
  local copies, waits for them, and re-layouts  2.5 us (3%)
  other arithmetic  0.9 us (1%)
    pallas_call x2, Pallas kernels, sketch(): pl.pallas_call(functools.partial(sketch_kernel, scale, count, pair), out_...  17.5 us
    pallas_call x1, Pallas kernels, unsketch(): pl.pallas_call(functools.partial(unsketch_kernel, count), out_shape=(jax....  14 us
    ppermute x7, starting transfers between devices, to_share(): lax.ppermute(value, 'dp', [(i, partner(i, step, dp_count)) for i in range...  12.1 us
    ppermute x7, starting transfers between devices, from_share(): lax.ppermute(value, 'dp', [(partner(i, step, dp_count), i) for i in range...  11.1 us
    ppermute x4, starting transfers between devices, from_turn(): return lax.ppermute(value, 'fsdp', pairs)  6.28 us
    pallas_call x1, Pallas kernels, backward(): pl.pallas_call(functools.partial(backward_kernel, turns, pair), out_shape...  4.3 us
    ppermute x4, waiting for transfers between devices, from_turn(): return lax.ppermute(value, 'fsdp', pairs)  4.09 us
    pallas_call x1, Pallas kernels, grads(): pl.pallas_call(functools.partial(grads_kernel, turns, pair), out_shape=(j...  3.64 us
  transfers between devices with their start and end apart: 21, of which 6 were waited for; matrix products, arithmetic and copies ran while one was open for 1% of the time, Pallas kernels for 44%

profile of v1, /device:TPU:0, one launch (start us, length us, event | category | flops | bytes accessed | tf_op | source)
XLA Modules:
  0.0 89.0 jit_solution(10043812013557054084)
XLA Ops:
  0.6 0.5 collective-permute-start.1
  1.1 0.1 stack.15.where
  1.2 1.6 %copy-done = bf16[128,8192]{1,0:T(8,128)(2,1)S(1)} copy-done((bf16[128,8192]{1,0:T(8,128)(2,1)S(1)}, bf16[128,8192]{1,0:T(8,128)(2,1)}, u32[]{:S(2)}) %copy-start) | copy-done | bytes 2097176
  2.8 0.8 copy-done.6
  3.6 2.0 %normed.1 = (bf16[2,128,2048]{2,1,0:T(8,128)(2,1)S(1)}, bf16[2,128,2048]{2,1,0:T(8,128)(2,1)S(1)}) custom-call(s32[5]{0:T(128)S(1)} %stack.15.where, bf16[128,8192]{1,0:T(8,128)(2,1)S(1)} %copy-done, f32[1,8192]{1,0:T(1,128)S(1)} %bitcast.43), custom_call_target="tpu_custom_call" | custom-call | tf_op jit(solution)/shard_map/normed/pallas_call | solution.py:109
  5.5 0.1 collective-permute-start.3
  5.7 0.0 copy-done.3
  5.7 0.5 collective-permute-start.4
  6.1 0.0 copy-done.4
  6.1 0.0 copy-done.5
  6.1 1.9 %codes.1 = (bf16[4,8,2048]{2,1,0:T(8,128)(2,1)S(1)}, f32[2048,32]{1,0:T(8,128)S(1)}) custom-call(s32[5]{0:T(128)S(1)} %stack.15.where, s32[5,8192]{1,0:T(8,128)S(1)} %copy-done.4, s32[5,8192]{1,0:T(8,128)S(1)} %copy-done.5), custom_call_target="tpu_custom_call" | custom-call | tf_op jit(solution)/shard_map/codes/pallas_call | solution.py:77
  8.0 2.7 %collective-permute-start.5 = (bf16[4,8,2048]{2,1,0:T(8,128)(2,1)S(1)}, bf16[4,8,2048]{2,1,0:T(8,128)(2,1)S(1)}, u32[]{:S(2)}, u32[]{:S(2)}) collective-permute-start(bf16[4,8,2048]{2,1,0:T(8,128)(2,1)S(1)} %get-tuple-element.16.refs_4_.refs_9_), channel_id=1, source_target_pairs={{2,0},{3,1},{0,2},{1,3},{6,4},{7,5},{4,6},{5,7},{10,8},{11,9},{8,1... | collective-permute-start | bytes 393224 | tf_op jit(solution)/shard_map/ppermute | solution.py:359
  10.7 0.0 collective-permute-done.4.refs_3_
  10.7 4.1 %collective-permute-done.5.refs_4_ = bf16[4,8,2048]{2,1,0:T(8,128)(2,1)S(1)} collective-permute-done((bf16[4,8,2048]{2,1,0:T(8,128)(2,1)S(1)}, bf16[4,8,2048]{2,1,0:T(8,128)(2,1)S(1)}, u32[]{:S(2)}, u32[]{:S(2)}) %collective-permute-start.5) | collective-permute-done | bytes 131104 | tf_op jit(solution)/shard_map/ppermute | solution.py:359
  14.7 0.0 collective-permute-done.3.refs_1_
  14.7 8.7 %sketch.3 = bf16[8,5,32,128]{3,2,1,0:T(8,128)(2,1)S(1)} custom-call(bf16[2,128,2048]{2,1,0:T(8,128)(2,1)S(1)} %get-tuple-element.14.refs_0_, bf16[2,128,2048]{2,1,0:T(8,128)(2,1)S(1)} %collective-permute-done.3.refs_1_, bf16[128,512]{1,0:T(8,128)(2,1)S(1)} %copy-done.3, bf16[128,512]{1,0:T(8,128)(2,1)S(1)} %collective-permute-done.4.refs_3_, ...), custom_call_target="tpu_custom_call" | custom-call | tf_op jit(solution)/shard_map/sketch/pallas_call | solution.py:176
  23.5 0.0 copy-start.2
  23.5 1.8 %collective-permute-start.6 = (bf16[8,5,32,128]{3,2,1,0:T(8,128)(2,1)S(1)}, bf16[8,5,32,128]{3,2,1,0:T(8,128)(2,1)S(1)}, u32[]{:S(2)}, u32[]{:S(2)}) collective-permute-start(bf16[8,5,32,128]{3,2,1,0:T(8,128)(2,1)S(1)} %sketch.3), channel_id=1, source_target_pairs={{2,0},{3,1},{0,2},{1,3},{6,4},{7,5},{4,6},{5,7},{10,8},{11,9},{8,1... | collective-permute-start | bytes 983048 | tf_op jit(solution)/shard_map/ppermute | solution.py:359
  25.3 0.3 collective-permute-start
  25.6 8.7 %sketch.2 = bf16[8,5,32,128]{3,2,1,0:T(8,128)(2,1)S(1)} custom-call(bf16[2,128,2048]{2,1,0:T(8,128)(2,1)S(1)} %get-tuple-element.14.refs_0_, bf16[2,128,2048]{2,1,0:T(8,128)(2,1)S(1)} %collective-permute-done.3.refs_1_, bf16[128,512]{1,0:T(8,128)(2,1)S(1)} %copy-done.3, bf16[128,512]{1,0:T(8,128)(2,1)S(1)} %collective-permute-done.4.refs_3_, ...), custom_call_target="tpu_custom_call" | custom-call | tf_op jit(solution)/shard_map/sketch/pallas_call | solution.py:176
  34.3 0.0 collective-permute-done.6
  34.4 0.1 convert_add_fusion
  34.5 4.8 %collective-permute-start.7 = (bf16[5,32,128]{2,1,0:T(8,128)(2,1)S(1)}, bf16[5,32,128]{2,1,0:T(8,128)(2,1)S(1)}, u32[]{:S(2)}, u32[]{:S(2)}) collective-permute-start(bf16[5,32,128]{2,1,0:T(8,128)(2,1)S(1)} %get-tuple-element.33), channel_id=1, source_target_pairs={{0,28},{4,24},{8,20},{12,16},{16,12},{20,8},{24,4},{28,0},{1,29},{... | collective-permute-start | bytes 122888 | tf_op jit(solution)/shard_map/ppermute | solution.py:365
  39.3 0.5 collective-permute-start.13
  39.9 0.0 collective-permute-start.12
  39.9 0.0 collective-permute-done.refs_1_
  39.9 0.7 collective-permute-start.11
  40.6 0.0 collective-permute-done.1.refs_3_
  40.6 2.4 %collective-permute-start.10 = (bf16[5,32,128]{2,1,0:T(8,128)(2,1)S(1)}, bf16[5,32,128]{2,1,0:T(8,128)(2,1)S(1)}, u32[]{:S(2)}, u32[]{:S(2)}) collective-permute-start(bf16[5,32,128]{2,1,0:T(8,128)(2,1)S(1)} %get-tuple-element.37), channel_id=1, source_target_pairs={{0,12},{4,8},{8,4},{12,0},{16,28},{20,24},{24,20},{28,16},{1,13},{... | collective-permute-start | bytes 122888 | tf_op jit(solution)/shard_map/ppermute | solution.py:365
  42.9 0.0 copy-done.8
  42.9 0.0 copy-done.2
  42.9 3.6 %input_grad.1 = (bf16[2,128,2048]{2,1,0:T(8,128)(2,1)S(1)}, bf16[2,128,2048]{2,1,0:T(8,128)(2,1)S(1)}) custom-call(bf16[128,512]{1,0:T(8,128)(2,1)S(1)} %copy-done.3, bf16[128,512]{1,0:T(8,128)(2,1)S(1)} %collective-permute-done.refs_1_, bf16[2048,512]{1,0:T(8,128)(2,1)S(1)} %copy-done.2, bf16[2048,512]{1,0:T(8,128)(2,1)} %copy-done.8), custom_call_target="tpu_custom_call" | custom-call | tf_op jit(solution)/shard_map/input_grad/pallas_call | solution.py:210
  46.6 0.0 copy-start.1
  46.6 0.0 copy-start.7
  46.6 0.0 collective-permute-done.7
  46.6 2.9 %collective-permute-start.9 = (bf16[5,32,128]{2,1,0:T(8,128)(2,1)S(1)}, bf16[5,32,128]{2,1,0:T(8,128)(2,1)S(1)}, u32[]{:S(2)}, u32[]{:S(2)}) collective-permute-start(bf16[5,32,128]{2,1,0:T(8,128)(2,1)S(1)} %get-tuple-element.38), channel_id=1, source_target_pairs={{0,20},{4,16},{8,28},{12,24},{16,4},{20,0},{24,12},{28,8},{1,21},{... | collective-permute-start | bytes 122888 | tf_op jit(solution)/shard_map/ppermute | solution.py:365
  49.6 0.0 collective-permute-done.13
  49.6 0.7 collective-permute-start.8
  50.3 0.0 collective-permute-done.12
  50.3 1.5 %collective-permute-start.2 = (bf16[2,128,2048]{2,1,0:T(8,128)(2,1)S(1)}, bf16[2,128,2048]{2,1,0:T(8,128)(2,1)S(1)}, u32[]{:S(2)}, u32[]{:S(2)}) collective-permute-start(bf16[2,128,2048]{2,1,0:T(8,128)(2,1)S(1)} %get-tuple-element.13), channel_id=1, source_target_pairs={{2,0},{3,1},{0,2},{1,3},{6,4},{7,5},{4,6},{5,7},{10,8},{11,9},{8,1... | collective-permute-start | bytes 3145736 | tf_op jit(solution)/shard_map/ppermute | solution.py:359
  51.8 0.0 copy-done.9
  51.8 0.1 broadcast_multiply_fusion
  51.9 0.0 collective-permute-done.11
  51.9 0.0 collective-permute-done.10
  51.9 1.5 %collective-permute-done.9 = bf16[5,32,128]{2,1,0:T(8,128)(2,1)S(1)} collective-permute-done((bf16[5,32,128]{2,1,0:T(8,128)(2,1)S(1)}, bf16[5,32,128]{2,1,0:T(8,128)(2,1)S(1)}, u32[]{:S(2)}, u32[]{:S(2)}) %collective-permute-start.9) | collective-permute-done | bytes 40992 | tf_op jit(solution)/shard_map/ppermute | solution.py:365
  53.4 2.0 %collective-permute-done.8 = bf16[5,32,128]{2,1,0:T(8,128)(2,1)S(1)} collective-permute-done((bf16[5,32,128]{2,1,0:T(8,128)(2,1)S(1)}, bf16[5,32,128]{2,1,0:T(8,128)(2,1)S(1)}, u32[]{:S(2)}, u32[]{:S(2)}) %collective-permute-start.8) | collective-permute-done | bytes 40992 | tf_op jit(solution)/shard_map/ppermute | solution.py:365
  55.4 0.7 fusion.10
  56.1 1.3 %collective-permute-start.20 = (bf16[5,32,128]{2,1,0:T(8,128)(2,1)S(1)}, bf16[5,32,128]{2,1,0:T(8,128)(2,1)S(1)}, u32[]{:S(2)}, u32[]{:S(2)}) collective-permute-start(bf16[5,32,128]{2,1,0:T(8,128)(2,1)S(1)} %get-tuple-element.28.refs_0_), channel_id=1, source_target_pairs={{28,0},{24,4},{20,8},{16,12},{12,16},{8,20},{4,24},{0,28},{29,1},{... | collective-permute-start | bytes 122888 | tf_op jit(solution)/shard_map/ppermute | solution.py:368
  57.4 3.4 %collective-permute-start.19 = (bf16[5,32,128]{2,1,0:T(8,128)(2,1)S(1)}, bf16[5,32,128]{2,1,0:T(8,128)(2,1)S(1)}, u32[]{:S(2)}, u32[]{:S(2)}) collective-permute-start(bf16[5,32,128]{2,1,0:T(8,128)(2,1)S(1)} %get-tuple-element.28.refs_0_), channel_id=1, source_target_pairs={{24,0},{28,4},{16,8},{20,12},{8,16},{12,20},{0,24},{4,28},{25,1},{... | collective-permute-start | bytes 122888 | tf_op jit(solution)/shard_map/ppermute | solution.py:368
  60.8 0.0 collective-permute-start.18
  60.8 2.9 %collective-permute-start.17 = (bf16[5,32,128]{2,1,0:T(8,128)(2,1)S(1)}, bf16[5,32,128]{2,1,0:T(8,128)(2,1)S(1)}, u32[]{:S(2)}, u32[]{:S(2)}) collective-permute-start(bf16[5,32,128]{2,1,0:T(8,128)(2,1)S(1)} %get-tuple-element.28.refs_0_), channel_id=1, source_target_pairs={{16,0},{20,4},{24,8},{28,12},{0,16},{4,20},{8,24},{12,28},{17,1},{... | collective-permute-start | bytes 122888 | tf_op jit(solution)/shard_map/ppermute | solution.py:368
  63.8 0.0 collective-permute-done.20.refs_7_
  63.8 0.0 collective-permute-start.16
  63.8 0.0 collective-permute-done.19.refs_6_
  63.8 2.9 %collective-permute-start.15 = (bf16[5,32,128]{2,1,0:T(8,128)(2,1)S(1)}, bf16[5,32,128]{2,1,0:T(8,128)(2,1)S(1)}, u32[]{:S(2)}, u32[]{:S(2)}) collective-permute-start(bf16[5,32,128]{2,1,0:T(8,128)(2,1)S(1)} %get-tuple-element.28.refs_0_), channel_id=1, source_target_pairs={{8,0},{12,4},{0,8},{4,12},{24,16},{28,20},{16,24},{20,28},{9,1},{1... | collective-permute-start | bytes 122888 | tf_op jit(solution)/shard_map/ppermute | solution.py:368
  66.7 0.0 collective-permute-done.18.refs_5_
  66.7 0.6 collective-permute-start.14
  67.3 0.0 collective-permute-done.17.refs_4_
  67.3 1.4 %collective-permute-done.16.refs_3_ = bf16[5,32,128]{2,1,0:T(8,128)(2,1)S(1)} collective-permute-done((bf16[5,32,128]{2,1,0:T(8,128)(2,1)S(1)}, bf16[5,32,128]{2,1,0:T(8,128)(2,1)S(1)}, u32[]{:S(2)}, u32[]{:S(2)}) %collective-permute-start.16) | collective-permute-done | bytes 40992 | tf_op jit(solution)/shard_map/ppermute | solution.py:368
  68.7 0.4 collective-permute-done.15.refs_2_
  69.1 1.6 %collective-permute-done.14.refs_1_ = bf16[5,32,128]{2,1,0:T(8,128)(2,1)S(1)} collective-permute-done((bf16[5,32,128]{2,1,0:T(8,128)(2,1)S(1)}, bf16[5,32,128]{2,1,0:T(8,128)(2,1)S(1)}, u32[]{:S(2)}, u32[]{:S(2)}) %collective-permute-start.14) | collective-permute-done | bytes 40992 | tf_op jit(solution)/shard_map/ppermute | solution.py:368
  70.7 14.0 %unsketch.1 = (f32[2048,512]{1,0:T(8,128)}, f32[5,32,128]{2,1,0:T(8,128)}) custom-call(bf16[5,32,128]{2,1,0:T(8,128)(2,1)S(1)} %get-tuple-element.28.refs_0_, bf16[5,32,128]{2,1,0:T(8,128)(2,1)S(1)} %collective-permute-done.14.refs_1_, bf16[5,32,128]{2,1,0:T(8,128)(2,1)S(1)} %collective-permute-done.15.refs_2_, ...), custom_call_target="tpu_custom_call" | custom-call | tf_op jit(solution)/shard_map/unsketch/pallas_call | solution.py:317
  84.7 0.0 collective-permute-done.2.refs_1_
  84.7 4.3 %hidden_grad.1 = bf16[128,8192]{1,0:T(8,128)(2,1)} custom-call(s32[5]{0:T(128)S(1)} %stack.15.where, bf16[128,8192]{1,0:T(8,128)(2,1)S(1)} %copy-done.1, f32[1,8192]{1,0:T(1,128)S(1)} %bitcast.44, bf16[2,128,2048]{2,1,0:T(8,128)(2,1)S(1)} %get-tuple-element.12.refs_0_, bf16[2,128,2048]{2,1,0:T(8,128)(2,1)S(1)} %collective-permute-done.2.refs_1_), custom_call_target="tpu_custom_call" | custom-call | tf_op jit(solution)/shard_map/hidden_grad/pallas_call | solution.py:251
  (12 shorter events, 0.0 us)
Async XLA Ops:
  0.6 39.9 %collective-permute-start.1 = (bf16[2048,512]{1,0:T(8,128)(2,1)}, bf16[2048,512]{1,0:T(8,128)(2,1)S(1)}, u32[]{:S(2)}, u32[]{:S(2)}) collective-permute-start(bf16[2048,512]{1,0:T(8,128)(2,1)} %refs_2_.3), channel_id=1, source_target_pairs={{0,1},{1,0},{2,3},{3,2},{4,5},{5,4},{6,7},{7,6},{8,9},{9,8},{10,11... | collective-permute-start | bytes 6291464 | tf_op jit(solution)/shard_map/ppermute | solution.py:353
  1.2 1.6 %copy-start = (bf16[128,8192]{1,0:T(8,128)(2,1)S(1)}, bf16[128,8192]{1,0:T(8,128)(2,1)}, u32[]{:S(2)}) copy-start(bf16[128,8192]{1,0:T(8,128)(2,1)} %hidden_ref.3) | copy-start | bytes 6291460
  2.8 0.8 copy-start.6
  3.6 2.1 %copy-start.3 = (bf16[128,512]{1,0:T(8,128)(2,1)S(1)}, bf16[128,512]{1,0:T(8,128)(2,1)}, u32[]{:S(2)}) copy-start(bf16[128,512]{1,0:T(8,128)(2,1)} %refs_2_.5) | copy-start | bytes 393220
  3.6 2.5 %copy-start.4 = (s32[5,8192]{1,0:T(8,128)S(1)}, s32[5,8192]{1,0:T(8,128)}, u32[]{:S(2)}) copy-start(s32[5,8192]{1,0:T(8,128)} %bucket_ref.1) | copy-start | bytes 491524
  3.6 2.5 %copy-start.5 = (s32[5,8192]{1,0:T(8,128)S(1)}, s32[5,8192]{1,0:T(8,128)}, u32[]{:S(2)}) copy-start(s32[5,8192]{1,0:T(8,128)} %sign_ref.1) | copy-start | bytes 491524
  5.5 9.2 %collective-permute-start.3 = (bf16[2,128,2048]{2,1,0:T(8,128)(2,1)S(1)}, bf16[2,128,2048]{2,1,0:T(8,128)(2,1)S(1)}, u32[]{:S(2)}, u32[]{:S(2)}) collective-permute-start(bf16[2,128,2048]{2,1,0:T(8,128)(2,1)S(1)} %get-tuple-element.15), channel_id=1, source_target_pairs={{0,1},{1,0},{2,3},{3,2},{4,5},{5,4},{6,7},{7,6},{8,9},{9,8},{10,11... | collective-permute-start | bytes 3145736 | tf_op jit(solution)/shard_map/ppermute | solution.py:353
  5.7 5.0 %collective-permute-start.4 = (bf16[128,512]{1,0:T(8,128)(2,1)S(1)}, bf16[128,512]{1,0:T(8,128)(2,1)S(1)}, u32[]{:S(2)}, u32[]{:S(2)}) collective-permute-start(bf16[128,512]{1,0:T(8,128)(2,1)S(1)} %copy-done.3), channel_id=1, source_target_pairs={{0,1},{1,0},{2,3},{3,2},{4,5},{5,4},{6,7},{7,6},{8,9},{9,8},{10,11... | collective-permute-start | bytes 393224 | tf_op jit(solution)/shard_map/ppermute | solution.py:353
  8.0 6.8 %collective-permute-start.5 = (bf16[4,8,2048]{2,1,0:T(8,128)(2,1)S(1)}, bf16[4,8,2048]{2,1,0:T(8,128)(2,1)S(1)}, u32[]{:S(2)}, u32[]{:S(2)}) collective-permute-start(bf16[4,8,2048]{2,1,0:T(8,128)(2,1)S(1)} %get-tuple-element.16.refs_4_.refs_9_), channel_id=1, source_target_pairs={{2,0},{3,1},{0,2},{1,3},{6,4},{7,5},{4,6},{5,7},{10,8},{11,9},{8,1... | collective-permute-start | bytes 393224 | tf_op jit(solution)/shard_map/ppermute | solution.py:359
  23.5 19.5 %copy-start.2 = (bf16[2048,512]{1,0:T(8,128)(2,1)S(1)}, bf16[2048,512]{1,0:T(8,128)(2,1)}, u32[]{:S(2)}) copy-start(bf16[2048,512]{1,0:T(8,128)(2,1)} %refs_2_.3) | copy-start | bytes 6291460
  23.5 10.8 %collective-permute-start.6 = (bf16[8,5,32,128]{3,2,1,0:T(8,128)(2,1)S(1)}, bf16[8,5,32,128]{3,2,1,0:T(8,128)(2,1)S(1)}, u32[]{:S(2)}, u32[]{:S(2)}) collective-permute-start(bf16[8,5,32,128]{3,2,1,0:T(8,128)(2,1)S(1)} %sketch.3), channel_id=1, source_target_pairs={{2,0},{3,1},{0,2},{1,3},{6,4},{7,5},{4,6},{5,7},{10,8},{11,9},{8,1... | collective-permute-start | bytes 983048 | tf_op jit(solution)/shard_map/ppermute | solution.py:359
  25.3 14.6 %collective-permute-start = (bf16[128,512]{1,0:T(8,128)(2,1)S(1)}, bf16[128,512]{1,0:T(8,128)(2,1)S(1)}, u32[]{:S(2)}, u32[]{:S(2)}) collective-permute-start(bf16[128,512]{1,0:T(8,128)(2,1)S(1)} %copy-done.3), channel_id=1, source_target_pairs={{2,0},{3,1},{0,2},{1,3},{6,4},{7,5},{4,6},{5,7},{10,8},{11,9},{8,1... | collective-permute-start | bytes 393224 | tf_op jit(solution)/shard_map/ppermute | solution.py:359
  34.5 12.1 %collective-permute-start.7 = (bf16[5,32,128]{2,1,0:T(8,128)(2,1)S(1)}, bf16[5,32,128]{2,1,0:T(8,128)(2,1)S(1)}, u32[]{:S(2)}, u32[]{:S(2)}) collective-permute-start(bf16[5,32,128]{2,1,0:T(8,128)(2,1)S(1)} %get-tuple-element.33), channel_id=1, source_target_pairs={{0,28},{4,24},{8,20},{12,16},{16,12},{20,8},{24,4},{28,0},{1,29},{... | collective-permute-start | bytes 122888 | tf_op jit(solution)/shard_map/ppermute | solution.py:365
  39.3 10.2 %collective-permute-start.13 = (bf16[5,32,128]{2,1,0:T(8,128)(2,1)S(1)}, bf16[5,32,128]{2,1,0:T(8,128)(2,1)S(1)}, u32[]{:S(2)}, u32[]{:S(2)}) collective-permute-start(bf16[5,32,128]{2,1,0:T(8,128)(2,1)S(1)} %get-tuple-element.34), channel_id=1, source_target_pairs={{0,4},{4,0},{8,12},{12,8},{16,20},{20,16},{24,28},{28,24},{1,5},{5... | collective-permute-start | bytes 122888 | tf_op jit(solution)/shard_map/ppermute | solution.py:365
  39.9 10.4 %collective-permute-start.12 = (bf16[5,32,128]{2,1,0:T(8,128)(2,1)S(1)}, bf16[5,32,128]{2,1,0:T(8,128)(2,1)S(1)}, u32[]{:S(2)}, u32[]{:S(2)}) collective-permute-start(bf16[5,32,128]{2,1,0:T(8,128)(2,1)S(1)} %get-tuple-element.35), channel_id=1, source_target_pairs={{0,8},{4,12},{8,0},{12,4},{16,24},{20,28},{24,16},{28,20},{1,9},{5... | collective-permute-start | bytes 122888 | tf_op jit(solution)/shard_map/ppermute | solution.py:365
  39.9 12.0 %collective-permute-start.11 = (bf16[5,32,128]{2,1,0:T(8,128)(2,1)S(1)}, bf16[5,32,128]{2,1,0:T(8,128)(2,1)S(1)}, u32[]{:S(2)}, u32[]{:S(2)}) collective-permute-start(bf16[5,32,128]{2,1,0:T(8,128)(2,1)S(1)} %get-tuple-element.36), channel_id=1, source_target_pairs={{0,16},{4,20},{8,24},{12,28},{16,0},{20,4},{24,8},{28,12},{1,17},{... | collective-permute-start | bytes 122888 | tf_op jit(solution)/shard_map/ppermute | solution.py:365
  40.6 2.4 %copy-start.8 = (bf16[2048,512]{1,0:T(8,128)(2,1)}, bf16[2048,512]{1,0:T(8,128)(2,1)S(1)}, u32[]{:S(2)}) copy-start(bf16[2048,512]{1,0:T(8,128)(2,1)S(1)} %collective-permute-done.1.refs_3_) | copy-start | bytes 6291460
  40.6 11.2 %copy-start.9 = (f32[1,5,4096]{2,0,1:T(1,128)S(1)}, f32[1,5,4096]{2,0,1:T(1,128)}, u32[]{:S(2)}) copy-start(f32[1,5,4096]{2,0,1:T(1,128)} %param.14) | copy-start | bytes 245764
  40.6 14.9 %copy-start.10 = (f32[1,5,4096]{2,0,1:T(1,128)S(1)}, f32[1,5,4096]{2,0,1:T(1,128)}, u32[]{:S(2)}) copy-start(f32[1,5,4096]{2,0,1:T(1,128)} %param.15) | copy-start | bytes 245764
  40.6 11.3 %collective-permute-start.10 = (bf16[5,32,128]{2,1,0:T(8,128)(2,1)S(1)}, bf16[5,32,128]{2,1,0:T(8,128)(2,1)S(1)}, u32[]{:S(2)}, u32[]{:S(2)}) collective-permute-start(bf16[5,32,128]{2,1,0:T(8,128)(2,1)S(1)} %get-tuple-element.37), channel_id=1, source_target_pairs={{0,12},{4,8},{8,4},{12,0},{16,28},{20,24},{24,20},{28,16},{1,13},{... | collective-permute-start | bytes 122888 | tf_op jit(solution)/shard_map/ppermute | solution.py:365
  46.6 38.1 %copy-start.1 = (bf16[128,8192]{1,0:T(8,128)(2,1)S(1)}, bf16[128,8192]{1,0:T(8,128)(2,1)}, u32[]{:S(2)}) copy-start(bf16[128,8192]{1,0:T(8,128)(2,1)} %hidden_ref.3) | copy-start | bytes 6291460
  46.6 38.1 %copy-start.7 = (f32[8192]{0:T(1024)S(1)}, f32[8192]{0:T(1024)}, u32[]{:S(2)}) copy-start(f32[8192]{0:T(1024)} %param.9) | copy-start | bytes 98308
  46.6 6.7 %collective-permute-start.9 = (bf16[5,32,128]{2,1,0:T(8,128)(2,1)S(1)}, bf16[5,32,128]{2,1,0:T(8,128)(2,1)S(1)}, u32[]{:S(2)}, u32[]{:S(2)}) collective-permute-start(bf16[5,32,128]{2,1,0:T(8,128)(2,1)S(1)} %get-tuple-element.38), channel_id=1, source_target_pairs={{0,20},{4,16},{8,28},{12,24},{16,4},{20,0},{24,12},{28,8},{1,21},{... | collective-permute-start | bytes 122888 | tf_op jit(solution)/shard_map/ppermute | solution.py:365
  49.6 5.8 %collective-permute-start.8 = (bf16[5,32,128]{2,1,0:T(8,128)(2,1)S(1)}, bf16[5,32,128]{2,1,0:T(8,128)(2,1)S(1)}, u32[]{:S(2)}, u32[]{:S(2)}) collective-permute-start(bf16[5,32,128]{2,1,0:T(8,128)(2,1)S(1)} %get-tuple-element.39), channel_id=1, source_target_pairs={{0,24},{4,28},{8,16},{12,20},{16,8},{20,12},{24,0},{28,4},{1,25},{... | collective-permute-start | bytes 122888 | tf_op jit(solution)/shard_map/ppermute | solution.py:365
  50.3 34.4 %collective-permute-start.2 = (bf16[2,128,2048]{2,1,0:T(8,128)(2,1)S(1)}, bf16[2,128,2048]{2,1,0:T(8,128)(2,1)S(1)}, u32[]{:S(2)}, u32[]{:S(2)}) collective-permute-start(bf16[2,128,2048]{2,1,0:T(8,128)(2,1)S(1)} %get-tuple-element.13), channel_id=1, source_target_pairs={{2,0},{3,1},{0,2},{1,3},{6,4},{7,5},{4,6},{5,7},{10,8},{11,9},{8,1... | collective-permute-start | bytes 3145736 | tf_op jit(solution)/shard_map/ppermute | solution.py:359
  56.1 7.7 %collective-permute-start.20 = (bf16[5,32,128]{2,1,0:T(8,128)(2,1)S(1)}, bf16[5,32,128]{2,1,0:T(8,128)(2,1)S(1)}, u32[]{:S(2)}, u32[]{:S(2)}) collective-permute-start(bf16[5,32,128]{2,1,0:T(8,128)(2,1)S(1)} %get-tuple-element.28.refs_0_), channel_id=1, source_target_pairs={{28,0},{24,4},{20,8},{16,12},{12,16},{8,20},{4,24},{0,28},{29,1},{... | collective-permute-start | bytes 122888 | tf_op jit(solution)/shard_map/ppermute | solution.py:368
  57.4 6.3 %collective-permute-start.19 = (bf16[5,32,128]{2,1,0:T(8,128)(2,1)S(1)}, bf16[5,32,128]{2,1,0:T(8,128)(2,1)S(1)}, u32[]{:S(2)}, u32[]{:S(2)}) collective-permute-start(bf16[5,32,128]{2,1,0:T(8,128)(2,1)S(1)} %get-tuple-element.28.refs_0_), channel_id=1, source_target_pairs={{24,0},{28,4},{16,8},{20,12},{8,16},{12,20},{0,24},{4,28},{25,1},{... | collective-permute-start | bytes 122888 | tf_op jit(solution)/shard_map/ppermute | solution.py:368
  60.8 5.9 %collective-permute-start.18 = (bf16[5,32,128]{2,1,0:T(8,128)(2,1)S(1)}, bf16[5,32,128]{2,1,0:T(8,128)(2,1)S(1)}, u32[]{:S(2)}, u32[]{:S(2)}) collective-permute-start(bf16[5,32,128]{2,1,0:T(8,128)(2,1)S(1)} %get-tuple-element.28.refs_0_), channel_id=1, source_target_pairs={{20,0},{16,4},{28,8},{24,12},{4,16},{0,20},{12,24},{8,28},{21,1},{... | collective-permute-start | bytes 122888 | tf_op jit(solution)/shard_map/ppermute | solution.py:368
  60.8 6.4 %collective-permute-start.17 = (bf16[5,32,128]{2,1,0:T(8,128)(2,1)S(1)}, bf16[5,32,128]{2,1,0:T(8,128)(2,1)S(1)}, u32[]{:S(2)}, u32[]{:S(2)}) collective-permute-start(bf16[5,32,128]{2,1,0:T(8,128)(2,1)S(1)} %get-tuple-element.28.refs_0_), channel_id=1, source_target_pairs={{16,0},{20,4},{24,8},{28,12},{0,16},{4,20},{8,24},{12,28},{17,1},{... | collective-permute-start | bytes 122888 | tf_op jit(solution)/shard_map/ppermute | solution.py:368
  63.8 4.9 %collective-permute-start.16 = (bf16[5,32,128]{2,1,0:T(8,128)(2,1)S(1)}, bf16[5,32,128]{2,1,0:T(8,128)(2,1)S(1)}, u32[]{:S(2)}, u32[]{:S(2)}) collective-permute-start(bf16[5,32,128]{2,1,0:T(8,128)(2,1)S(1)} %get-tuple-element.28.refs_0_), channel_id=1, source_target_pairs={{12,0},{8,4},{4,8},{0,12},{28,16},{24,20},{20,24},{16,28},{13,1},{... | collective-permute-start | bytes 122888 | tf_op jit(solution)/shard_map/ppermute | solution.py:368
  63.8 5.3 %collective-permute-start.15 = (bf16[5,32,128]{2,1,0:T(8,128)(2,1)S(1)}, bf16[5,32,128]{2,1,0:T(8,128)(2,1)S(1)}, u32[]{:S(2)}, u32[]{:S(2)}) collective-permute-start(bf16[5,32,128]{2,1,0:T(8,128)(2,1)S(1)} %get-tuple-element.28.refs_0_), channel_id=1, source_target_pairs={{8,0},{12,4},{0,8},{4,12},{24,16},{28,20},{16,24},{20,28},{9,1},{1... | collective-permute-start | bytes 122888 | tf_op jit(solution)/shard_map/ppermute | solution.py:368
  66.7 4.0 %collective-permute-start.14 = (bf16[5,32,128]{2,1,0:T(8,128)(2,1)S(1)}, bf16[5,32,128]{2,1,0:T(8,128)(2,1)S(1)}, u32[]{:S(2)}, u32[]{:S(2)}) collective-permute-start(bf16[5,32,128]{2,1,0:T(8,128)(2,1)S(1)} %get-tuple-element.28.refs_0_), channel_id=1, source_target_pairs={{4,0},{0,4},{12,8},{8,12},{20,16},{16,20},{28,24},{24,28},{5,1},{1... | collective-permute-start | bytes 122888 | tf_op jit(solution)/shard_map/ppermute | solution.py:368

commit v2 on v1

--- a/solution.py
+++ b/solution.py
@@ -17,6 +17,7 @@
 DECAY = 0.9
 THRESHOLD = 1.0
 MIB = 1024 * 1024
+SMALL = pl.CostEstimate(flops=1, bytes_accessed=1, transcendentals=0)
 
 
 def params(limit=48):
@@ -33,23 +34,24 @@
     return middle_three(items[4], upper_pair, lower_pair)
 
 
+def picked(code, numbers):
+    sign = jnp.where(code < 0, -1.0, 1.0).astype(jnp.bfloat16)
+    return jnp.where(jnp.abs(code) == numbers, sign, jnp.zeros((), jnp.bfloat16))
+
+
 def partner(index, step, count):
     if count & (count - 1) == 0:
         return index ^ step
     return (index + step) % count
 
 
-def turn(index, step, count):
-    return (index + step) % count
-
-
-def prep_kernel(where, bucket_ref, sign_ref, rows_ref, cols_ref, stacked):
-    share, count = where[1], where[2]
+def codes(wrap, bucket_ref, sign_ref, rows_ref, stacked):
+    share = lax.axis_index("dp") * (NBB // lax.axis_size("dp"))
     quads = rows_ref.shape[0]
     width = quads * BLOCK
     groups = bucket_ref.shape[1] // width
     bucket = bucket_ref[...]
-    bucket = jnp.where(count == 1, bucket ^ share, lax.rem(bucket + (NBB - share), NBB))
+    bucket = lax.rem(bucket + (NBB - share), NBB) if wrap else bucket ^ share
     code = ((bucket + 1) * (2 * sign_ref[...] - 1)).astype(jnp.float32)
     stacked[...] = jnp.zeros_like(stacked)
     for group in range(groups):
@@ -64,32 +66,17 @@
             rows_ref[quad, :, group * BLOCK : (group + 1) * BLOCK] = moved[
                 group * PAD : (group + 1) * PAD, quad * BLOCK : (quad + 1) * BLOCK
             ].astype(rows_ref.dtype)
-    for quad in range(quads):
-        cols_ref[:, quad * PAD : (quad + 1) * PAD] = (
-            rows_ref[quad].astype(jnp.float32).T
-        )
-
-
-def prep(where, bucket, sign_bits, quads):
-    blocks = bucket.shape[1]
-    features = blocks // quads
-    vmem = pl.BlockSpec(memory_space=pltpu.VMEM)
-    return pl.pallas_call(
-        prep_kernel,
-        out_shape=(
-            jax.ShapeDtypeStruct((quads, PAD, features), jnp.bfloat16),
-            jax.ShapeDtypeStruct((features, quads * PAD), jnp.float32),
-        ),
-        in_specs=[pl.BlockSpec(memory_space=pltpu.SMEM), vmem, vmem],
-        out_specs=(vmem, vmem),
-        scratch_shapes=[pltpu.VMEM((features // BLOCK * PAD, quads * BLOCK), jnp.float32)],
-        compiler_params=params(),
-        name="codes",
-    )(where, bucket, sign_bits)
-
-
-def norm_kernel(pair, turns, where, hidden_ref, gain_ref, *out_refs):
-    core, place = where[3], where[4]
+
+
+def front_kernel(wrap, pair, turns, bucket_ref, sign_ref, hidden_ref, gain_ref, *refs):
+    rows_ref, out_refs, stacked = refs[0], refs[1 : 1 + pair], refs[1 + pair]
+
+    @pl.when(pl.program_id(0) == 0)
+    def _():
+        codes(wrap, bucket_ref, sign_ref, rows_ref, stacked)
+
+    fsdp_at = lax.axis_index("fsdp")
+    core, place = lax.rem(fsdp_at, pair), fsdp_at // pair
     features = out_refs[0].shape[2]
     values = hidden_ref[...].astype(jnp.float32)
     inverse_rms = lax.rsqrt(jnp.mean(values * values, axis=1, keepdims=True) + EPS)
@@ -101,24 +88,28 @@
             out_refs[other][step] = (normed * gain_ref[:, span]).astype(jnp.bfloat16)
 
 
-def norm(where, hidden, gain, pair, turns):
+def front(bucket, sign_bits, hidden, gain, quads, wrap, pair, turns, tile=64):
     tokens, width = hidden.shape
     features = width // (pair * turns)
-    tile = min(tokens, 32)
+    tile = min(tokens, tile)
     out = jax.ShapeDtypeStruct((turns, tokens, features), jnp.bfloat16)
     return pl.pallas_call(
-        functools.partial(norm_kernel, pair, turns),
-        out_shape=(out,) * pair,
+        functools.partial(front_kernel, wrap, pair, turns),
+        out_shape=(jax.ShapeDtypeStruct((quads, PAD, features), jnp.bfloat16),) + (out,) * pair,
         grid=(tokens // tile,),
         in_specs=[
-            pl.BlockSpec(memory_space=pltpu.SMEM),
+            pl.BlockSpec(bucket.shape, lambda i: (0, 0)),
+            pl.BlockSpec(bucket.shape, lambda i: (0, 0)),
             pl.BlockSpec((tile, width), lambda i: (i, 0)),
             pl.BlockSpec((1, width), lambda i: (0, 0)),
         ],
-        out_specs=(pl.BlockSpec((turns, tile, features), lambda i: (0, i, 0)),) * pair,
-        compiler_params=params(),
-        name="normed",
-    )(where, hidden, gain)
+        out_specs=(pl.BlockSpec((quads, PAD, features), lambda i: (0, 0, 0)),)
+        + (pl.BlockSpec((turns, tile, features), lambda i: (0, i, 0)),) * pair,
+        scratch_shapes=[pltpu.VMEM((features // BLOCK * PAD, quads * BLOCK), jnp.float32)],
+        compiler_params=params(60),
+        cost_estimate=SMALL,
+        name="codes_and_normed",
+    )(bucket, sign_bits, hidden, gain)
 
 
 def sketch_kernel(scale, count, pair, *refs):
@@ -151,9 +142,7 @@
     for row in range(ROWS):
         picks = []
         for quad in range(quads):
-            code = rows_ref[quad, row : row + 1, :]
-            sign = jnp.where(code < 0, -1.0, 1.0).astype(jnp.bfloat16)
-            picks.append(jnp.where(jnp.abs(code) == numbers, sign, jnp.zeros((), jnp.bfloat16)))
+            picks.append(picked(rows_ref[quad, row : row + 1, :], numbers))
         pick = jnp.concatenate(picks, axis=1)
         total[row] += jnp.dot(pick, both, preferred_element_type=jnp.float32)
 
@@ -168,7 +157,7 @@
                 )
 
 
-def sketch(inputs, cots, rows, which, scale, count, tile=512):
+def sketch(inputs, cots, rows, which, scale, count, tile=2048):
     tokens, features = inputs[0].shape[1:]
     quads = rows.shape[0]
     tile = min(tile, features)
@@ -183,6 +172,7 @@
         out_specs=pl.BlockSpec((count, ROWS, NBB // count, BLOCK), lambda i: (0, 0, 0, 0)),
         scratch_shapes=[pltpu.VMEM((ROWS, NBB, 2 * BLOCK), jnp.float32)],
         compiler_params=params(),
+        cost_estimate=SMALL,
         name="sketch",
     )(*inputs, *cots, rows)
 
@@ -202,7 +192,7 @@
             out_refs[step][other] = grad[step * tokens : (step + 1) * tokens]
 
 
-def grads(cots, weights, tile=512):
+def grads(cots, weights, tile=1024):
     turns, pair = len(cots), len(weights)
     tokens, width = cots[0].shape
     features = weights[0].shape[0]
@@ -215,13 +205,15 @@
         + [pl.BlockSpec((tile, width), lambda i: (i, 0))] * pair,
         out_specs=(pl.BlockSpec((pair, tokens, tile), lambda i: (0, 0, i)),) * turns,
         compiler_params=params(),
+        cost_estimate=SMALL,
         name="input_grad",
     )(*cots, *weights)
 
 
-def backward_kernel(turns, pair, where, hidden_ref, gain_ref, *refs):
+def backward_kernel(turns, pair, hidden_ref, gain_ref, *refs):
     grad_refs, out_ref = refs[:turns], refs[turns]
-    core, place = where[3], where[4]
+    fsdp_at = lax.axis_index("fsdp")
+    core, place = lax.rem(fsdp_at, pair), fsdp_at // pair
     features = grad_refs[0].shape[2]
     width = hidden_ref.shape[1]
     values = hidden_ref[...].astype(jnp.float32)
@@ -243,62 +235,57 @@
         out_ref[:, span] = (inverse_rms * (scaled - normed * mean_term)).astype(jnp.bfloat16)
 
 
-def backward(where, hidden, gain, grad_parts):
+def backward(hidden, gain, grad_parts):
     tokens, width = hidden.shape
     turns, pair = len(grad_parts), grad_parts[0].shape[0]
     features = grad_parts[0].shape[2]
-    tile = min(tokens, 32)
+    tile = min(tokens, 64)
     return pl.pallas_call(
         functools.partial(backward_kernel, turns, pair),
         out_shape=jax.ShapeDtypeStruct((tokens, width), jnp.bfloat16),
         grid=(tokens // tile,),
         in_specs=[
-            pl.BlockSpec(memory_space=pltpu.SMEM),
             pl.BlockSpec((tile, width), lambda i: (i, 0)),
             pl.BlockSpec((1, width), lambda i: (0, 0)),
         ]
         + [pl.BlockSpec((pair, tile, features), lambda i: (0, i, 0))] * turns,
         out_specs=pl.BlockSpec((tile, width), lambda i: (i, 0)),
         compiler_params=params(),
+        cost_estimate=SMALL,
         name="hidden_grad",
-    )(where, hidden, gain, *grad_parts)
+    )(hidden, gain, *grad_parts)
 
 
 def unsketch_kernel(count, *refs):
-    part_refs, cols_ref, rows_ref, error_ref = refs[:count], *refs[count : count + 3]
-    update_ref, error_new_ref, total = refs[count + 3 :]
+    part_refs, rows_ref, error_ref = refs[:count], *refs[count : count + 2]
+    update_ref, error_new_ref, total, tables = refs[count + 2 :]
     step = pl.program_id(0)
-    quads = rows_ref.shape[0]
+    quads, tile = rows_ref.shape[0], rows_ref.shape[2]
     share = NBB // count
-    tile = cols_ref.shape[0]
-    tables = [jnp.concatenate([ref[row] for ref in part_refs], axis=0) for row in range(ROWS)]
-    lanes = (lax.broadcasted_iota(jnp.int32, (tile, NBB), 1) + 1).astype(jnp.float32)
-    numbers = lax.broadcasted_iota(jnp.int32, (share, tile), 0).astype(jnp.bfloat16) + 1
+    numbers = lax.broadcasted_iota(jnp.int32, (NBB, tile), 0).astype(jnp.bfloat16) + 1
 
     @pl.when(step == 0)
     def _():
         total[...] = jnp.zeros_like(total)
+        for row in range(ROWS):
+            table = jnp.concatenate([ref[row] for ref in part_refs], axis=0)
+            tables[row] = table.astype(jnp.float32).T.astype(jnp.bfloat16)
 
     for quad in range(quads):
-        reads = []
+        reads, own = [], []
         for row in range(ROWS):
-            code = cols_ref[:, quad * PAD + row : quad * PAD + row + 1]
-            pick = jnp.where(jnp.abs(code) == lanes, 1.0, 0.0).astype(jnp.bfloat16)
-            read = jnp.dot(pick, tables[row], preferred_element_type=jnp.float32)
-            reads.append(jnp.where(code < 0, -read, read))
+            pick = picked(rows_ref[quad, row : row + 1, :], numbers)
+            own.append(pick[:share])
+            reads.append(jnp.dot(tables[row], pick, preferred_element_type=jnp.float32))
         estimate = middle_five(reads)
-        update = estimate - jnp.clip(estimate, -THRESHOLD, THRESHOLD)
+        update = (estimate - jnp.clip(estimate, -THRESHOLD, THRESHOLD)).T
         update_ref[:, quad * BLOCK : (quad + 1) * BLOCK] = update
         upper = update.astype(jnp.bfloat16)
         lower = (update - upper.astype(jnp.float32)).astype(jnp.bfloat16)
         both = jnp.concatenate([upper, lower], axis=1)
-        picks = []
-        for row in range(ROWS):
-            code = rows_ref[quad, row : row + 1, :]
-            sign = jnp.where(code < 0, -1.0, 1.0).astype(jnp.bfloat16)
-            picks.append(jnp.where(jnp.abs(code) == numbers, sign, jnp.zeros((), jnp.bfloat16)))
-        pick = jnp.concatenate(picks, axis=0)
-        total[...] += jnp.dot(pick, both, preferred_element_type=jnp.float32)
+        total[...] += jnp.dot(
+            jnp.concatenate(own, axis=0), both, preferred_element_type=jnp.float32
+        )
 
     @pl.when(step == pl.num_programs(0) - 1)
     def _():
@@ -307,10 +294,9 @@
             error_new_ref[row] = error_ref[row] - (total[rows, :BLOCK] + total[rows, BLOCK:])
 
 
-def unsketch(parts, cols, rows, error_mid, tile=512):
+def unsketch(parts, rows, error_mid, tile=1024):
     count = len(parts)
-    features = cols.shape[0]
-    quads = rows.shape[0]
+    quads, _, features = rows.shape
     share = NBB // count
     tile = min(tile, features)
     table_spec = pl.BlockSpec((ROWS, share, BLOCK), lambda i: (0, 0, 0))
@@ -322,16 +308,16 @@
         ),
         grid=(features // tile,),
         in_specs=[table_spec] * count
-        + [
-            pl.BlockSpec((tile, quads * PAD), lambda i: (i, 0)),
-            pl.BlockSpec((quads, PAD, tile), lambda i: (0, 0, i)),
-            table_spec,
+        + [pl.BlockSpec((quads, PAD, tile), lambda i: (0, 0, i)), table_spec],
+        out_specs=(pl.BlockSpec((tile, quads * BLOCK), lambda i: (i, 0)), table_spec),
+        scratch_shapes=[
+            pltpu.VMEM((ROWS * share, 2 * BLOCK), jnp.float32),
+            pltpu.VMEM((ROWS, BLOCK, NBB), jnp.bfloat16),
         ],
-        out_specs=(pl.BlockSpec((tile, quads * BLOCK), lambda i: (i, 0)), table_spec),
-        scratch_shapes=[pltpu.VMEM((ROWS * share, 2 * BLOCK), jnp.float32)],
         compiler_params=params(),
+        cost_estimate=SMALL,
         name="unsketch",
-    )(*parts, cols, rows, error_mid)
+    )(*parts, rows, error_mid)
 
 
 def on_device(hidden_states, gain, key_weight, key_cotangent, bucket, sign_bits, momentum, error):
@@ -343,10 +329,7 @@
     quads = key_cotangent.shape[1] // BLOCK
     share = NBB // dp_count
     scale = 1.0 / math.sqrt(tokens * fsdp_count)
-    dp_at, fsdp_at = lax.axis_index("dp"), lax.axis_index("fsdp")
-    core, place = fsdp_at % pair, fsdp_at // pair
-    power = 1 if dp_count & (dp_count - 1) == 0 else 0
-    where = jnp.stack([jnp.int32(0), dp_at * share, jnp.int32(power), core, place]).astype(jnp.int32)
+    wrap = dp_count & (dp_count - 1) != 0
     gain = gain.reshape(1, width)
 
     def across(value):
@@ -367,33 +350,34 @@
     def from_share(value, step):
         return lax.ppermute(value, "dp", [(partner(i, step, dp_count), i) for i in range(dp_count)])
 
-    rows, cols = prep(where, bucket, sign_bits, quads)
+    weights = [key_weight] + ([across(key_weight)] if pair == 2 else [])
+    turn_cots = [key_cotangent] + [from_turn(key_cotangent, step) for step in range(1, turns)]
+    cots = [key_cotangent] + ([across(key_cotangent)] if pair == 2 else [])
+    rows, *inputs = front(
+        bucket, sign_bits, hidden_states, gain, quads, wrap, pair, turns
+    )
+    rows, inputs, turn_cots = lax.optimization_barrier((rows, inputs, turn_cots))
     rows_at = [rows] + [from_turn(rows, step) for step in range(1, turns)]
-    inputs = list(norm(where, hidden_states, gain, pair, turns))
-    cots = [key_cotangent]
     if pair == 2:
         inputs[1] = across(inputs[1])
-        cots.append(across(key_cotangent))
+    grad_parts = grads(turn_cots, weights)
+    rows_at, grad_parts = lax.optimization_barrier((rows_at, grad_parts))
     received = []
     for step in range(1, turns):
         table = sketch(inputs, cots, rows_at[step], step, scale, dp_count)
         received.append(to_turn(table, step))
     table = sketch(inputs, cots, rows, 0, scale, dp_count).astype(jnp.float32)
-    for other in received:
-        table = table + other.astype(jnp.float32)
-
-    weights = [key_weight] + ([across(key_weight)] if pair == 2 else [])
-    turn_cots = [key_cotangent] + [from_turn(key_cotangent, step) for step in range(1, turns)]
-    grad_parts = grads(turn_cots, weights)
     grad_parts = [grad_parts[0]] + [
         from_turn(grad_parts[turns - step], step) for step in range(1, turns)
     ]
-    hidden_grad = backward(where, hidden_states, gain, grad_parts)
-
+    hidden_grad = backward(hidden_states, gain, grad_parts)
+
+    for other in received:
+        table = table + other.astype(jnp.float32)
     sent = table.astype(jnp.bfloat16)
     total = table[0]
     order = sorted(range(1, dp_count), key=lambda step: -bin(step).count("1") * 100 - step)
-    arrived = [to_share(sent[step], step) for step in order]
+    arrived = [to_share(sent[step], step) for step in range(1, dp_count)]
     for part in arrived:
         total = total + part.astype(jnp.float32)
     momentum_new = DECAY * momentum.reshape(ROWS, share, BLOCK) + total / dp_count
@@ -401,7 +385,8 @@
     error_sent = error_mid.astype(jnp.bfloat16)
     gathered = {step: from_share(error_sent, step) for step in order}
     parts = [error_sent] + [gathered[step] for step in range(1, dp_count)]
-    update, error_new = unsketch(parts, cols, rows, error_mid)
+    parts, hidden_grad = lax.optimization_barrier((parts, hidden_grad))
+    update, error_new = unsketch(parts, rows, error_mid)
     return (
         hidden_grad,
         momentum_new.reshape(momentum.shape),

time: 89.3 us -> 72.1 us (0.81)
  Pallas kernels: 43.2 us -> 31 us
  waiting for transfers between devices: 11 us -> 7.97 us
  local copies, waits for them, and re-layouts: 2.5 us -> 0.06 us
    pallas_call x1, Pallas kernels: 14 us -> 7.66 us  [unsketch(): pl.pallas_call(functools.partial(unsketch_kernel, count), out_shape=(jax....]
    pallas_call x2, Pallas kernels: 17.5 us -> 12.6 us  [sketch(): pl.pallas_call(functools.partial(sketch_kernel, scale, count, pair), out_...]
    ppermute x7, waiting for transfers between devices: 3.43 us -> 0.86 us  [from_share(): lax.ppermute(value, 'dp', [(partner(i, step, dp_count), i) for i in range...]
    unnamed x22 -> x16, local copies, waits for them, and re-layouts: 2.39 us -> 0.04 us
    ppermute x4, starting transfers between devices: 6.28 us -> 7.87 us  [from_turn(): return lax.ppermute(value, 'fsdp', pairs)]
    pallas_call x2 -> x1, Pallas kernels: 3.8 us -> 3.93 us  [front(): pl.pallas_call(functools.partial(front_kernel, wrap, pair, turns), out_sh...]
  transfers between devices with their start and end apart: 21 -> 21, of which waited for: 6 -> 9; matrix products, arithmetic and copies ran while one was open for 1% -> 1% of each run, Pallas kernels for 44% -> 24%
where the time goes in v2:
time: 72.1 us; the launch traced here: 71.9 us
  starting transfers between devices  31.1 us (43%)
  Pallas kernels  31 us (43%)
  waiting for transfers between devices  7.97 us (11%)
  other arithmetic  1.08 us (1%)
  between operations  0.78 us (1%)
    pallas_call x2, Pallas kernels, sketch(): pl.pallas_call(functools.partial(sketch_kernel, scale, count, pair), out_...  12.6 us
    ppermute x7, starting transfers between devices, from_share(): lax.ppermute(value, 'dp', [(partner(i, step, dp_count), i) for i in range...  11.2 us
    ppermute x7, starting transfers between devices, to_share(): lax.ppermute(value, 'dp', [(i, partner(i, step, dp_count)) for i in range...  11.2 us
    ppermute x4, starting transfers between devices, from_turn(): return lax.ppermute(value, 'fsdp', pairs)  7.87 us
    pallas_call x1, Pallas kernels, unsketch(): pl.pallas_call(functools.partial(unsketch_kernel, count), out_shape=(jax....  7.66 us
    ppermute x4, waiting for transfers between devices, from_turn(): return lax.ppermute(value, 'fsdp', pairs)  4.08 us
    pallas_call x1, Pallas kernels, front(): pl.pallas_call(functools.partial(front_kernel, wrap, pair, turns), out_sh...  3.93 us
    pallas_call x1, Pallas kernels, backward(): pl.pallas_call(functools.partial(backward_kernel, turns, pair), out_shape...  3.93 us
  transfers between devices with their start and end apart: 21, of which 9 were waited for; matrix products, arithmetic and copies ran while one was open for 1% of the time, Pallas kernels for 24%

profile of v2, /device:TPU:0, one launch (start us, length us, event | category | flops | bytes accessed | tf_op | source)
XLA Modules:
  0.0 71.9 jit_solution(6857369254281496710)
XLA Ops:
  0.6 0.0 copy-start.2
  0.6 0.0 copy-start.3
  0.7 0.5 collective-permute-start.4
  1.2 2.6 %collective-permute-start = (bf16[128,512]{1,0:T(8,128)(2,1)}, bf16[128,512]{1,0:T(8,128)(2,1)S(1)}, u32[]{:S(2)}, u32[]{:S(2)}) collective-permute-start(bf16[128,512]{1,0:T(8,128)(2,1)} %refs_2_.5), channel_id=1, source_target_pairs={{2,0},{3,1},{0,2},{1,3},{6,4},{7,5},{4,6},{5,7},{10,8},{11,9},{8,1... | collective-permute-start | bytes 393224 | tf_op jit(solution)/shard_map/ppermute | solution.py:342
  3.8 3.9 %codes_and_normed.1 = (bf16[4,8,2048]{2,1,0:T(8,128)(2,1)}, bf16[2,128,2048]{2,1,0:T(8,128)(2,1)}, bf16[2,128,2048]{2,1,0:T(8,128)(2,1)}) custom-call(s32[5,8192]{1,0:T(8,128)} %bucket_ref.1, s32[5,8192]{1,0:T(8,128)} %sign_ref.1, bf16[128,8192]{1,0:T(8,128)(2,1)} %hidden_ref.3, f32[1,8192]{1,0:T(1,128)} %bitcast.40), custom_call_target="tpu_custom_call" | custom-call | flops 1 | bytes 1 | tf_op jit(solution)/shard_map/codes_and_normed/pallas_call | solution.py:96
  7.7 0.4 collective-permute-done.refs_1_
  8.1 0.0 collective-permute-start.1
  8.1 1.8 %collective-permute-start.3 = (bf16[4,8,2048]{2,1,0:T(8,128)(2,1)}, bf16[4,8,2048]{2,1,0:T(8,128)(2,1)S(1)}, u32[]{:S(2)}, u32[]{:S(2)}) collective-permute-start(bf16[4,8,2048]{2,1,0:T(8,128)(2,1)} %get-tuple-element.33.refs_4_.refs_8_), channel_id=1, source_target_pairs={{2,0},{3,1},{0,2},{1,3},{6,4},{7,5},{4,6},{5,7},{10,8},{11,9},{8,1... | collective-permute-start | bytes 393224 | tf_op jit(solution)/shard_map/ppermute | solution.py:342
  9.8 0.0 copy-done.3
  9.8 0.2 collective-permute-start.2
  10.1 0.0 collective-permute-done.4.refs_3_
  10.1 0.0 copy-done.2
  10.1 2.8 %input_grad.1 = (bf16[2,128,2048]{2,1,0:T(8,128)(2,1)S(1)}, bf16[2,128,2048]{2,1,0:T(8,128)(2,1)S(1)}) custom-call(bf16[128,512]{1,0:T(8,128)(2,1)S(1)} %copy-done.3, bf16[128,512]{1,0:T(8,128)(2,1)S(1)} %collective-permute-done.refs_1_, bf16[2048,512]{1,0:T(8,128)(2,1)S(1)} %copy-done.2, bf16[2048,512]{1,0:T(8,128)(2,1)} %collective-permute-done.4.refs_3_), custom_call_target="tpu_custom_call" | custom-call | flops 1 | bytes 1 | tf_op jit(solution)/shard_map/input_grad/pallas_call | solution.py:200
  12.9 0.0 copy-start.4
  12.9 1.3 %collective-permute-done.3.refs_4_ = bf16[4,8,2048]{2,1,0:T(8,128)(2,1)S(1)} collective-permute-done((bf16[4,8,2048]{2,1,0:T(8,128)(2,1)}, bf16[4,8,2048]{2,1,0:T(8,128)(2,1)S(1)}, u32[]{:S(2)}, u32[]{:S(2)}) %collective-permute-start.3) | collective-permute-done | bytes 131104 | tf_op jit(solution)/shard_map/ppermute | solution.py:342
  14.2 0.0 collective-permute-done.2.refs_3_
  14.2 0.0 collective-permute-done.1.refs_1_
  14.2 0.0 copy-done.1
  14.2 6.3 %sketch.3 = bf16[8,5,32,128]{3,2,1,0:T(8,128)(2,1)S(1)} custom-call(bf16[2,128,2048]{2,1,0:T(8,128)(2,1)S(1)} %copy-done.1, bf16[2,128,2048]{2,1,0:T(8,128)(2,1)S(1)} %collective-permute-done.1.refs_1_, bf16[128,512]{1,0:T(8,128)(2,1)S(1)} %copy-done.3, bf16[128,512]{1,0:T(8,128)(2,1)S(1)} %collective-permute-done.2.refs_3_, ...), custom_call_target="tpu_custom_call" | custom-call | flops 1 | bytes 1 | tf_op jit(solution)/shard_map/sketch/pallas_call | solution.py:165
  20.5 0.0 copy-start.6
  20.5 0.0 copy-start.7
  20.6 1.8 %collective-permute-start.5 = (bf16[8,5,32,128]{3,2,1,0:T(8,128)(2,1)S(1)}, bf16[8,5,32,128]{3,2,1,0:T(8,128)(2,1)S(1)}, u32[]{:S(2)}, u32[]{:S(2)}) collective-permute-start(bf16[8,5,32,128]{3,2,1,0:T(8,128)(2,1)S(1)} %sketch.3), channel_id=1, source_target_pairs={{2,0},{3,1},{0,2},{1,3},{6,4},{7,5},{4,6},{5,7},{10,8},{11,9},{8,1... | collective-permute-start | bytes 983048 | tf_op jit(solution)/shard_map/ppermute | solution.py:342
  22.4 0.0 copy-done.4
  22.4 6.3 %sketch.2 = bf16[8,5,32,128]{3,2,1,0:T(8,128)(2,1)S(1)} custom-call(bf16[2,128,2048]{2,1,0:T(8,128)(2,1)S(1)} %copy-done.1, bf16[2,128,2048]{2,1,0:T(8,128)(2,1)S(1)} %collective-permute-done.1.refs_1_, bf16[128,512]{1,0:T(8,128)(2,1)S(1)} %copy-done.3, bf16[128,512]{1,0:T(8,128)(2,1)S(1)} %collective-permute-done.2.refs_3_, bf16[4,8,2048]{2,1,0:T(8,128)(2,1)S(1)} %copy-done.4), custom_call_target="tpu_custom_call" | custom-call | flops 1 | bytes 1 | tf_op jit(solution)/shard_map/sketch/pallas_call | solution.py:165
  28.7 0.0 copy-start
  28.7 0.0 copy-start.5
  28.7 1.3 %collective-permute-done.5 = bf16[8,5,32,128]{3,2,1,0:T(8,128)(2,1)S(1)} collective-permute-done((bf16[8,5,32,128]{3,2,1,0:T(8,128)(2,1)S(1)}, bf16[8,5,32,128]{3,2,1,0:T(8,128)(2,1)S(1)}, u32[]{:S(2)}, u32[]{:S(2)}) %collective-permute-start.5) | collective-permute-done | bytes 327712 | tf_op jit(solution)/shard_map/ppermute | solution.py:342
  30.0 0.1 convert_add_fusion
  30.1 1.8 %collective-permute-start.6 = (bf16[5,32,128]{2,1,0:T(8,128)(2,1)S(1)}, bf16[5,32,128]{2,1,0:T(8,128)(2,1)S(1)}, u32[]{:S(2)}, u32[]{:S(2)}) collective-permute-start(bf16[5,32,128]{2,1,0:T(8,128)(2,1)S(1)} %get-tuple-element.65), channel_id=1, source_target_pairs={{0,4},{4,0},{8,12},{12,8},{16,20},{20,16},{24,28},{28,24},{1,5},{5... | collective-permute-start | bytes 122888 | tf_op jit(solution)/shard_map/ppermute | solution.py:348
  31.9 3.6 %collective-permute-start.12 = (bf16[5,32,128]{2,1,0:T(8,128)(2,1)S(1)}, bf16[5,32,128]{2,1,0:T(8,128)(2,1)S(1)}, u32[]{:S(2)}, u32[]{:S(2)}) collective-permute-start(bf16[5,32,128]{2,1,0:T(8,128)(2,1)S(1)} %get-tuple-element.66), channel_id=1, source_target_pairs={{0,28},{4,24},{8,20},{12,16},{16,12},{20,8},{24,4},{28,0},{1,29},{... | collective-permute-start | bytes 122888 | tf_op jit(solution)/shard_map/ppermute | solution.py:348
  35.5 0.0 collective-permute-start.11
  35.5 1.7 %collective-permute-start.20 = (bf16[2,128,2048]{2,1,0:T(8,128)(2,1)S(1)}, bf16[2,128,2048]{2,1,0:T(8,128)(2,1)S(1)}, u32[]{:S(2)}, u32[]{:S(2)}) collective-permute-start(bf16[2,128,2048]{2,1,0:T(8,128)(2,1)S(1)} %get-tuple-element.40), channel_id=1, source_target_pairs={{2,0},{3,1},{0,2},{1,3},{6,4},{7,5},{4,6},{5,7},{10,8},{11,9},{8,1... | collective-permute-start | bytes 3145736 | tf_op jit(solution)/shard_map/ppermute | solution.py:342
  37.2 1.7 %collective-permute-start.10 = (bf16[5,32,128]{2,1,0:T(8,128)(2,1)S(1)}, bf16[5,32,128]{2,1,0:T(8,128)(2,1)S(1)}, u32[]{:S(2)}, u32[]{:S(2)}) collective-permute-start(bf16[5,32,128]{2,1,0:T(8,128)(2,1)S(1)} %get-tuple-element.68), channel_id=1, source_target_pairs={{0,20},{4,16},{8,28},{12,24},{16,4},{20,0},{24,12},{28,8},{1,21},{... | collective-permute-start | bytes 122888 | tf_op jit(solution)/shard_map/ppermute | solution.py:348
  38.9 0.0 collective-permute-done.6
  38.9 2.1 %collective-permute-start.9 = (bf16[5,32,128]{2,1,0:T(8,128)(2,1)S(1)}, bf16[5,32,128]{2,1,0:T(8,128)(2,1)S(1)}, u32[]{:S(2)}, u32[]{:S(2)}) collective-permute-start(bf16[5,32,128]{2,1,0:T(8,128)(2,1)S(1)} %get-tuple-element.69), channel_id=1, source_target_pairs={{0,16},{4,20},{8,24},{12,28},{16,0},{20,4},{24,8},{28,12},{1,17},{... | collective-permute-start | bytes 122888 | tf_op jit(solution)/shard_map/ppermute | solution.py:348
  41.1 0.0 collective-permute-done.12
  41.1 1.3 %collective-permute-start.8 = (bf16[5,32,128]{2,1,0:T(8,128)(2,1)S(1)}, bf16[5,32,128]{2,1,0:T(8,128)(2,1)S(1)}, u32[]{:S(2)}, u32[]{:S(2)}) collective-permute-start(bf16[5,32,128]{2,1,0:T(8,128)(2,1)S(1)} %get-tuple-element.70), channel_id=1, source_target_pairs={{0,12},{4,8},{8,4},{12,0},{16,28},{20,24},{24,20},{28,16},{1,13},{... | collective-permute-start | bytes 122888 | tf_op jit(solution)/shard_map/ppermute | solution.py:348
  42.4 0.0 collective-permute-done.11
  42.4 0.7 collective-permute-start.7
  43.1 0.0 copy-done.6
  43.1 0.3 broadcast_multiply_fusion
  43.4 0.3 collective-permute-done.10
  43.7 0.4 collective-permute-done.9
  44.1 1.9 %collective-permute-done.8 = bf16[5,32,128]{2,1,0:T(8,128)(2,1)S(1)} collective-permute-done((bf16[5,32,128]{2,1,0:T(8,128)(2,1)S(1)}, bf16[5,32,128]{2,1,0:T(8,128)(2,1)S(1)}, u32[]{:S(2)}, u32[]{:S(2)}) %collective-permute-start.8) | collective-permute-done | bytes 40992 | tf_op jit(solution)/shard_map/ppermute | solution.py:348
  46.0 0.4 collective-permute-done.7
  46.4 0.7 fusion.10
  47.1 3.7 %collective-permute-start.19 = (bf16[5,32,128]{2,1,0:T(8,128)(2,1)S(1)}, bf16[5,32,128]{2,1,0:T(8,128)(2,1)S(1)}, u32[]{:S(2)}, u32[]{:S(2)}) collective-permute-start(bf16[5,32,128]{2,1,0:T(8,128)(2,1)S(1)} %get-tuple-element.42.refs_0_), channel_id=1, source_target_pairs={{28,0},{24,4},{20,8},{16,12},{12,16},{8,20},{4,24},{0,28},{29,1},{... | collective-permute-start | bytes 122888 | tf_op jit(solution)/shard_map/ppermute | solution.py:351
  50.7 1.1 %collective-permute-start.18 = (bf16[5,32,128]{2,1,0:T(8,128)(2,1)S(1)}, bf16[5,32,128]{2,1,0:T(8,128)(2,1)S(1)}, u32[]{:S(2)}, u32[]{:S(2)}) collective-permute-start(bf16[5,32,128]{2,1,0:T(8,128)(2,1)S(1)} %get-tuple-element.42.refs_0_), channel_id=1, source_target_pairs={{24,0},{28,4},{16,8},{20,12},{8,16},{12,20},{0,24},{4,28},{25,1},{... | collective-permute-start | bytes 122888 | tf_op jit(solution)/shard_map/ppermute | solution.py:351
  51.8 1.0 %collective-permute-start.17 = (bf16[5,32,128]{2,1,0:T(8,128)(2,1)S(1)}, bf16[5,32,128]{2,1,0:T(8,128)(2,1)S(1)}, u32[]{:S(2)}, u32[]{:S(2)}) collective-permute-start(bf16[5,32,128]{2,1,0:T(8,128)(2,1)S(1)} %get-tuple-element.42.refs_0_), channel_id=1, source_target_pairs={{20,0},{16,4},{28,8},{24,12},{4,16},{0,20},{12,24},{8,28},{21,1},{... | collective-permute-start | bytes 122888 | tf_op jit(solution)/shard_map/ppermute | solution.py:351
  52.9 1.9 %collective-permute-start.16 = (bf16[5,32,128]{2,1,0:T(8,128)(2,1)S(1)}, bf16[5,32,128]{2,1,0:T(8,128)(2,1)S(1)}, u32[]{:S(2)}, u32[]{:S(2)}) collective-permute-start(bf16[5,32,128]{2,1,0:T(8,128)(2,1)S(1)} %get-tuple-element.42.refs_0_), channel_id=1, source_target_pairs={{16,0},{20,4},{24,8},{28,12},{0,16},{4,20},{8,24},{12,28},{17,1},{... | collective-permute-start | bytes 122888 | tf_op jit(solution)/shard_map/ppermute | solution.py:351
  54.7 0.0 collective-permute-done.19.refs_7_
  54.7 1.3 %collective-permute-start.15 = (bf16[5,32,128]{2,1,0:T(8,128)(2,1)S(1)}, bf16[5,32,128]{2,1,0:T(8,128)(2,1)S(1)}, u32[]{:S(2)}, u32[]{:S(2)}) collective-permute-start(bf16[5,32,128]{2,1,0:T(8,128)(2,1)S(1)} %get-tuple-element.42.refs_0_), channel_id=1, source_target_pairs={{12,0},{8,4},{4,8},{0,12},{28,16},{24,20},{20,24},{16,28},{13,1},{... | collective-permute-start | bytes 122888 | tf_op jit(solution)/shard_map/ppermute | solution.py:351
  56.0 0.8 %collective-permute-done.18.refs_6_ = bf16[5,32,128]{2,1,0:T(8,128)(2,1)S(1)} collective-permute-done((bf16[5,32,128]{2,1,0:T(8,128)(2,1)S(1)}, bf16[5,32,128]{2,1,0:T(8,128)(2,1)S(1)}, u32[]{:S(2)}, u32[]{:S(2)}) %collective-permute-start.18) | collective-permute-done | bytes 40992 | tf_op jit(solution)/shard_map/ppermute | solution.py:351
  56.9 0.8 %collective-permute-start.14 = (bf16[5,32,128]{2,1,0:T(8,128)(2,1)S(1)}, bf16[5,32,128]{2,1,0:T(8,128)(2,1)S(1)}, u32[]{:S(2)}, u32[]{:S(2)}) collective-permute-start(bf16[5,32,128]{2,1,0:T(8,128)(2,1)S(1)} %get-tuple-element.42.refs_0_), channel_id=1, source_target_pairs={{8,0},{12,4},{0,8},{4,12},{24,16},{28,20},{16,24},{20,28},{9,1},{1... | collective-permute-start | bytes 122888 | tf_op jit(solution)/shard_map/ppermute | solution.py:351
  57.7 1.2 %collective-permute-done.20.refs_1_ = bf16[2,128,2048]{2,1,0:T(8,128)(2,1)S(1)} collective-permute-done((bf16[2,128,2048]{2,1,0:T(8,128)(2,1)S(1)}, bf16[2,128,2048]{2,1,0:T(8,128)(2,1)S(1)}, u32[]{:S(2)}, u32[]{:S(2)}) %collective-permute-start.20) | collective-permute-done | bytes 1048608 | tf_op jit(solution)/shard_map/ppermute | solution.py:342
  58.8 1.5 %collective-permute-start.13 = (bf16[5,32,128]{2,1,0:T(8,128)(2,1)S(1)}, bf16[5,32,128]{2,1,0:T(8,128)(2,1)S(1)}, u32[]{:S(2)}, u32[]{:S(2)}) collective-permute-start(bf16[5,32,128]{2,1,0:T(8,128)(2,1)S(1)} %get-tuple-element.42.refs_0_), channel_id=1, source_target_pairs={{4,0},{0,4},{12,8},{8,12},{20,16},{16,20},{28,24},{24,28},{5,1},{1... | collective-permute-start | bytes 122888 | tf_op jit(solution)/shard_map/ppermute | solution.py:351
  60.3 0.0 copy-done
  60.3 3.9 %hidden_grad.1 = bf16[128,8192]{1,0:T(8,128)(2,1)} custom-call(bf16[128,8192]{1,0:T(8,128)(2,1)S(1)} %copy-done, f32[1,8192]{1,0:T(1,128)S(1)} %bitcast.41, bf16[2,128,2048]{2,1,0:T(8,128)(2,1)S(1)} %get-tuple-element.39.refs_0_, bf16[2,128,2048]{2,1,0:T(8,128)(2,1)S(1)} %collective-permute-done.20.refs_1_), custom_call_target="tpu_custom_call" | custom-call | flops 1 | bytes 1 | tf_op jit(solution)/shard_map/hidden_grad/pallas_call | solution.py:243
  64.2 0.0 collective-permute-done.17.refs_5_
  64.2 0.0 collective-permute-done.16.refs_4_
  64.3 0.0 collective-permute-done.15.refs_3_
  64.3 0.0 collective-permute-done.14.refs_2_
  64.3 0.0 collective-permute-done.13.refs_1_
  64.3 7.7 %unsketch.1 = (f32[2048,512]{1,0:T(8,128)}, f32[5,32,128]{2,1,0:T(8,128)}) custom-call(bf16[5,32,128]{2,1,0:T(8,128)(2,1)S(1)} %get-tuple-element.42.refs_0_, bf16[5,32,128]{2,1,0:T(8,128)(2,1)S(1)} %collective-permute-done.13.refs_1_, bf16[5,32,128]{2,1,0:T(8,128)(2,1)S(1)} %collective-permute-done.14.refs_2_, ...), custom_call_target="tpu_custom_call" | custom-call | flops 1 | bytes 1 | tf_op jit(solution)/shard_map/unsketch/pallas_call | solution.py:303
  (4 shorter events, 0.0 us)
Async XLA Ops:
  0.6 9.4 %copy-start.2 = (bf16[2048,512]{1,0:T(8,128)(2,1)S(1)}, bf16[2048,512]{1,0:T(8,128)(2,1)}, u32[]{:S(2)}) copy-start(bf16[2048,512]{1,0:T(8,128)(2,1)} %refs_2_.4) | copy-start | bytes 6291460
  0.6 9.2 %copy-start.3 = (bf16[128,512]{1,0:T(8,128)(2,1)S(1)}, bf16[128,512]{1,0:T(8,128)(2,1)}, u32[]{:S(2)}) copy-start(bf16[128,512]{1,0:T(8,128)(2,1)} %refs_2_.5) | copy-start | bytes 393220
  0.7 9.4 %collective-permute-start.4 = (bf16[2048,512]{1,0:T(8,128)(2,1)}, bf16[2048,512]{1,0:T(8,128)(2,1)}, u32[]{:S(2)}, u32[]{:S(2)}) collective-permute-start(bf16[2048,512]{1,0:T(8,128)(2,1)} %refs_2_.4), channel_id=1, source_target_pairs={{0,1},{1,0},{2,3},{3,2},{4,5},{5,4},{6,7},{7,6},{8,9},{9,8},{10,11... | collective-permute-start | bytes 6291464 | tf_op jit(solution)/shard_map/ppermute | solution.py:336
  1.2 6.9 %collective-permute-start = (bf16[128,512]{1,0:T(8,128)(2,1)}, bf16[128,512]{1,0:T(8,128)(2,1)S(1)}, u32[]{:S(2)}, u32[]{:S(2)}) collective-permute-start(bf16[128,512]{1,0:T(8,128)(2,1)} %refs_2_.5), channel_id=1, source_target_pairs={{2,0},{3,1},{0,2},{1,3},{6,4},{7,5},{4,6},{5,7},{10,8},{11,9},{8,1... | collective-permute-start | bytes 393224 | tf_op jit(solution)/shard_map/ppermute | solution.py:342
  8.1 6.1 %copy-start.1 = (bf16[2,128,2048]{2,1,0:T(8,128)(2,1)S(1)}, bf16[2,128,2048]{2,1,0:T(8,128)(2,1)}, u32[]{:S(2)}) copy-start(bf16[2,128,2048]{2,1,0:T(8,128)(2,1)} %get-tuple-element.31.refs_0_) | copy-start | bytes 3145732
  8.1 6.1 %collective-permute-start.1 = (bf16[2,128,2048]{2,1,0:T(8,128)(2,1)}, bf16[2,128,2048]{2,1,0:T(8,128)(2,1)S(1)}, u32[]{:S(2)}, u32[]{:S(2)}) collective-permute-start(bf16[2,128,2048]{2,1,0:T(8,128)(2,1)} %get-tuple-element.32), channel_id=1, source_target_pairs={{0,1},{1,0},{2,3},{3,2},{4,5},{5,4},{6,7},{7,6},{8,9},{9,8},{10,11... | collective-permute-start | bytes 3145736 | tf_op jit(solution)/shard_map/ppermute | solution.py:336
  8.1 6.1 %collective-permute-start.3 = (bf16[4,8,2048]{2,1,0:T(8,128)(2,1)}, bf16[4,8,2048]{2,1,0:T(8,128)(2,1)S(1)}, u32[]{:S(2)}, u32[]{:S(2)}) collective-permute-start(bf16[4,8,2048]{2,1,0:T(8,128)(2,1)} %get-tuple-element.33.refs_4_.refs_8_), channel_id=1, source_target_pairs={{2,0},{3,1},{0,2},{1,3},{6,4},{7,5},{4,6},{5,7},{10,8},{11,9},{8,1... | collective-permute-start | bytes 393224 | tf_op jit(solution)/shard_map/ppermute | solution.py:342
  9.8 4.4 %collective-permute-start.2 = (bf16[128,512]{1,0:T(8,128)(2,1)S(1)}, bf16[128,512]{1,0:T(8,128)(2,1)S(1)}, u32[]{:S(2)}, u32[]{:S(2)}) collective-permute-start(bf16[128,512]{1,0:T(8,128)(2,1)S(1)} %copy-done.3), channel_id=1, source_target_pairs={{0,1},{1,0},{2,3},{3,2},{4,5},{5,4},{6,7},{7,6},{8,9},{9,8},{10,11... | collective-permute-start | bytes 393224 | tf_op jit(solution)/shard_map/ppermute | solution.py:336
  12.9 9.4 %copy-start.4 = (bf16[4,8,2048]{2,1,0:T(8,128)(2,1)S(1)}, bf16[4,8,2048]{2,1,0:T(8,128)(2,1)}, u32[]{:S(2)}) copy-start(bf16[4,8,2048]{2,1,0:T(8,128)(2,1)} %get-tuple-element.33.refs_4_.refs_8_) | copy-start | bytes 393220
  20.5 22.5 %copy-start.6 = (f32[1,5,4096]{2,0,1:T(1,128)S(1)}, f32[1,5,4096]{2,0,1:T(1,128)}, u32[]{:S(2)}) copy-start(f32[1,5,4096]{2,0,1:T(1,128)} %param.14) | copy-start | bytes 245764
  20.5 25.8 %copy-start.7 = (f32[1,5,4096]{2,0,1:T(1,128)S(1)}, f32[1,5,4096]{2,0,1:T(1,128)}, u32[]{:S(2)}) copy-start(f32[1,5,4096]{2,0,1:T(1,128)} %param.15) | copy-start | bytes 245764
  20.6 9.4 %collective-permute-start.5 = (bf16[8,5,32,128]{3,2,1,0:T(8,128)(2,1)S(1)}, bf16[8,5,32,128]{3,2,1,0:T(8,128)(2,1)S(1)}, u32[]{:S(2)}, u32[]{:S(2)}) collective-permute-start(bf16[8,5,32,128]{3,2,1,0:T(8,128)(2,1)S(1)} %sketch.3), channel_id=1, source_target_pairs={{2,0},{3,1},{0,2},{1,3},{6,4},{7,5},{4,6},{5,7},{10,8},{11,9},{8,1... | collective-permute-start | bytes 983048 | tf_op jit(solution)/shard_map/ppermute | solution.py:342
  28.7 31.6 %copy-start = (bf16[128,8192]{1,0:T(8,128)(2,1)S(1)}, bf16[128,8192]{1,0:T(8,128)(2,1)}, u32[]{:S(2)}) copy-start(bf16[128,8192]{1,0:T(8,128)(2,1)} %hidden_ref.3) | copy-start | bytes 6291460
  28.7 31.6 %copy-start.5 = (f32[8192]{0:T(1024)S(1)}, f32[8192]{0:T(1024)}, u32[]{:S(2)}) copy-start(f32[8192]{0:T(1024)} %param.9) | copy-start | bytes 98308
  30.1 8.8 %collective-permute-start.6 = (bf16[5,32,128]{2,1,0:T(8,128)(2,1)S(1)}, bf16[5,32,128]{2,1,0:T(8,128)(2,1)S(1)}, u32[]{:S(2)}, u32[]{:S(2)}) collective-permute-start(bf16[5,32,128]{2,1,0:T(8,128)(2,1)S(1)} %get-tuple-element.65), channel_id=1, source_target_pairs={{0,4},{4,0},{8,12},{12,8},{16,20},{20,16},{24,28},{28,24},{1,5},{5... | collective-permute-start | bytes 122888 | tf_op jit(solution)/shard_map/ppermute | solution.py:348
  31.9 9.2 %collective-permute-start.12 = (bf16[5,32,128]{2,1,0:T(8,128)(2,1)S(1)}, bf16[5,32,128]{2,1,0:T(8,128)(2,1)S(1)}, u32[]{:S(2)}, u32[]{:S(2)}) collective-permute-start(bf16[5,32,128]{2,1,0:T(8,128)(2,1)S(1)} %get-tuple-element.66), channel_id=1, source_target_pairs={{0,28},{4,24},{8,20},{12,16},{16,12},{20,8},{24,4},{28,0},{1,29},{... | collective-permute-start | bytes 122888 | tf_op jit(solution)/shard_map/ppermute | solution.py:348
  35.5 6.9 %collective-permute-start.11 = (bf16[5,32,128]{2,1,0:T(8,128)(2,1)S(1)}, bf16[5,32,128]{2,1,0:T(8,128)(2,1)S(1)}, u32[]{:S(2)}, u32[]{:S(2)}) collective-permute-start(bf16[5,32,128]{2,1,0:T(8,128)(2,1)S(1)} %get-tuple-element.67), channel_id=1, source_target_pairs={{0,24},{4,28},{8,16},{12,20},{16,8},{20,12},{24,0},{28,4},{1,25},{... | collective-permute-start | bytes 122888 | tf_op jit(solution)/shard_map/ppermute | solution.py:348
  35.5 23.3 %collective-permute-start.20 = (bf16[2,128,2048]{2,1,0:T(8,128)(2,1)S(1)}, bf16[2,128,2048]{2,1,0:T(8,128)(2,1)S(1)}, u32[]{:S(2)}, u32[]{:S(2)}) collective-permute-start(bf16[2,128,2048]{2,1,0:T(8,128)(2,1)S(1)} %get-tuple-element.40), channel_id=1, source_target_pairs={{2,0},{3,1},{0,2},{1,3},{6,4},{7,5},{4,6},{5,7},{10,8},{11,9},{8,1... | collective-permute-start | bytes 3145736 | tf_op jit(solution)/shard_map/ppermute | solution.py:342
  37.2 6.5 %collective-permute-start.10 = (bf16[5,32,128]{2,1,0:T(8,128)(2,1)S(1)}, bf16[5,32,128]{2,1,0:T(8,128)(2,1)S(1)}, u32[]{:S(2)}, u32[]{:S(2)}) collective-permute-start(bf16[5,32,128]{2,1,0:T(8,128)(2,1)S(1)} %get-tuple-element.68), channel_id=1, source_target_pairs={{0,20},{4,16},{8,28},{12,24},{16,4},{20,0},{24,12},{28,8},{1,21},{... | collective-permute-start | bytes 122888 | tf_op jit(solution)/shard_map/ppermute | solution.py:348
  38.9 5.2 %collective-permute-start.9 = (bf16[5,32,128]{2,1,0:T(8,128)(2,1)S(1)}, bf16[5,32,128]{2,1,0:T(8,128)(2,1)S(1)}, u32[]{:S(2)}, u32[]{:S(2)}) collective-permute-start(bf16[5,32,128]{2,1,0:T(8,128)(2,1)S(1)} %get-tuple-element.69), channel_id=1, source_target_pairs={{0,16},{4,20},{8,24},{12,28},{16,0},{20,4},{24,8},{28,12},{1,17},{... | collective-permute-start | bytes 122888 | tf_op jit(solution)/shard_map/ppermute | solution.py:348
  41.1 4.9 %collective-permute-start.8 = (bf16[5,32,128]{2,1,0:T(8,128)(2,1)S(1)}, bf16[5,32,128]{2,1,0:T(8,128)(2,1)S(1)}, u32[]{:S(2)}, u32[]{:S(2)}) collective-permute-start(bf16[5,32,128]{2,1,0:T(8,128)(2,1)S(1)} %get-tuple-element.70), channel_id=1, source_target_pairs={{0,12},{4,8},{8,4},{12,0},{16,28},{20,24},{24,20},{28,16},{1,13},{... | collective-permute-start | bytes 122888 | tf_op jit(solution)/shard_map/ppermute | solution.py:348
  42.4 4.0 %collective-permute-start.7 = (bf16[5,32,128]{2,1,0:T(8,128)(2,1)S(1)}, bf16[5,32,128]{2,1,0:T(8,128)(2,1)S(1)}, u32[]{:S(2)}, u32[]{:S(2)}) collective-permute-start(bf16[5,32,128]{2,1,0:T(8,128)(2,1)S(1)} %get-tuple-element.71), channel_id=1, source_target_pairs={{0,8},{4,12},{8,0},{12,4},{16,24},{20,28},{24,16},{28,20},{1,9},{5... | collective-permute-start | bytes 122888 | tf_op jit(solution)/shard_map/ppermute | solution.py:348
  47.1 7.7 %collective-permute-start.19 = (bf16[5,32,128]{2,1,0:T(8,128)(2,1)S(1)}, bf16[5,32,128]{2,1,0:T(8,128)(2,1)S(1)}, u32[]{:S(2)}, u32[]{:S(2)}) collective-permute-start(bf16[5,32,128]{2,1,0:T(8,128)(2,1)S(1)} %get-tuple-element.42.refs_0_), channel_id=1, source_target_pairs={{28,0},{24,4},{20,8},{16,12},{12,16},{8,20},{4,24},{0,28},{29,1},{... | collective-permute-start | bytes 122888 | tf_op jit(solution)/shard_map/ppermute | solution.py:351
  50.7 6.1 %collective-permute-start.18 = (bf16[5,32,128]{2,1,0:T(8,128)(2,1)S(1)}, bf16[5,32,128]{2,1,0:T(8,128)(2,1)S(1)}, u32[]{:S(2)}, u32[]{:S(2)}) collective-permute-start(bf16[5,32,128]{2,1,0:T(8,128)(2,1)S(1)} %get-tuple-element.42.refs_0_), channel_id=1, source_target_pairs={{24,0},{28,4},{16,8},{20,12},{8,16},{12,20},{0,24},{4,28},{25,1},{... | collective-permute-start | bytes 122888 | tf_op jit(solution)/shard_map/ppermute | solution.py:351
  51.8 12.4 %collective-permute-start.17 = (bf16[5,32,128]{2,1,0:T(8,128)(2,1)S(1)}, bf16[5,32,128]{2,1,0:T(8,128)(2,1)S(1)}, u32[]{:S(2)}, u32[]{:S(2)}) collective-permute-start(bf16[5,32,128]{2,1,0:T(8,128)(2,1)S(1)} %get-tuple-element.42.refs_0_), channel_id=1, source_target_pairs={{20,0},{16,4},{28,8},{24,12},{4,16},{0,20},{12,24},{8,28},{21,1},{... | collective-permute-start | bytes 122888 | tf_op jit(solution)/shard_map/ppermute | solution.py:351
  52.9 11.4 %collective-permute-start.16 = (bf16[5,32,128]{2,1,0:T(8,128)(2,1)S(1)}, bf16[5,32,128]{2,1,0:T(8,128)(2,1)S(1)}, u32[]{:S(2)}, u32[]{:S(2)}) collective-permute-start(bf16[5,32,128]{2,1,0:T(8,128)(2,1)S(1)} %get-tuple-element.42.refs_0_), channel_id=1, source_target_pairs={{16,0},{20,4},{24,8},{28,12},{0,16},{4,20},{8,24},{12,28},{17,1},{... | collective-permute-start | bytes 122888 | tf_op jit(solution)/shard_map/ppermute | solution.py:351
  54.7 9.5 %collective-permute-start.15 = (bf16[5,32,128]{2,1,0:T(8,128)(2,1)S(1)}, bf16[5,32,128]{2,1,0:T(8,128)(2,1)S(1)}, u32[]{:S(2)}, u32[]{:S(2)}) collective-permute-start(bf16[5,32,128]{2,1,0:T(8,128)(2,1)S(1)} %get-tuple-element.42.refs_0_), channel_id=1, source_target_pairs={{12,0},{8,4},{4,8},{0,12},{28,16},{24,20},{20,24},{16,28},{13,1},{... | collective-permute-start | bytes 122888 | tf_op jit(solution)/shard_map/ppermute | solution.py:351
  56.9 7.4 %collective-permute-start.14 = (bf16[5,32,128]{2,1,0:T(8,128)(2,1)S(1)}, bf16[5,32,128]{2,1,0:T(8,128)(2,1)S(1)}, u32[]{:S(2)}, u32[]{:S(2)}) collective-permute-start(bf16[5,32,128]{2,1,0:T(8,128)(2,1)S(1)} %get-tuple-element.42.refs_0_), channel_id=1, source_target_pairs={{8,0},{12,4},{0,8},{4,12},{24,16},{28,20},{16,24},{20,28},{9,1},{1... | collective-permute-start | bytes 122888 | tf_op jit(solution)/shard_map/ppermute | solution.py:351
  58.8 5.4 %collective-permute-start.13 = (bf16[5,32,128]{2,1,0:T(8,128)(2,1)S(1)}, bf16[5,32,128]{2,1,0:T(8,128)(2,1)S(1)}, u32[]{:S(2)}, u32[]{:S(2)}) collective-permute-start(bf16[5,32,128]{2,1,0:T(8,128)(2,1)S(1)} %get-tuple-element.42.refs_0_), channel_id=1, source_target_pairs={{4,0},{0,4},{12,8},{8,12},{20,16},{16,20},{28,24},{24,28},{5,1},{1... | collective-permute-start | bytes 122888 | tf_op jit(solution)/shard_map/ppermute | solution.py:351

commit v3 on v2

v3 whole, which is shorter than its diff:
```python
import functools
import math

import jax
import jax.numpy as jnp
from jax import lax
from jax.experimental import pallas as pl
from jax.experimental.pallas import tpu as pltpu
from jax.sharding import PartitionSpec as P

ROWS = 5
NBB = 256
BLOCK = 128
PAD = 8

EPS = 1e-05
DECAY = 0.9
THRESHOLD = 1.0
MIB = 1024 * 1024
HALVES = 2
SMALL = pl.CostEstimate(flops=1, bytes_accessed=1, transcendentals=0)


def params(limit=48):
    return pltpu.CompilerParams(vmem_limit_bytes=limit * MIB)


def middle_three(first, second, third):
    return jnp.maximum(jnp.minimum(first, second), jnp.minimum(jnp.maximum(first, second), third))


def middle_five(items):
    upper_pair = jnp.minimum(jnp.maximum(items[0], items[1]), jnp.maximum(items[2], items[3]))
    lower_pair = jnp.maximum(jnp.minimum(items[0], items[1]), jnp.minimum(items[2], items[3]))
    return middle_three(items[4], upper_pair, lower_pair)


def picked(code, numbers):
    sign = jnp.where(code < 0, -1.0, 1.0).astype(jnp.bfloat16)
    return jnp.where(jnp.abs(code) == numbers, sign, jnp.zeros((), jnp.bfloat16))


def partner(index, step, count):
    if count & (count - 1) == 0:
        return index ^ step
    return (index + step) % count


def codes(wrap, bucket_ref, sign_ref, rows_ref, packed_ref, stacked, packed):
    share = lax.axis_index("dp") * (NBB // lax.axis_size("dp"))
    quads = rows_ref.shape[0]
    width = quads * BLOCK
    groups = bucket_ref.shape[1] // width
    bucket = bucket_ref[...]
    bucket = lax.rem(bucket + (NBB - share), NBB) if wrap else bucket ^ share
    code = ((bucket + 1) * (2 * sign_ref[...] - 1)).astype(jnp.float32)
    stacked[...] = jnp.zeros_like(stacked)
    for group in range(groups):
        stacked[group * PAD : group * PAD + ROWS, :] = code[:, group * width : (group + 1) * width]
    source = lax.broadcasted_iota(jnp.int32, (width, width), 0)
    target = lax.broadcasted_iota(jnp.int32, (width, width), 1)
    chosen = source == quads * (target % BLOCK) + target // BLOCK
    order = jnp.where(chosen, 1.0, 0.0).astype(jnp.bfloat16)
    moved = jnp.dot(stacked[...].astype(jnp.bfloat16), order, preferred_element_type=jnp.float32)
    for group in range(groups):
        for quad in range(quads):
            part = moved[group * PAD : (group + 1) * PAD, quad * BLOCK : (quad + 1) * BLOCK]
            rows_ref[quad, :, group * BLOCK : (group + 1) * BLOCK] = part.astype(rows_ref.dtype)
            half, place = divmod(group, groups // HALVES)
            first = (quad * HALVES + half) * ROWS
            packed[first : first + ROWS, place * BLOCK : (place + 1) * BLOCK] = part[:ROWS]
    packed_ref[...] = packed[...].astype(packed_ref.dtype)


def front_kernel(wrap, pair, turns, bucket_ref, sign_ref, hidden_ref, gain_ref, *refs):
    rows_ref, packed_ref, out_refs = refs[0], refs[1], refs[2 : 2 + pair]

    @pl.when(pl.program_id(0) == 0)
    def _():
        codes(wrap, bucket_ref, sign_ref, rows_ref, packed_ref, *refs[2 + pair :])

    fsdp_at = lax.axis_index("fsdp")
    core, place = lax.rem(fsdp_at, pair), fsdp_at // pair
    features = out_refs[0].shape[2]
    values = hidden_ref[...].astype(jnp.float32)
    inverse_rms = lax.rsqrt(jnp.mean(values * values, axis=1, keepdims=True) + EPS)
    for other in range(pair):
        for step in range(turns):
            slab = lax.rem(place + step, turns) * pair + (core ^ other)
            span = pl.ds(pl.multiple_of(slab * features, BLOCK), features)
            normed = hidden_ref[:, span].astype(jnp.float32) * inverse_rms
            out_refs[other][step] = (normed * gain_ref[:, span]).astype(jnp.bfloat16)


def front(bucket, sign_bits, hidden, gain, quads, wrap, pair, turns, tile=64):
    tokens, width = hidden.shape
    features = width // (pair * turns)
    tile = min(tokens, tile)
    out = jax.ShapeDtypeStruct((turns, tokens, features), jnp.bfloat16)
    packed = (quads * HALVES * ROWS, features // HALVES)
    return pl.pallas_call(
        functools.partial(front_kernel, wrap, pair, turns),
        out_shape=(
            jax.ShapeDtypeStruct((quads, PAD, features), jnp.bfloat16),
            jax.ShapeDtypeStruct(packed, jnp.bfloat16),
        )
        + (out,) * pair,
        grid=(tokens // tile,),
        in_specs=[
            pl.BlockSpec(bucket.shape, lambda i: (0, 0)),
            pl.BlockSpec(bucket.shape, lambda i: (0, 0)),
            pl.BlockSpec((tile, width), lambda i: (i, 0)),
            pl.BlockSpec((1, width), lambda i: (0, 0)),
        ],
        out_specs=(
            pl.BlockSpec((quads, PAD, features), lambda i: (0, 0, 0)),
            pl.BlockSpec(packed, lambda i: (0, 0)),
        )
        + (pl.BlockSpec((turns, tile, features), lambda i: (0, i, 0)),) * pair,
        scratch_shapes=[
            pltpu.VMEM((features // BLOCK * PAD, quads * BLOCK), jnp.float32),
            pltpu.VMEM(packed, jnp.float32),
        ],
        compiler_params=params(60),
        cost_estimate=SMALL,
        name="codes_and_normed",
    )(bucket, sign_bits, hidden, gain)


def sketch_kernel(scale, count, near, pair, quads, *refs):
    inputs_refs, cot_refs, rows_ref = refs[:pair], refs[pair : 2 * pair], refs[2 * pair]
    table_ref = refs[2 * pair + 1]
    contract = (((0,), (0,)), ((), ()))
    inputs = jnp.concatenate([ref[0] for ref in inputs_refs], axis=0)
    cots = jnp.concatenate([ref[...] for ref in cot_refs], axis=0)
    grad = lax.dot_general(inputs, cots, contract, preferred_element_type=jnp.float32) * scale
    upper = grad.astype(jnp.bfloat16)
    lower = (grad - upper.astype(jnp.float32)).astype(jnp.bfloat16)
    both = jnp.concatenate(
        [
            jnp.concatenate(
                [part[:, quad * BLOCK : (quad + 1) * BLOCK] for part in (upper, lower)], axis=1
            )
            for quad in range(quads)
        ],
        axis=0,
    )
    features = inputs.shape[1]
    pieces = 1 if len(rows_ref.shape) == 3 else HALVES
    numbers = lax.broadcasted_iota(jnp.int32, (NBB, features // pieces), 0)
    numbers = numbers.astype(jnp.bfloat16) + 1
    share = NBB // count
    for row in range(ROWS):
        picks = []
        for quad in range(quads):
            for piece in range(pieces):
                if pieces == 1:
                    code = rows_ref[quad, row : row + 1, :]
                else:
                    at = (quad * HALVES + piece) * ROWS + row
                    code = rows_ref[at : at + 1, :]
                picks.append(picked(code, numbers))
        pick = jnp.concatenate(picks, axis=1)
        sums = jnp.dot(pick, both, preferred_element_type=jnp.float32)
        table = sums[:, :BLOCK] + sums[:, BLOCK:]
        for part in range(count):
            table_ref[part % near * (count // near) + part // near, row] = table[part * share : (part + 1) * share, :].astype(
                table_ref.dtype
            )


def sketch(inputs, cots, rows, which, scale, count, near):
    tokens, features = inputs[0].shape[1:]
    quads = cots[0].shape[1] // BLOCK
    pair = len(inputs)
    table = (count, ROWS, NBB // count, BLOCK)
    return pl.pallas_call(
        functools.partial(sketch_kernel, scale, count, near, pair, quads),
        out_shape=jax.ShapeDtypeStruct(table, jnp.bfloat16),
        grid=(1,),
        in_specs=[pl.BlockSpec((1, tokens, features), lambda i: (which, 0, 0))] * pair
        + [pl.BlockSpec(cots[0].shape, lambda i: (0, 0))] * pair
        + [pl.BlockSpec(rows.shape, lambda i: (0,) * rows.ndim)],
        out_specs=pl.BlockSpec(table, lambda i: (0, 0, 0, 0)),
        compiler_params=params(),
        cost_estimate=pl.CostEstimate(
            flops=4 * ROWS * NBB * quads * features * BLOCK,
            bytes_accessed=4 * pair * tokens * features,
            transcendentals=0,
        ),
        name="sketch",
    )(*inputs, *cots, rows)


def grads_kernel(turns, *refs):
    cot_refs, weight_refs, out_refs = refs[:turns], refs[turns:-turns], refs[-turns:]
    cots = jnp.concatenate([ref[...] for ref in cot_refs], axis=0)
    tokens = cot_refs[0].shape[0]
    for index, weight_ref in enumerate(weight_refs):
        grad = lax.dot_general(
            cots, weight_ref[...], (((1,), (1,)), ((), ())), preferred_element_type=jnp.float32
        ).astype(jnp.bfloat16)
        for step in range(turns):
            out_refs[step][index] = grad[step * tokens : (step + 1) * tokens]


def grads(cots, weights, pieces):
    turns = len(cots)
    tokens, width = cots[0].shape
    size = weights[0].shape[0] // HALVES
    out = (len(pieces), tokens, size)
    return pl.pallas_call(
        functools.partial(grads_kernel, turns),
        out_shape=(jax.ShapeDtypeStruct(out, jnp.bfloat16),) * turns,
        grid=(1,),
        in_specs=[pl.BlockSpec((tokens, width), lambda i: (0, 0))] * turns
        + [
            pl.BlockSpec((size, width), functools.partial(lambda half, i: (half, 0), half))
            for _, half in pieces
        ],
        out_specs=(pl.BlockSpec(out, lambda i: (0, 0, 0)),) * turns,
        compiler_params=params(),
        cost_estimate=SMALL,
        name="input_grad",
    )(*cots, *[weights[other] for other, _ in pieces])


def backward_kernel(turns, pair, pieces, hidden_ref, gain_ref, *refs):
    grad_refs, out_ref = refs[:-1], refs[-1]
    fsdp_at = lax.axis_index("fsdp")
    core, place = lax.rem(fsdp_at, pair), fsdp_at // pair
    width = hidden_ref.shape[1]
    features = width // (turns * pair)
    size = features // HALVES
    spans = []
    squares = jnp.zeros((hidden_ref.shape[0], BLOCK), jnp.float32)
    products = squares
    for (step, halves), grad_ref in zip(pieces, grad_refs):
        for index, (other, half) in enumerate(halves):
            slab = lax.rem(place + step, turns) * pair + (core ^ other)
            start = slab * features + half * size
            for part in range(0, size, BLOCK):
                span = pl.ds(pl.multiple_of(start + part, BLOCK), BLOCK)
                values = hidden_ref[:, span].astype(jnp.float32)
                grad = grad_ref[index, :, part : part + BLOCK].astype(jnp.float32)
                squares += values * values
                products += grad * gain_ref[:, span] * values
            spans.append((grad_ref, index, pl.ds(pl.multiple_of(start, BLOCK), size)))
    inverse_rms = lax.rsqrt(jnp.sum(squares, axis=1, keepdims=True) / width + EPS)
    mean_term = inverse_rms * jnp.sum(products, axis=1, keepdims=True) / width
    shrink = inverse_rms * (inverse_rms * mean_term)
    for grad_ref, index, span in spans:
        scaled = grad_ref[index].astype(jnp.float32) * gain_ref[:, span]
        values = hidden_ref[:, span].astype(jnp.float32)
        out_ref[:, span] = (inverse_rms * scaled - shrink * values).astype(jnp.bfloat16)


def backward(hidden, gain, grad_parts, pieces, turns, pair, tile=32):
    tokens, width = hidden.shape
    tile = min(tokens, tile)
    return pl.pallas_call(
        functools.partial(backward_kernel, turns, pair, pieces),
        out_shape=jax.ShapeDtypeStruct((tokens, width), jnp.bfloat16),
        grid=(tokens // tile,),
        in_specs=[
            pl.BlockSpec((tile, width), lambda i: (i, 0)),
            pl.BlockSpec((1, width), lambda i: (0, 0)),
        ]
        + [
            pl.BlockSpec((part.shape[0], tile, part.shape[2]), lambda i: (0, i, 0))
            for part in grad_parts
        ],
        out_specs=pl.BlockSpec((tile, width), lambda i: (i, 0)),
        compiler_params=params(),
        cost_estimate=SMALL,
        name="hidden_grad",
    )(hidden, gain, *grad_parts)


def unsketch_kernel(groups, share, *refs):
    part_refs, rows_ref, error_ref = refs[:groups], *refs[groups : groups + 2]
    update_ref, error_new_ref, total, tables = refs[groups + 2 :]
    step = pl.program_id(0)
    quads, tile = rows_ref.shape[0], rows_ref.shape[2]
    numbers = lax.broadcasted_iota(jnp.int32, (NBB, tile), 0).astype(jnp.bfloat16) + 1

    @pl.when(step == 0)
    def _():
        total[...] = jnp.zeros_like(total)
        for row in range(ROWS):
            table = jnp.concatenate(
                [ref[near, row] for ref in part_refs for near in range(ref.shape[0])], axis=0
            )
            tables[row] = table.astype(jnp.float32).T.astype(jnp.bfloat16)

    for quad in range(quads):
        reads, own = [], []
        for row in range(ROWS):
            pick = picked(rows_ref[quad, row : row + 1, :], numbers)
            own.append(pick[:share])
            reads.append(jnp.dot(tables[row], pick, preferred_element_type=jnp.float32))
        estimate = middle_five(reads)
        update = (estimate - jnp.clip(estimate, -THRESHOLD, THRESHOLD)).T
        update_ref[:, quad * BLOCK : (quad + 1) * BLOCK] = update
        upper = update.astype(jnp.bfloat16)
        lower = (update - upper.astype(jnp.float32)).astype(jnp.bfloat16)
        both = jnp.concatenate([upper, lower], axis=1)
        total[...] += jnp.dot(
            jnp.concatenate(own, axis=0), both, preferred_element_type=jnp.float32
        )

    @pl.when(step == pl.num_programs(0) - 1)
    def _():
        for row in range(ROWS):
            rows = slice(row * share, (row + 1) * share)
            error_new_ref[row] = error_ref[row] - (total[rows, :BLOCK] + total[rows, BLOCK:])


def unsketch(parts, rows, error_mid, tile=1024):
    groups, near, share = len(parts), parts[0].shape[0], parts[0].shape[2]
    quads, _, features = rows.shape
    tile = min(tile, features)
    table_spec = pl.BlockSpec((ROWS, share, BLOCK), lambda i: (0, 0, 0))
    return pl.pallas_call(
        functools.partial(unsketch_kernel, groups, share),
        out_shape=(
            jax.ShapeDtypeStruct((features, quads * BLOCK), jnp.float32),
            jax.ShapeDtypeStruct((ROWS, share, BLOCK), jnp.float32),
        ),
        grid=(features // tile,),
        in_specs=[pl.BlockSpec((near, ROWS, share, BLOCK), lambda i: (0, 0, 0, 0))] * groups
        + [pl.BlockSpec((quads, PAD, tile), lambda i: (0, 0, i)), table_spec],
        out_specs=(pl.BlockSpec((tile, quads * BLOCK), lambda i: (i, 0)), table_spec),
        scratch_shapes=[
            pltpu.VMEM((ROWS * share, 2 * BLOCK), jnp.float32),
            pltpu.VMEM((ROWS, BLOCK, NBB), jnp.bfloat16),
        ],
        compiler_params=params(),
        cost_estimate=SMALL,
        name="unsketch",
    )(*parts, rows, error_mid)


def on_device(hidden_states, gain, key_weight, key_cotangent, bucket, sign_bits, momentum, error):
    fsdp_count = lax.axis_size("fsdp")
    dp_count = lax.axis_size("dp")
    pair = 2 if fsdp_count % 2 == 0 else 1
    turns = fsdp_count // pair
    tokens, width = hidden_states.shape
    quads = key_cotangent.shape[1] // BLOCK
    share = NBB // dp_count
    scale = 1.0 / math.sqrt(tokens * fsdp_count)
    wrap = dp_count & (dp_count - 1) != 0
    near = 1 if wrap or dp_count == 1 else 2
    gain = gain.reshape(1, width)
    decayed = DECAY * momentum.reshape(ROWS, share, BLOCK)
    carried, decayed = lax.optimization_barrier(
        (error.reshape(ROWS, share, BLOCK) + decayed, decayed)
    )

    def across(value):
        return lax.ppermute(value, "fsdp", [(i, i ^ 1) for i in range(fsdp_count)])

    def from_turn(value, step):
        pairs = [
            (((i // pair + step) % turns) * pair + i % pair, i) for i in range(fsdp_count)
        ]
        return lax.ppermute(value, "fsdp", pairs)

    def to_turn(value, step):
        return from_turn(value, turns - step)

    def to_share(value, step):
        return lax.ppermute(value, "dp", [(i, partner(i, step, dp_count)) for i in range(dp_count)])

    def from_share(value, step):
        return lax.ppermute(value, "dp", [(partner(i, step, dp_count), i) for i in range(dp_count)])

    turn_cots = [key_cotangent] + [from_turn(key_cotangent, step) for step in range(1, turns)]
    rows, packed, *inputs = front(
        bucket, sign_bits, hidden_states, gain, quads, wrap, pair, turns
    )
    packed, inputs, turn_cots, cotangent = lax.optimization_barrier(
        (packed, inputs, turn_cots, key_cotangent)
    )
    packed_at = [from_turn(packed, step) for step in range(1, turns)]
    cots, weights = [key_cotangent], [key_weight]
    if pair == 2:
        inputs[1] = across(inputs[1])
        cots.append(across(cotangent))
    first_half, *halves = [(other, half) for other in range(pair) for half in range(HALVES)]
    back = range(turns - 1, 0, -1)
    first_grads = grads(turn_cots, weights, [first_half])
    inputs, first_grads = lax.optimization_barrier((inputs, first_grads))
    first_grads = [first_grads[0]] + [from_turn(first_grads[step], step) for step in back]
    tables = [
        sketch(inputs, cots, packed_at[step - 1], step, scale, dp_count, near)
        for step in range(1, turns)
    ]
    tables, first_grads, weight = lax.optimization_barrier((tables, first_grads, key_weight))
    if pair == 2:
        weights.append(across(weight))
    received = [to_turn(tables[step - 1], step) for step in range(1, turns)]
    table = sketch(inputs, cots, rows, 0, scale, dp_count, near)
    table, turn_cots = lax.optimization_barrier((table, turn_cots))
    table = table.astype(jnp.float32)
    last_grads = grads(turn_cots, weights, halves)
    received, last_grads = lax.optimization_barrier((received, last_grads))
    last_grads = [last_grads[0]] + [from_turn(last_grads[step], step) for step in back]
    grad_parts = first_grads + last_grads
    pieces = [(step, [first_half]) for step in range(turns)]
    pieces += [(step, halves) for step in range(turns)]
    hidden_grad = backward(hidden_states, gain, grad_parts, pieces, turns, pair)

    for other in received:
        table = table + other.astype(jnp.float32)
    if near == 2:
        halves_at = dp_count // near
        arrived = to_share(table[halves_at:].astype(jnp.bfloat16), 1)
        table = table[:halves_at] + arrived.astype(jnp.float32)
    sent = table.astype(jnp.bfloat16)
    total = table[0]
    for step in range(near, dp_count, near):
        total = total + to_share(sent[step // near], step).astype(jnp.float32)
    error_mid = carried + total / dp_count
    error_sent = error_mid.astype(jnp.bfloat16)[None]
    error_sent, total = lax.optimization_barrier((error_sent, total))
    momentum_new = decayed + total / dp_count
    if near == 2:
        error_sent = jnp.concatenate([error_sent, from_share(error_sent, 1)], axis=0)
    parts = [error_sent] + [from_share(error_sent, step) for step in range(near, dp_count, near)]
    parts, hidden_grad = lax.optimization_barrier((parts, hidden_grad))
    update, error_new = unsketch(parts, rows, error_mid)
    return (
        hidden_grad,
        momentum_new.reshape(momentum.shape),
        error_new.reshape(error.shape),
        update,
    )


def solution(mesh):
    in_specs = (
        P(("dp", "fsdp"), None),
        P(),
        P("fsdp", None),
        P(("dp", "fsdp"), None),
        P(None, "fsdp"),
        P(None, "fsdp"),
        P("fsdp", None, "dp"),
        P("fsdp", None, "dp"),
    )
    out_specs = (
        P(("dp", "fsdp"), None),
        P("fsdp", None, "dp"),
        P("fsdp", None, "dp"),
        P("fsdp", None),
    )
    return jax.shard_map(
        on_device, mesh=mesh, in_specs=in_specs, out_specs=out_specs, check_vma=False
    )
```

time: 72.1 us -> 65.5 us (0.908)
  starting transfers between devices: 31.1 us -> 21.2 us
  waiting for transfers between devices: 7.97 us -> 12.9 us
  Pallas kernels: 31 us -> 29.4 us
    ppermute x7 -> x4, starting transfers between devices: 11.2 us -> 5.79 us  [to_share(): lax.ppermute(value, 'dp', [(i, partner(i, step, dp_count)) for i in range...]
    ppermute x7 -> x4, starting transfers between devices: 11.2 us -> 6 us  [from_share(): lax.ppermute(value, 'dp', [(partner(i, step, dp_count), i) for i in range...]
    ppermute x7 -> x4, waiting for transfers between devices: 3.02 us -> 7.95 us  [to_share(): lax.ppermute(value, 'dp', [(i, partner(i, step, dp_count)) for i in range...]
    ppermute x4 -> x5, waiting for transfers between devices: 4.08 us -> 1.78 us  [from_turn(): return lax.ppermute(value, 'fsdp', pairs)]
    ppermute x7 -> x4, waiting for transfers between devices: 0.86 us -> 2.51 us  [from_share(): lax.ppermute(value, 'dp', [(partner(i, step, dp_count), i) for i in range...]
    pallas_call x5 -> x6, Pallas kernels: 27.1 us -> 25.5 us  [the longest x2 12.6 us: sketch(): pl.pallas_call(functools.partial(sketch_kernel, scale, count, near, pair,...]
    ppermute x4 -> x5, starting transfers between devices: 7.87 us -> 8.76 us  [from_turn(): return lax.ppermute(value, 'fsdp', pairs)]
  transfers between devices with their start and end apart: 21 -> 16, of which waited for: 9 -> 7; matrix products, arithmetic and copies ran while one was open for 1% -> 1% of each run, Pallas kernels for 24% -> 33%
where the time goes in v3:
time: 65.5 us; the launch traced here: 65.4 us
  Pallas kernels  29.4 us (45%)
  starting transfers between devices  21.2 us (32%)
  waiting for transfers between devices  12.9 us (20%)
  other arithmetic  0.92 us (1%)
  between operations  0.83 us (1%)
    pallas_call x2, Pallas kernels, sketch(): pl.pallas_call(functools.partial(sketch_kernel, scale, count, near, pair,...  12.6 us
    ppermute x5, starting transfers between devices, from_turn(): return lax.ppermute(value, 'fsdp', pairs)  8.76 us
    ppermute x4, waiting for transfers between devices, to_share(): lax.ppermute(value, 'dp', [(i, partner(i, step, dp_count)) for i in range...  7.95 us
    pallas_call x1, Pallas kernels, unsketch(): pl.pallas_call(functools.partial(unsketch_kernel, groups, share), out_sha...  7.65 us
    ppermute x4, starting transfers between devices, from_share(): lax.ppermute(value, 'dp', [(partner(i, step, dp_count), i) for i in range...  6 us
    ppermute x4, starting transfers between devices, to_share(): lax.ppermute(value, 'dp', [(i, partner(i, step, dp_count)) for i in range...  5.79 us
    pallas_call x1, Pallas kernels, front(): pl.pallas_call(functools.partial(front_kernel, wrap, pair, turns), out_sh...  3.96 us
    pallas_call x1, Pallas kernels, backward(): pl.pallas_call(functools.partial(backward_kernel, turns, pair, pieces), o...  3.56 us
  transfers between devices with their start and end apart: 16, of which 7 were waited for; matrix products, arithmetic and copies ran while one was open for 1% of the time, Pallas kernels for 33%

profile of v3, /device:TPU:0, one launch (start us, length us, event | category | flops | bytes accessed | tf_op | source)
XLA Modules:
  0.0 65.4 jit_solution(15086529604829094457)
XLA Ops:
  0.6 0.0 copy-start.2
  0.6 0.0 copy-start
  0.7 3.0 %collective-permute-start = (bf16[128,512]{1,0:T(8,128)(2,1)}, bf16[128,512]{1,0:T(8,128)(2,1)S(1)}, u32[]{:S(2)}, u32[]{:S(2)}) collective-permute-start(bf16[128,512]{1,0:T(8,128)(2,1)} %refs_0_.1), channel_id=1, source_target_pairs={{2,0},{3,1},{0,2},{1,3},{6,4},{7,5},{4,6},{5,7},{10,8},{11,9},{8,1... | collective-permute-start | bytes 393224 | tf_op jit(solution)/shard_map/ppermute | solution.py:368
  3.7 4.0 %codes_and_normed.1 = (bf16[4,8,2048]{2,1,0:T(8,128)(2,1)}, bf16[40,1024]{1,0:T(8,128)(2,1)}, bf16[2,128,2048]{2,1,0:T(8,128)(2,1)}, bf16[2,128,2048]{2,1,0:T(8,128)(2,1)}) custom-call(s32[5,8192]{1,0:T(8,128)} %bucket_ref.1, s32[5,8192]{1,0:T(8,128)} %sign_ref.1, bf16[128,8192]{1,0:T(8,128)(2,1)} %hidden_ref.3, f32[1,8192]{1,0:T(1,128)} %bitcast.22), custom_call_target="tpu_custom_call" | custom-call | flops 1 | bytes 1 | tf_op jit(solution)/shard_map/codes_and_normed/pallas_call | solution.py:101
  7.6 0.0 copy-start.5
  7.6 0.0 collective-permute-done.refs_1_
  7.7 0.1 collective-permute-start.1
  7.7 0.0 copy-done.2
  7.7 0.5 collective-permute-start.2
  8.2 1.4 %collective-permute-start.3 = (bf16[40,1024]{1,0:T(8,128)(2,1)}, bf16[40,1024]{1,0:T(8,128)(2,1)S(1)}, u32[]{:S(2)}, u32[]{:S(2)}) collective-permute-start(bf16[40,1024]{1,0:T(8,128)(2,1)} %get-tuple-element.58), channel_id=1, source_target_pairs={{2,0},{3,1},{0,2},{1,3},{6,4},{7,5},{4,6},{5,7},{10,8},{11,9},{8,1... | collective-permute-start | bytes 245768 | tf_op jit(solution)/shard_map/ppermute | solution.py:368
  9.6 0.0 copy-done
  9.6 0.5 input_grad.2
  10.1 0.7 collective-permute-done.1.refs_1_
  10.8 0.0 copy-start.4
  10.8 1.4 %collective-permute-start.4 = (bf16[1,128,1024]{2,1,0:T(8,128)(2,1)S(1)}, bf16[1,128,1024]{2,1,0:T(8,128)(2,1)S(1)}, u32[]{:S(2)}, u32[]{:S(2)}) collective-permute-start(bf16[1,128,1024]{2,1,0:T(8,128)(2,1)S(1)} %get-tuple-element.60), channel_id=1, source_target_pairs={{2,0},{3,1},{0,2},{1,3},{6,4},{7,5},{4,6},{5,7},{10,8},{11,9},{8,1... | collective-permute-start | bytes 786440 | tf_op jit(solution)/shard_map/ppermute | solution.py:368
  12.2 0.7 %collective-permute-done.3.refs_4_ = bf16[40,1024]{1,0:T(8,128)(2,1)S(1)} collective-permute-done((bf16[40,1024]{1,0:T(8,128)(2,1)}, bf16[40,1024]{1,0:T(8,128)(2,1)S(1)}, u32[]{:S(2)}, u32[]{:S(2)}) %collective-permute-start.3) | collective-permute-done | bytes 81952 | tf_op jit(solution)/shard_map/ppermute | solution.py:368
  12.9 0.0 collective-permute-done.2.refs_3_
  12.9 0.0 copy-done.5
  12.9 6.3 %sketch.3 = bf16[8,5,32,128]{3,2,1,0:T(8,128)(2,1)S(1)} custom-call(bf16[2,128,2048]{2,1,0:T(8,128)(2,1)S(1)} %copy-done.5, bf16[2,128,2048]{2,1,0:T(8,128)(2,1)S(1)} %collective-permute-done.1.refs_1_, bf16[128,512]{1,0:T(8,128)(2,1)S(1)} %copy-done.2, bf16[128,512]{1,0:T(8,128)(2,1)S(1)} %collective-permute-done.2.refs_3_, ...), custom_call_target="tpu_custom_call" | custom-call | flops 5368709120 | bytes 2097152 | tf_op jit(solution)/shard_map/sketch/pallas_call | solution.py:177
  19.2 0.0 collective-permute-done.4.refs_1_
  19.2 0.1 collective-permute-start.6
  19.3 1.5 %collective-permute-start.5 = (bf16[8,5,32,128]{3,2,1,0:T(8,128)(2,1)S(1)}, bf16[8,5,32,128]{3,2,1,0:T(8,128)(2,1)S(1)}, u32[]{:S(2)}, u32[]{:S(2)}) collective-permute-start(bf16[8,5,32,128]{3,2,1,0:T(8,128)(2,1)S(1)} %sketch.3), channel_id=1, source_target_pairs={{2,0},{3,1},{0,2},{1,3},{6,4},{7,5},{4,6},{5,7},{10,8},{11,9},{8,1... | collective-permute-start | bytes 983048 | tf_op jit(solution)/shard_map/ppermute | solution.py:368
  20.8 0.0 copy-done.4
  20.8 6.3 %sketch.2 = bf16[8,5,32,128]{3,2,1,0:T(8,128)(2,1)S(1)} custom-call(bf16[2,128,2048]{2,1,0:T(8,128)(2,1)S(1)} %copy-done.5, bf16[2,128,2048]{2,1,0:T(8,128)(2,1)S(1)} %collective-permute-done.1.refs_1_, bf16[128,512]{1,0:T(8,128)(2,1)S(1)} %copy-done.2, bf16[128,512]{1,0:T(8,128)(2,1)S(1)} %collective-permute-done.2.refs_3_, bf16[4,8,2048]{2,1,0:T(8,128)(2,1)S(1)} %copy-done.4), custom_call_target="tpu_custom_call" | custom-call | flops 5368709120 | bytes 2097152 | tf_op jit(solution)/shard_map/sketch/pallas_call | solution.py:177
  27.1 0.0 collective-permute-done.6.refs_3_.refs_4_
  27.1 1.2 %input_grad.3 = (bf16[3,128,1024]{2,1,0:T(8,128)(2,1)S(1)}, bf16[3,128,1024]{2,1,0:T(8,128)(2,1)S(1)}) custom-call(bf16[128,512]{1,0:T(8,128)(2,1)S(1)} %copy-done.2, bf16[128,512]{1,0:T(8,128)(2,1)S(1)} %collective-permute-done.refs_1_, bf16[2048,512]{1,0:T(8,128)(2,1)S(1)} %copy-done, bf16[2048,512]{1,0:T(8,128)(2,1)S(1)} %collective-permute-done.6.refs_3_.refs_4_, ...), custom_call_target="tpu_custom_call" | custom-call | flops 1 | bytes 1 | tf_op jit(solution)/shard_map/input_grad/pallas_call | solution.py:212
  28.3 0.0 copy-start.6
  28.3 0.0 copy-start.7
  28.3 1.1 %collective-permute-done.5 = bf16[8,5,32,128]{3,2,1,0:T(8,128)(2,1)S(1)} collective-permute-done((bf16[8,5,32,128]{3,2,1,0:T(8,128)(2,1)S(1)}, bf16[8,5,32,128]{3,2,1,0:T(8,128)(2,1)S(1)}, u32[]{:S(2)}, u32[]{:S(2)}) %collective-permute-start.5) | collective-permute-done | bytes 327712 | tf_op jit(solution)/shard_map/ppermute | solution.py:368
  29.4 0.0 copy-start.1
  29.4 0.0 copy-start.3
  29.4 0.1 convert_add_fusion
  29.6 1.6 %collective-permute-start.7 = (bf16[4,5,32,128]{3,2,1,0:T(8,128)(2,1)S(1)}, bf16[4,5,32,128]{3,2,1,0:T(8,128)(2,1)S(1)}, u32[]{:S(2)}, u32[]{:S(2)}) collective-permute-start(bf16[4,5,32,128]{3,2,1,0:T(8,128)(2,1)S(1)} %slice.43), channel_id=1, source_target_pairs={{0,4},{4,0},{8,12},{12,8},{16,20},{20,16},{24,28},{28,24},{1,5},{5... | collective-permute-start | bytes 491528 | tf_op jit(solution)/shard_map/ppermute | solution.py:374
  31.1 1.4 %collective-permute-start.15 = (bf16[3,128,1024]{2,1,0:T(8,128)(2,1)S(1)}, bf16[3,128,1024]{2,1,0:T(8,128)(2,1)S(1)}, u32[]{:S(2)}, u32[]{:S(2)}) collective-permute-start(bf16[3,128,1024]{2,1,0:T(8,128)(2,1)S(1)} %get-tuple-element.72), channel_id=1, source_target_pairs={{2,0},{3,1},{0,2},{1,3},{6,4},{7,5},{4,6},{5,7},{10,8},{11,9},{8,1... | collective-permute-start | bytes 2359304 | tf_op jit(solution)/shard_map/ppermute | solution.py:368
  32.5 2.9 %collective-permute-done.7 = bf16[4,5,32,128]{3,2,1,0:T(8,128)(2,1)S(1)} collective-permute-done((bf16[4,5,32,128]{3,2,1,0:T(8,128)(2,1)S(1)}, bf16[4,5,32,128]{3,2,1,0:T(8,128)(2,1)S(1)}, u32[]{:S(2)}, u32[]{:S(2)}) %collective-permute-start.7) | collective-permute-done | bytes 163872 | tf_op jit(solution)/shard_map/ppermute | solution.py:374
  35.4 0.1 fusion.4
  35.5 1.6 %collective-permute-start.8 = (bf16[5,32,128]{2,1,0:T(8,128)(2,1)S(1)}, bf16[5,32,128]{2,1,0:T(8,128)(2,1)S(1)}, u32[]{:S(2)}, u32[]{:S(2)}) collective-permute-start(bf16[5,32,128]{2,1,0:T(8,128)(2,1)S(1)} %get-tuple-element.95), channel_id=1, source_target_pairs={{0,8},{4,12},{8,0},{12,4},{16,24},{20,28},{24,16},{28,20},{1,9},{5... | collective-permute-start | bytes 122888 | tf_op jit(solution)/shard_map/ppermute | solution.py:374
  37.1 2.5 %collective-permute-start.10 = (bf16[5,32,128]{2,1,0:T(8,128)(2,1)S(1)}, bf16[5,32,128]{2,1,0:T(8,128)(2,1)S(1)}, u32[]{:S(2)}, u32[]{:S(2)}) collective-permute-start(bf16[5,32,128]{2,1,0:T(8,128)(2,1)S(1)} %get-tuple-element.96), channel_id=1, source_target_pairs={{0,24},{4,28},{8,16},{12,20},{16,8},{20,12},{24,0},{28,4},{1,25},{... | collective-permute-start | bytes 122888 | tf_op jit(solution)/shard_map/ppermute | solution.py:374
  39.6 0.1 collective-permute-start.9
  39.7 0.0 copy-done.6
  39.7 0.1 broadcast_multiply_fusion
  39.8 0.0 copy-done.7
  39.8 0.0 collective-permute-done.8
  39.8 3.1 %collective-permute-done.10 = bf16[5,32,128]{2,1,0:T(8,128)(2,1)S(1)} collective-permute-done((bf16[5,32,128]{2,1,0:T(8,128)(2,1)S(1)}, bf16[5,32,128]{2,1,0:T(8,128)(2,1)S(1)}, u32[]{:S(2)}, u32[]{:S(2)}) %collective-permute-start.10) | collective-permute-done | bytes 40992 | tf_op jit(solution)/shard_map/ppermute | solution.py:374
  42.9 2.0 %collective-permute-done.9 = bf16[5,32,128]{2,1,0:T(8,128)(2,1)S(1)} collective-permute-done((bf16[5,32,128]{2,1,0:T(8,128)(2,1)S(1)}, bf16[5,32,128]{2,1,0:T(8,128)(2,1)S(1)}, u32[]{:S(2)}, u32[]{:S(2)}) %collective-permute-start.9) | collective-permute-done | bytes 40992 | tf_op jit(solution)/shard_map/ppermute | solution.py:374
  45.0 1.6 %collective-permute-start.11 = (bf16[1,5,32,128]{3,2,1,0:T(8,128)(2,1)S(1)}, bf16[1,5,32,128]{3,2,1,0:T(8,128)(2,1)S(1)}, u32[]{:S(2)}, u32[]{:S(2)}) collective-permute-start(bf16[1,5,32,128]{3,2,1,0:T(8,128)(2,1)S(1)} %get-tuple-element.68), channel_id=1, source_target_pairs={{4,0},{0,4},{12,8},{8,12},{20,16},{16,20},{28,24},{24,28},{5,1},{1... | collective-permute-start | bytes 122888 | tf_op jit(solution)/shard_map/ppermute | solution.py:377
  46.5 2.5 %collective-permute-done.11 = bf16[1,5,32,128]{3,2,1,0:T(8,128)(2,1)S(1)} collective-permute-done((bf16[1,5,32,128]{3,2,1,0:T(8,128)(2,1)S(1)}, bf16[1,5,32,128]{3,2,1,0:T(8,128)(2,1)S(1)}, u32[]{:S(2)}, u32[]{:S(2)}) %collective-permute-start.11) | collective-permute-done | bytes 40992 | tf_op jit(solution)/shard_map/ppermute | solution.py:377
  49.0 1.4 %collective-permute-start.14 = (bf16[2,5,32,128]{3,2,1,0:T(8,128)(2,1)S(1)}, bf16[2,5,32,128]{3,2,1,0:T(8,128)(2,1)S(1)}, u32[]{:S(2)}, u32[]{:S(2)}) collective-permute-start(bf16[2,5,32,128]{3,2,1,0:T(8,128)(2,1)S(1)} %constant_dynamic-update-slice_fusion.refs_0_), channel_id=1, source_target_pairs={{24,0},{28,4},{16,8},{20,12},{8,16},{12,20},{0,24},{4,28},{25,1},{... | collective-permute-start | bytes 245768 | tf_op jit(solution)/shard_map/ppermute | solution.py:377
  50.4 0.5 collective-permute-start.13
  50.9 2.6 %collective-permute-start.12 = (bf16[2,5,32,128]{3,2,1,0:T(8,128)(2,1)S(1)}, bf16[2,5,32,128]{3,2,1,0:T(8,128)(2,1)S(1)}, u32[]{:S(2)}, u32[]{:S(2)}) collective-permute-start(bf16[2,5,32,128]{3,2,1,0:T(8,128)(2,1)S(1)} %constant_dynamic-update-slice_fusion.refs_0_), channel_id=1, source_target_pairs={{8,0},{12,4},{0,8},{4,12},{24,16},{28,20},{16,24},{20,28},{9,1},{1... | collective-permute-start | bytes 245768 | tf_op jit(solution)/shard_map/ppermute | solution.py:377
  53.5 0.6 multiply_add_fusion
  54.1 0.0 collective-permute-done.15.refs_3_
  54.1 0.0 copy-done.1
  54.1 0.0 copy-done.3
  54.1 3.6 %hidden_grad.1 = bf16[128,8192]{1,0:T(8,128)(2,1)} custom-call(bf16[128,8192]{1,0:T(8,128)(2,1)S(1)} %copy-done.1, f32[1,8192]{1,0:T(1,128)S(1)} %bitcast.23, bf16[1,128,1024]{2,1,0:T(8,128)(2,1)S(1)} %get-tuple-element.69.refs_0_, bf16[1,128,1024]{2,1,0:T(8,128)(2,1)S(1)} %collective-permute-done.4.refs_1_, ...), custom_call_target="tpu_custom_call" | custom-call | flops 1 | bytes 1 | tf_op jit(solution)/shard_map/hidden_grad/pallas_call | solution.py:261
  57.7 0.0 collective-permute-done.14.refs_3_
  57.7 0.0 collective-permute-done.13.refs_2_
  57.7 0.0 collective-permute-done.12.refs_1_
  57.7 7.6 %unsketch.1 = (f32[2048,512]{1,0:T(8,128)}, f32[5,32,128]{2,1,0:T(8,128)}) custom-call(bf16[2,5,32,128]{3,2,1,0:T(8,128)(2,1)S(1)} %constant_dynamic-update-slice_fusion.refs_0_, bf16[2,5,32,128]{3,2,1,0:T(8,128)(2,1)S(1)} %collective-permute-done.12.refs_1_, bf16[2,5,32,128]{3,2,1,0:T(8,128)(2,1)S(1)} %collective-permute-done.13.refs_2_, ...), custom_call_target="tpu_custom_call" | custom-call | flops 1 | bytes 1 | tf_op jit(solution)/shard_map/unsketch/pallas_call | solution.py:324
  (6 shorter events, 0.1 us)
Async XLA Ops:
  0.6 7.1 %copy-start.2 = (bf16[128,512]{1,0:T(8,128)(2,1)S(1)}, bf16[128,512]{1,0:T(8,128)(2,1)}, u32[]{:S(2)}) copy-start(bf16[128,512]{1,0:T(8,128)(2,1)} %refs_0_.1) | copy-start | bytes 393220
  0.6 9.0 %copy-start = (bf16[2048,512]{1,0:T(8,128)(2,1)S(1)}, bf16[2048,512]{1,0:T(8,128)(2,1)}, u32[]{:S(2)}) copy-start(bf16[2048,512]{1,0:T(8,128)(2,1)} %refs_2_.7) | copy-start | bytes 6291460
  0.7 7.0 %collective-permute-start = (bf16[128,512]{1,0:T(8,128)(2,1)}, bf16[128,512]{1,0:T(8,128)(2,1)S(1)}, u32[]{:S(2)}, u32[]{:S(2)}) collective-permute-start(bf16[128,512]{1,0:T(8,128)(2,1)} %refs_0_.1), channel_id=1, source_target_pairs={{2,0},{3,1},{0,2},{1,3},{6,4},{7,5},{4,6},{5,7},{10,8},{11,9},{8,1... | collective-permute-start | bytes 393224 | tf_op jit(solution)/shard_map/ppermute | solution.py:368
  7.6 5.2 %copy-start.5 = (bf16[2,128,2048]{2,1,0:T(8,128)(2,1)S(1)}, bf16[2,128,2048]{2,1,0:T(8,128)(2,1)}, u32[]{:S(2)}) copy-start(bf16[2,128,2048]{2,1,0:T(8,128)(2,1)} %get-tuple-element.53.refs_0_) | copy-start | bytes 3145732
  7.7 3.1 %collective-permute-start.1 = (bf16[2,128,2048]{2,1,0:T(8,128)(2,1)}, bf16[2,128,2048]{2,1,0:T(8,128)(2,1)S(1)}, u32[]{:S(2)}, u32[]{:S(2)}) collective-permute-start(bf16[2,128,2048]{2,1,0:T(8,128)(2,1)} %get-tuple-element.48), channel_id=1, source_target_pairs={{0,1},{1,0},{2,3},{3,2},{4,5},{5,4},{6,7},{7,6},{8,9},{9,8},{10,11... | collective-permute-start | bytes 3145736 | tf_op jit(solution)/shard_map/ppermute | solution.py:362
  7.7 5.1 %collective-permute-start.2 = (bf16[128,512]{1,0:T(8,128)(2,1)S(1)}, bf16[128,512]{1,0:T(8,128)(2,1)S(1)}, u32[]{:S(2)}, u32[]{:S(2)}) collective-permute-start(bf16[128,512]{1,0:T(8,128)(2,1)S(1)} %copy-done.2), channel_id=1, source_target_pairs={{0,1},{1,0},{2,3},{3,2},{4,5},{5,4},{6,7},{7,6},{8,9},{9,8},{10,11... | collective-permute-start | bytes 393224 | tf_op jit(solution)/shard_map/ppermute | solution.py:362
  8.2 4.7 %collective-permute-start.3 = (bf16[40,1024]{1,0:T(8,128)(2,1)}, bf16[40,1024]{1,0:T(8,128)(2,1)S(1)}, u32[]{:S(2)}, u32[]{:S(2)}) collective-permute-start(bf16[40,1024]{1,0:T(8,128)(2,1)} %get-tuple-element.58), channel_id=1, source_target_pairs={{2,0},{3,1},{0,2},{1,3},{6,4},{7,5},{4,6},{5,7},{10,8},{11,9},{8,1... | collective-permute-start | bytes 245768 | tf_op jit(solution)/shard_map/ppermute | solution.py:368
  10.8 10.0 %copy-start.4 = (bf16[4,8,2048]{2,1,0:T(8,128)(2,1)S(1)}, bf16[4,8,2048]{2,1,0:T(8,128)(2,1)}, u32[]{:S(2)}) copy-start(bf16[4,8,2048]{2,1,0:T(8,128)(2,1)} %get-tuple-element.56.refs_4_) | copy-start | bytes 393220
  10.8 8.4 %collective-permute-start.4 = (bf16[1,128,1024]{2,1,0:T(8,128)(2,1)S(1)}, bf16[1,128,1024]{2,1,0:T(8,128)(2,1)S(1)}, u32[]{:S(2)}, u32[]{:S(2)}) collective-permute-start(bf16[1,128,1024]{2,1,0:T(8,128)(2,1)S(1)} %get-tuple-element.60), channel_id=1, source_target_pairs={{2,0},{3,1},{0,2},{1,3},{6,4},{7,5},{4,6},{5,7},{10,8},{11,9},{8,1... | collective-permute-start | bytes 786440 | tf_op jit(solution)/shard_map/ppermute | solution.py:368
  19.2 7.9 %collective-permute-start.6 = (bf16[2048,512]{1,0:T(8,128)(2,1)S(1)}, bf16[2048,512]{1,0:T(8,128)(2,1)S(1)}, u32[]{:S(2)}, u32[]{:S(2)}) collective-permute-start(bf16[2048,512]{1,0:T(8,128)(2,1)S(1)} %copy-done), channel_id=1, source_target_pairs={{0,1},{1,0},{2,3},{3,2},{4,5},{5,4},{6,7},{7,6},{8,9},{9,8},{10,11... | collective-permute-start | bytes 6291464 | tf_op jit(solution)/shard_map/ppermute | solution.py:362
  19.3 10.1 %collective-permute-start.5 = (bf16[8,5,32,128]{3,2,1,0:T(8,128)(2,1)S(1)}, bf16[8,5,32,128]{3,2,1,0:T(8,128)(2,1)S(1)}, u32[]{:S(2)}, u32[]{:S(2)}) collective-permute-start(bf16[8,5,32,128]{3,2,1,0:T(8,128)(2,1)S(1)} %sketch.3), channel_id=1, source_target_pairs={{2,0},{3,1},{0,2},{1,3},{6,4},{7,5},{4,6},{5,7},{10,8},{11,9},{8,1... | collective-permute-start | bytes 983048 | tf_op jit(solution)/shard_map/ppermute | solution.py:368
  28.3 11.4 %copy-start.6 = (f32[1,5,4096]{2,0,1:T(1,128)S(1)}, f32[1,5,4096]{2,0,1:T(1,128)}, u32[]{:S(2)}) copy-start(f32[1,5,4096]{2,0,1:T(1,128)} %param.14) | copy-start | bytes 245764
  28.3 11.5 %copy-start.7 = (f32[1,5,4096]{2,0,1:T(1,128)S(1)}, f32[1,5,4096]{2,0,1:T(1,128)}, u32[]{:S(2)}) copy-start(f32[1,5,4096]{2,0,1:T(1,128)} %param.15) | copy-start | bytes 245764
  29.4 24.7 %copy-start.1 = (bf16[128,8192]{1,0:T(8,128)(2,1)S(1)}, bf16[128,8192]{1,0:T(8,128)(2,1)}, u32[]{:S(2)}) copy-start(bf16[128,8192]{1,0:T(8,128)(2,1)} %hidden_ref.3) | copy-start | bytes 6291460
  29.4 24.7 %copy-start.3 = (f32[8192]{0:T(1024)S(1)}, f32[8192]{0:T(1024)}, u32[]{:S(2)}) copy-start(f32[8192]{0:T(1024)} %param.9) | copy-start | bytes 98308
  29.6 5.8 %collective-permute-start.7 = (bf16[4,5,32,128]{3,2,1,0:T(8,128)(2,1)S(1)}, bf16[4,5,32,128]{3,2,1,0:T(8,128)(2,1)S(1)}, u32[]{:S(2)}, u32[]{:S(2)}) collective-permute-start(bf16[4,5,32,128]{3,2,1,0:T(8,128)(2,1)S(1)} %slice.43), channel_id=1, source_target_pairs={{0,4},{4,0},{8,12},{12,8},{16,20},{20,16},{24,28},{28,24},{1,5},{5... | collective-permute-start | bytes 491528 | tf_op jit(solution)/shard_map/ppermute | solution.py:374
  31.1 23.0 %collective-permute-start.15 = (bf16[3,128,1024]{2,1,0:T(8,128)(2,1)S(1)}, bf16[3,128,1024]{2,1,0:T(8,128)(2,1)S(1)}, u32[]{:S(2)}, u32[]{:S(2)}) collective-permute-start(bf16[3,128,1024]{2,1,0:T(8,128)(2,1)S(1)} %get-tuple-element.72), channel_id=1, source_target_pairs={{2,0},{3,1},{0,2},{1,3},{6,4},{7,5},{4,6},{5,7},{10,8},{11,9},{8,1... | collective-permute-start | bytes 2359304 | tf_op jit(solution)/shard_map/ppermute | solution.py:368
  35.5 4.4 %collective-permute-start.8 = (bf16[5,32,128]{2,1,0:T(8,128)(2,1)S(1)}, bf16[5,32,128]{2,1,0:T(8,128)(2,1)S(1)}, u32[]{:S(2)}, u32[]{:S(2)}) collective-permute-start(bf16[5,32,128]{2,1,0:T(8,128)(2,1)S(1)} %get-tuple-element.95), channel_id=1, source_target_pairs={{0,8},{4,12},{8,0},{12,4},{16,24},{20,28},{24,16},{28,20},{1,9},{5... | collective-permute-start | bytes 122888 | tf_op jit(solution)/shard_map/ppermute | solution.py:374
  37.1 5.8 %collective-permute-start.10 = (bf16[5,32,128]{2,1,0:T(8,128)(2,1)S(1)}, bf16[5,32,128]{2,1,0:T(8,128)(2,1)S(1)}, u32[]{:S(2)}, u32[]{:S(2)}) collective-permute-start(bf16[5,32,128]{2,1,0:T(8,128)(2,1)S(1)} %get-tuple-element.96), channel_id=1, source_target_pairs={{0,24},{4,28},{8,16},{12,20},{16,8},{20,12},{24,0},{28,4},{1,25},{... | collective-permute-start | bytes 122888 | tf_op jit(solution)/shard_map/ppermute | solution.py:374
  39.6 5.3 %collective-permute-start.9 = (bf16[5,32,128]{2,1,0:T(8,128)(2,1)S(1)}, bf16[5,32,128]{2,1,0:T(8,128)(2,1)S(1)}, u32[]{:S(2)}, u32[]{:S(2)}) collective-permute-start(bf16[5,32,128]{2,1,0:T(8,128)(2,1)S(1)} %get-tuple-element.97), channel_id=1, source_target_pairs={{0,16},{4,20},{8,24},{12,28},{16,0},{20,4},{24,8},{28,12},{1,17},{... | collective-permute-start | bytes 122888 | tf_op jit(solution)/shard_map/ppermute | solution.py:374
  45.0 4.1 %collective-permute-start.11 = (bf16[1,5,32,128]{3,2,1,0:T(8,128)(2,1)S(1)}, bf16[1,5,32,128]{3,2,1,0:T(8,128)(2,1)S(1)}, u32[]{:S(2)}, u32[]{:S(2)}) collective-permute-start(bf16[1,5,32,128]{3,2,1,0:T(8,128)(2,1)S(1)} %get-tuple-element.68), channel_id=1, source_target_pairs={{4,0},{0,4},{12,8},{8,12},{20,16},{16,20},{28,24},{24,28},{5,1},{1... | collective-permute-start | bytes 122888 | tf_op jit(solution)/shard_map/ppermute | solution.py:377
  49.0 8.7 %collective-permute-start.14 = (bf16[2,5,32,128]{3,2,1,0:T(8,128)(2,1)S(1)}, bf16[2,5,32,128]{3,2,1,0:T(8,128)(2,1)S(1)}, u32[]{:S(2)}, u32[]{:S(2)}) collective-permute-start(bf16[2,5,32,128]{3,2,1,0:T(8,128)(2,1)S(1)} %constant_dynamic-update-slice_fusion.refs_0_), channel_id=1, source_target_pairs={{24,0},{28,4},{16,8},{20,12},{8,16},{12,20},{0,24},{4,28},{25,1},{... | collective-permute-start | bytes 245768 | tf_op jit(solution)/shard_map/ppermute | solution.py:377
  50.4 7.3 %collective-permute-start.13 = (bf16[2,5,32,128]{3,2,1,0:T(8,128)(2,1)S(1)}, bf16[2,5,32,128]{3,2,1,0:T(8,128)(2,1)S(1)}, u32[]{:S(2)}, u32[]{:S(2)}) collective-permute-start(bf16[2,5,32,128]{3,2,1,0:T(8,128)(2,1)S(1)} %constant_dynamic-update-slice_fusion.refs_0_), channel_id=1, source_target_pairs={{16,0},{20,4},{24,8},{28,12},{0,16},{4,20},{8,24},{12,28},{17,1},{... | collective-permute-start | bytes 245768 | tf_op jit(solution)/shard_map/ppermute | solution.py:377
  50.9 6.8 %collective-permute-start.12 = (bf16[2,5,32,128]{3,2,1,0:T(8,128)(2,1)S(1)}, bf16[2,5,32,128]{3,2,1,0:T(8,128)(2,1)S(1)}, u32[]{:S(2)}, u32[]{:S(2)}) collective-permute-start(bf16[2,5,32,128]{3,2,1,0:T(8,128)(2,1)S(1)} %constant_dynamic-update-slice_fusion.refs_0_), channel_id=1, source_target_pairs={{8,0},{12,4},{0,8},{4,12},{24,16},{28,20},{16,24},{20,28},{9,1},{1... | collective-permute-start | bytes 245768 | tf_op jit(solution)/shard_map/ppermute | solution.py:377

commit v4 on v3

--- a/solution.py
+++ b/solution.py
@@ -82,14 +82,21 @@
     fsdp_at = lax.axis_index("fsdp")
     core, place = lax.rem(fsdp_at, pair), fsdp_at // pair
     features = out_refs[0].shape[2]
-    values = hidden_ref[...].astype(jnp.float32)
-    inverse_rms = lax.rsqrt(jnp.mean(values * values, axis=1, keepdims=True) + EPS)
+    tile, width = hidden_ref.shape
+    squares = jnp.zeros((tile, BLOCK), jnp.float32)
+    for part in range(0, width, BLOCK):
+        values = hidden_ref[:, part : part + BLOCK].astype(jnp.float32)
+        squares += values * values
+    inverse_rms = lax.rsqrt(jnp.sum(squares, axis=1, keepdims=True) / width + EPS)
     for other in range(pair):
         for step in range(turns):
             slab = lax.rem(place + step, turns) * pair + (core ^ other)
-            span = pl.ds(pl.multiple_of(slab * features, BLOCK), features)
-            normed = hidden_ref[:, span].astype(jnp.float32) * inverse_rms
-            out_refs[other][step] = (normed * gain_ref[:, span]).astype(jnp.bfloat16)
+            for part in range(0, features, 2 * BLOCK):
+                span = pl.ds(pl.multiple_of(slab * features + part, BLOCK), 2 * BLOCK)
+                normed = hidden_ref[:, span].astype(jnp.float32) * inverse_rms
+                out_refs[other][step, :, part : part + 2 * BLOCK] = (
+                    normed * gain_ref[:, span]
+                ).astype(jnp.bfloat16)
 
 
 def front(bucket, sign_bits, hidden, gain, quads, wrap, pair, turns, tile=64):
@@ -133,7 +140,7 @@
     contract = (((0,), (0,)), ((), ()))
     inputs = jnp.concatenate([ref[0] for ref in inputs_refs], axis=0)
     cots = jnp.concatenate([ref[...] for ref in cot_refs], axis=0)
-    grad = lax.dot_general(inputs, cots, contract, preferred_element_type=jnp.float32) * scale
+    grad = lax.dot_general(inputs, cots, contract, preferred_element_type=jnp.float32)
     upper = grad.astype(jnp.bfloat16)
     lower = (grad - upper.astype(jnp.float32)).astype(jnp.bfloat16)
     both = jnp.concatenate(
@@ -162,7 +169,7 @@
                 picks.append(picked(code, numbers))
         pick = jnp.concatenate(picks, axis=1)
         sums = jnp.dot(pick, both, preferred_element_type=jnp.float32)
-        table = sums[:, :BLOCK] + sums[:, BLOCK:]
+        table = (sums[:, :BLOCK] + sums[:, BLOCK:]) * scale
         for part in range(count):
             table_ref[part % near * (count // near) + part // near, row] = table[part * share : (part + 1) * share, :].astype(
                 table_ref.dtype
@@ -420,7 +427,7 @@
         table = table[:halves_at] + arrived.astype(jnp.float32)
     sent = table.astype(jnp.bfloat16)
     total = table[0]
-    for step in range(near, dp_count, near):
+    for step in range(dp_count - near, 0, -near):
         total = total + to_share(sent[step // near], step).astype(jnp.float32)
     error_mid = carried + total / dp_count
     error_sent = error_mid.astype(jnp.bfloat16)[None]

time: 65.5 us -> 64.7 us (0.988)
  waiting for transfers between devices: 12.9 us -> 11.1 us
  starting transfers between devices: 21.2 us -> 22.6 us
    ppermute x4, waiting for transfers between devices: 7.95 us -> 6.7 us  [to_share(): lax.ppermute(value, 'dp', [(i, partner(i, step, dp_count)) for i in range...]
    ppermute x5, starting transfers between devices: 8.76 us -> 9.75 us  [from_turn(): return lax.ppermute(value, 'fsdp', pairs)]
  transfers between devices with their start and end apart: 16 -> 16, of which waited for: 7 -> 9; matrix products, arithmetic and copies ran while one was open for 1% -> 1% of each run, Pallas kernels for 33% -> 33%
where the time goes in v4:
time: 64.7 us; the launch traced here: 64.5 us
  Pallas kernels  29.1 us (45%)
  starting transfers between devices  22.6 us (35%)
  waiting for transfers between devices  11.1 us (17%)
  other arithmetic  0.92 us (1%)
  between operations  0.8 us (1%)
    pallas_call x2, Pallas kernels, sketch(): pl.pallas_call(functools.partial(sketch_kernel, scale, count, near, pair,...  12.7 us
    ppermute x5, starting transfers between devices, from_turn(): return lax.ppermute(value, 'fsdp', pairs)  9.75 us
    pallas_call x1, Pallas kernels, unsketch(): pl.pallas_call(functools.partial(unsketch_kernel, groups, share), out_sha...  7.61 us
    ppermute x4, waiting for transfers between devices, to_share(): lax.ppermute(value, 'dp', [(i, partner(i, step, dp_count)) for i in range...  6.7 us
    ppermute x4, starting transfers between devices, to_share(): lax.ppermute(value, 'dp', [(i, partner(i, step, dp_count)) for i in range...  6.25 us
    ppermute x4, starting transfers between devices, from_share(): lax.ppermute(value, 'dp', [(partner(i, step, dp_count), i) for i in range...  6 us
    pallas_call x1, Pallas kernels, front(): pl.pallas_call(functools.partial(front_kernel, wrap, pair, turns), out_sh...  3.66 us
    pallas_call x1, Pallas kernels, backward(): pl.pallas_call(functools.partial(backward_kernel, turns, pair, pieces), o...  3.56 us
  transfers between devices with their start and end apart: 16, of which 9 were waited for; matrix products, arithmetic and copies ran while one was open for 1% of the time, Pallas kernels for 33%

profile of v4, /device:TPU:0, one launch (start us, length us, event | category | flops | bytes accessed | tf_op | source)
XLA Modules:
  0.0 64.5 jit_solution(8483107373277474781)
XLA Ops:
  0.6 0.0 copy-start.2
  0.6 0.0 copy-start
  0.7 3.0 %collective-permute-start = (bf16[128,512]{1,0:T(8,128)(2,1)}, bf16[128,512]{1,0:T(8,128)(2,1)S(1)}, u32[]{:S(2)}, u32[]{:S(2)}) collective-permute-start(bf16[128,512]{1,0:T(8,128)(2,1)} %refs_0_.1), channel_id=1, source_target_pairs={{2,0},{3,1},{0,2},{1,3},{6,4},{7,5},{4,6},{5,7},{10,8},{11,9},{8,1... | collective-permute-start | bytes 393224 | tf_op jit(solution)/shard_map/ppermute | solution.py:375
  3.7 3.7 %codes_and_normed.1 = (bf16[4,8,2048]{2,1,0:T(8,128)(2,1)}, bf16[40,1024]{1,0:T(8,128)(2,1)}, bf16[2,128,2048]{2,1,0:T(8,128)(2,1)}, bf16[2,128,2048]{2,1,0:T(8,128)(2,1)}) custom-call(s32[5,8192]{1,0:T(8,128)} %bucket_ref.1, s32[5,8192]{1,0:T(8,128)} %sign_ref.1, bf16[128,8192]{1,0:T(8,128)(2,1)} %hidden_ref.3, f32[1,8192]{1,0:T(1,128)} %bitcast.22), custom_call_target="tpu_custom_call" | custom-call | flops 1 | bytes 1 | tf_op jit(solution)/shard_map/codes_and_normed/pallas_call | solution.py:108
  7.3 0.0 copy-start.5
  7.3 0.0 collective-permute-done.refs_1_
  7.4 0.0 collective-permute-start.1
  7.4 0.0 copy-done.2
  7.4 0.5 collective-permute-start.2
  7.9 1.7 %collective-permute-start.3 = (bf16[40,1024]{1,0:T(8,128)(2,1)}, bf16[40,1024]{1,0:T(8,128)(2,1)S(1)}, u32[]{:S(2)}, u32[]{:S(2)}) collective-permute-start(bf16[40,1024]{1,0:T(8,128)(2,1)} %get-tuple-element.58), channel_id=1, source_target_pairs={{2,0},{3,1},{0,2},{1,3},{6,4},{7,5},{4,6},{5,7},{10,8},{11,9},{8,1... | collective-permute-start | bytes 245768 | tf_op jit(solution)/shard_map/ppermute | solution.py:375
  9.6 0.0 copy-done
  9.6 0.5 input_grad.2
  10.1 0.4 collective-permute-done.1.refs_1_
  10.5 0.0 copy-start.4
  10.5 1.7 %collective-permute-start.4 = (bf16[1,128,1024]{2,1,0:T(8,128)(2,1)S(1)}, bf16[1,128,1024]{2,1,0:T(8,128)(2,1)S(1)}, u32[]{:S(2)}, u32[]{:S(2)}) collective-permute-start(bf16[1,128,1024]{2,1,0:T(8,128)(2,1)S(1)} %get-tuple-element.60), channel_id=1, source_target_pairs={{2,0},{3,1},{0,2},{1,3},{6,4},{7,5},{4,6},{5,7},{10,8},{11,9},{8,1... | collective-permute-start | bytes 786440 | tf_op jit(solution)/shard_map/ppermute | solution.py:375
  12.2 0.4 collective-permute-done.3.refs_4_
  12.6 0.0 collective-permute-done.2.refs_3_
  12.6 0.0 copy-done.5
  12.6 6.3 %sketch.3 = bf16[8,5,32,128]{3,2,1,0:T(8,128)(2,1)S(1)} custom-call(bf16[2,128,2048]{2,1,0:T(8,128)(2,1)S(1)} %copy-done.5, bf16[2,128,2048]{2,1,0:T(8,128)(2,1)S(1)} %collective-permute-done.1.refs_1_, bf16[128,512]{1,0:T(8,128)(2,1)S(1)} %copy-done.2, bf16[128,512]{1,0:T(8,128)(2,1)S(1)} %collective-permute-done.2.refs_3_, ...), custom_call_target="tpu_custom_call" | custom-call | flops 5368709120 | bytes 2097152 | tf_op jit(solution)/shard_map/sketch/pallas_call | solution.py:184
  18.9 0.0 collective-permute-done.4.refs_1_
  18.9 0.1 collective-permute-start.6
  19.0 1.8 %collective-permute-start.5 = (bf16[8,5,32,128]{3,2,1,0:T(8,128)(2,1)S(1)}, bf16[8,5,32,128]{3,2,1,0:T(8,128)(2,1)S(1)}, u32[]{:S(2)}, u32[]{:S(2)}) collective-permute-start(bf16[8,5,32,128]{3,2,1,0:T(8,128)(2,1)S(1)} %sketch.3), channel_id=1, source_target_pairs={{2,0},{3,1},{0,2},{1,3},{6,4},{7,5},{4,6},{5,7},{10,8},{11,9},{8,1... | collective-permute-start | bytes 983048 | tf_op jit(solution)/shard_map/ppermute | solution.py:375
  20.8 0.0 copy-done.4
  20.8 6.4 %sketch.2 = bf16[8,5,32,128]{3,2,1,0:T(8,128)(2,1)S(1)} custom-call(bf16[2,128,2048]{2,1,0:T(8,128)(2,1)S(1)} %copy-done.5, bf16[2,128,2048]{2,1,0:T(8,128)(2,1)S(1)} %collective-permute-done.1.refs_1_, bf16[128,512]{1,0:T(8,128)(2,1)S(1)} %copy-done.2, bf16[128,512]{1,0:T(8,128)(2,1)S(1)} %collective-permute-done.2.refs_3_, bf16[4,8,2048]{2,1,0:T(8,128)(2,1)S(1)} %copy-done.4), custom_call_target="tpu_custom_call" | custom-call | flops 5368709120 | bytes 2097152 | tf_op jit(solution)/shard_map/sketch/pallas_call | solution.py:184
  27.2 0.0 collective-permute-done.6.refs_3_.refs_4_
  27.2 1.0 %input_grad.3 = (bf16[3,128,1024]{2,1,0:T(8,128)(2,1)S(1)}, bf16[3,128,1024]{2,1,0:T(8,128)(2,1)S(1)}) custom-call(bf16[128,512]{1,0:T(8,128)(2,1)S(1)} %copy-done.2, bf16[128,512]{1,0:T(8,128)(2,1)S(1)} %collective-permute-done.refs_1_, bf16[2048,512]{1,0:T(8,128)(2,1)S(1)} %copy-done, bf16[2048,512]{1,0:T(8,128)(2,1)S(1)} %collective-permute-done.6.refs_3_.refs_4_, ...), custom_call_target="tpu_custom_call" | custom-call | flops 1 | bytes 1 | tf_op jit(solution)/shard_map/input_grad/pallas_call | solution.py:219
  28.2 0.0 copy-start.6
  28.2 0.0 copy-start.7
  28.3 0.9 %collective-permute-done.5 = bf16[8,5,32,128]{3,2,1,0:T(8,128)(2,1)S(1)} collective-permute-done((bf16[8,5,32,128]{3,2,1,0:T(8,128)(2,1)S(1)}, bf16[8,5,32,128]{3,2,1,0:T(8,128)(2,1)S(1)}, u32[]{:S(2)}, u32[]{:S(2)}) %collective-permute-start.5) | collective-permute-done | bytes 327712 | tf_op jit(solution)/shard_map/ppermute | solution.py:375
  29.1 0.0 copy-start.1
  29.1 0.0 copy-start.3
  29.1 0.1 convert_add_fusion
  29.3 1.7 %collective-permute-start.7 = (bf16[4,5,32,128]{3,2,1,0:T(8,128)(2,1)S(1)}, bf16[4,5,32,128]{3,2,1,0:T(8,128)(2,1)S(1)}, u32[]{:S(2)}, u32[]{:S(2)}) collective-permute-start(bf16[4,5,32,128]{3,2,1,0:T(8,128)(2,1)S(1)} %slice.43), channel_id=1, source_target_pairs={{0,4},{4,0},{8,12},{12,8},{16,20},{20,16},{24,28},{28,24},{1,5},{5... | collective-permute-start | bytes 491528 | tf_op jit(solution)/shard_map/ppermute | solution.py:381
  31.0 1.5 %collective-permute-start.15 = (bf16[3,128,1024]{2,1,0:T(8,128)(2,1)S(1)}, bf16[3,128,1024]{2,1,0:T(8,128)(2,1)S(1)}, u32[]{:S(2)}, u32[]{:S(2)}) collective-permute-start(bf16[3,128,1024]{2,1,0:T(8,128)(2,1)S(1)} %get-tuple-element.72), channel_id=1, source_target_pairs={{2,0},{3,1},{0,2},{1,3},{6,4},{7,5},{4,6},{5,7},{10,8},{11,9},{8,1... | collective-permute-start | bytes 2359304 | tf_op jit(solution)/shard_map/ppermute | solution.py:375
  32.5 2.6 %collective-permute-done.7 = bf16[4,5,32,128]{3,2,1,0:T(8,128)(2,1)S(1)} collective-permute-done((bf16[4,5,32,128]{3,2,1,0:T(8,128)(2,1)S(1)}, bf16[4,5,32,128]{3,2,1,0:T(8,128)(2,1)S(1)}, u32[]{:S(2)}, u32[]{:S(2)}) %collective-permute-start.7) | collective-permute-done | bytes 163872 | tf_op jit(solution)/shard_map/ppermute | solution.py:381
  35.1 0.1 fusion.4
  35.2 3.9 %collective-permute-start.8 = (bf16[5,32,128]{2,1,0:T(8,128)(2,1)S(1)}, bf16[5,32,128]{2,1,0:T(8,128)(2,1)S(1)}, u32[]{:S(2)}, u32[]{:S(2)}) collective-permute-start(bf16[5,32,128]{2,1,0:T(8,128)(2,1)S(1)} %get-tuple-element.95), channel_id=1, source_target_pairs={{0,24},{4,28},{8,16},{12,20},{16,8},{20,12},{24,0},{28,4},{1,25},{... | collective-permute-start | bytes 122888 | tf_op jit(solution)/shard_map/ppermute | solution.py:381
  39.0 0.0 collective-permute-start.10
  39.0 0.6 collective-permute-start.9
  39.7 0.0 copy-done.6
  39.7 0.1 broadcast_multiply_fusion
  39.8 0.0 copy-done.7
  39.8 1.2 %collective-permute-done.8 = bf16[5,32,128]{2,1,0:T(8,128)(2,1)S(1)} collective-permute-done((bf16[5,32,128]{2,1,0:T(8,128)(2,1)S(1)}, bf16[5,32,128]{2,1,0:T(8,128)(2,1)S(1)}, u32[]{:S(2)}, u32[]{:S(2)}) %collective-permute-start.8) | collective-permute-done | bytes 40992 | tf_op jit(solution)/shard_map/ppermute | solution.py:381
  41.0 2.0 %collective-permute-done.10 = bf16[5,32,128]{2,1,0:T(8,128)(2,1)S(1)} collective-permute-done((bf16[5,32,128]{2,1,0:T(8,128)(2,1)S(1)}, bf16[5,32,128]{2,1,0:T(8,128)(2,1)S(1)}, u32[]{:S(2)}, u32[]{:S(2)}) %collective-permute-start.10) | collective-permute-done | bytes 40992 | tf_op jit(solution)/shard_map/ppermute | solution.py:381
  43.0 0.9 %collective-permute-done.9 = bf16[5,32,128]{2,1,0:T(8,128)(2,1)S(1)} collective-permute-done((bf16[5,32,128]{2,1,0:T(8,128)(2,1)S(1)}, bf16[5,32,128]{2,1,0:T(8,128)(2,1)S(1)}, u32[]{:S(2)}, u32[]{:S(2)}) %collective-permute-start.9) | collective-permute-done | bytes 40992 | tf_op jit(solution)/shard_map/ppermute | solution.py:381
  44.0 1.6 %collective-permute-start.11 = (bf16[1,5,32,128]{3,2,1,0:T(8,128)(2,1)S(1)}, bf16[1,5,32,128]{3,2,1,0:T(8,128)(2,1)S(1)}, u32[]{:S(2)}, u32[]{:S(2)}) collective-permute-start(bf16[1,5,32,128]{3,2,1,0:T(8,128)(2,1)S(1)} %get-tuple-element.68), channel_id=1, source_target_pairs={{4,0},{0,4},{12,8},{8,12},{20,16},{16,20},{28,24},{24,28},{5,1},{1... | collective-permute-start | bytes 122888 | tf_op jit(solution)/shard_map/ppermute | solution.py:384
  45.5 2.5 %collective-permute-done.11 = bf16[1,5,32,128]{3,2,1,0:T(8,128)(2,1)S(1)} collective-permute-done((bf16[1,5,32,128]{3,2,1,0:T(8,128)(2,1)S(1)}, bf16[1,5,32,128]{3,2,1,0:T(8,128)(2,1)S(1)}, u32[]{:S(2)}, u32[]{:S(2)}) %collective-permute-start.11) | collective-permute-done | bytes 40992 | tf_op jit(solution)/shard_map/ppermute | solution.py:384
  48.0 2.0 %collective-permute-start.14 = (bf16[2,5,32,128]{3,2,1,0:T(8,128)(2,1)S(1)}, bf16[2,5,32,128]{3,2,1,0:T(8,128)(2,1)S(1)}, u32[]{:S(2)}, u32[]{:S(2)}) collective-permute-start(bf16[2,5,32,128]{3,2,1,0:T(8,128)(2,1)S(1)} %constant_dynamic-update-slice_fusion.refs_0_), channel_id=1, source_target_pairs={{24,0},{28,4},{16,8},{20,12},{8,16},{12,20},{0,24},{4,28},{25,1},{... | collective-permute-start | bytes 245768 | tf_op jit(solution)/shard_map/ppermute | solution.py:384
  50.0 1.6 %collective-permute-start.13 = (bf16[2,5,32,128]{3,2,1,0:T(8,128)(2,1)S(1)}, bf16[2,5,32,128]{3,2,1,0:T(8,128)(2,1)S(1)}, u32[]{:S(2)}, u32[]{:S(2)}) collective-permute-start(bf16[2,5,32,128]{3,2,1,0:T(8,128)(2,1)S(1)} %constant_dynamic-update-slice_fusion.refs_0_), channel_id=1, source_target_pairs={{16,0},{20,4},{24,8},{28,12},{0,16},{4,20},{8,24},{12,28},{17,1},{... | collective-permute-start | bytes 245768 | tf_op jit(solution)/shard_map/ppermute | solution.py:384
  51.6 0.9 %collective-permute-start.12 = (bf16[2,5,32,128]{3,2,1,0:T(8,128)(2,1)S(1)}, bf16[2,5,32,128]{3,2,1,0:T(8,128)(2,1)S(1)}, u32[]{:S(2)}, u32[]{:S(2)}) collective-permute-start(bf16[2,5,32,128]{3,2,1,0:T(8,128)(2,1)S(1)} %constant_dynamic-update-slice_fusion.refs_0_), channel_id=1, source_target_pairs={{8,0},{12,4},{0,8},{4,12},{24,16},{28,20},{16,24},{20,28},{9,1},{1... | collective-permute-start | bytes 245768 | tf_op jit(solution)/shard_map/ppermute | solution.py:384
  52.5 0.6 %multiply_add_fusion = f32[5,32,128]{2,1,0:T(8,128)} fusion(f32[5,32,128]{2,1,0:T(8,128)S(1)} %bitcast.25, f32[5,32,128]{2,1,0:T(8,128)S(1)} %get-tuple-element.75), kind=kLoop, calls=%fused_computation.7 | loop fusion | flops 40960 | bytes 245760 | tf_op jit(solution)/shard_map/add | solution.py:435
  53.1 0.0 collective-permute-done.15.refs_3_
  53.1 0.0 copy-done.1
  53.1 0.0 copy-done.3
  53.1 3.6 %hidden_grad.1 = bf16[128,8192]{1,0:T(8,128)(2,1)} custom-call(bf16[128,8192]{1,0:T(8,128)(2,1)S(1)} %copy-done.1, f32[1,8192]{1,0:T(1,128)S(1)} %bitcast.23, bf16[1,128,1024]{2,1,0:T(8,128)(2,1)S(1)} %get-tuple-element.69.refs_0_, bf16[1,128,1024]{2,1,0:T(8,128)(2,1)S(1)} %collective-permute-done.4.refs_1_, ...), custom_call_target="tpu_custom_call" | custom-call | flops 1 | bytes 1 | tf_op jit(solution)/shard_map/hidden_grad/pallas_call | solution.py:268
  56.7 0.0 collective-permute-done.14.refs_3_
  56.7 0.0 collective-permute-done.13.refs_2_
  56.7 0.2 collective-permute-done.12.refs_1_
  56.9 7.6 %unsketch.1 = (f32[2048,512]{1,0:T(8,128)}, f32[5,32,128]{2,1,0:T(8,128)}) custom-call(bf16[2,5,32,128]{3,2,1,0:T(8,128)(2,1)S(1)} %constant_dynamic-update-slice_fusion.refs_0_, bf16[2,5,32,128]{3,2,1,0:T(8,128)(2,1)S(1)} %collective-permute-done.12.refs_1_, bf16[2,5,32,128]{3,2,1,0:T(8,128)(2,1)S(1)} %collective-permute-done.13.refs_2_, ...), custom_call_target="tpu_custom_call" | custom-call | flops 1 | bytes 1 | tf_op jit(solution)/shard_map/unsketch/pallas_call | solution.py:331
  (6 shorter events, 0.1 us)
Async XLA Ops:
  0.6 6.8 %copy-start.2 = (bf16[128,512]{1,0:T(8,128)(2,1)S(1)}, bf16[128,512]{1,0:T(8,128)(2,1)}, u32[]{:S(2)}) copy-start(bf16[128,512]{1,0:T(8,128)(2,1)} %refs_0_.1) | copy-start | bytes 393220
  0.6 9.0 %copy-start = (bf16[2048,512]{1,0:T(8,128)(2,1)S(1)}, bf16[2048,512]{1,0:T(8,128)(2,1)}, u32[]{:S(2)}) copy-start(bf16[2048,512]{1,0:T(8,128)(2,1)} %refs_2_.7) | copy-start | bytes 6291460
  0.7 6.7 %collective-permute-start = (bf16[128,512]{1,0:T(8,128)(2,1)}, bf16[128,512]{1,0:T(8,128)(2,1)S(1)}, u32[]{:S(2)}, u32[]{:S(2)}) collective-permute-start(bf16[128,512]{1,0:T(8,128)(2,1)} %refs_0_.1), channel_id=1, source_target_pairs={{2,0},{3,1},{0,2},{1,3},{6,4},{7,5},{4,6},{5,7},{10,8},{11,9},{8,1... | collective-permute-start | bytes 393224 | tf_op jit(solution)/shard_map/ppermute | solution.py:375
  7.3 5.2 %copy-start.5 = (bf16[2,128,2048]{2,1,0:T(8,128)(2,1)S(1)}, bf16[2,128,2048]{2,1,0:T(8,128)(2,1)}, u32[]{:S(2)}) copy-start(bf16[2,128,2048]{2,1,0:T(8,128)(2,1)} %get-tuple-element.53.refs_0_) | copy-start | bytes 3145732
  7.4 3.1 %collective-permute-start.1 = (bf16[2,128,2048]{2,1,0:T(8,128)(2,1)}, bf16[2,128,2048]{2,1,0:T(8,128)(2,1)S(1)}, u32[]{:S(2)}, u32[]{:S(2)}) collective-permute-start(bf16[2,128,2048]{2,1,0:T(8,128)(2,1)} %get-tuple-element.48), channel_id=1, source_target_pairs={{0,1},{1,0},{2,3},{3,2},{4,5},{5,4},{6,7},{7,6},{8,9},{9,8},{10,11... | collective-permute-start | bytes 3145736 | tf_op jit(solution)/shard_map/ppermute | solution.py:369
  7.4 5.1 %collective-permute-start.2 = (bf16[128,512]{1,0:T(8,128)(2,1)S(1)}, bf16[128,512]{1,0:T(8,128)(2,1)S(1)}, u32[]{:S(2)}, u32[]{:S(2)}) collective-permute-start(bf16[128,512]{1,0:T(8,128)(2,1)S(1)} %copy-done.2), channel_id=1, source_target_pairs={{0,1},{1,0},{2,3},{3,2},{4,5},{5,4},{6,7},{7,6},{8,9},{9,8},{10,11... | collective-permute-start | bytes 393224 | tf_op jit(solution)/shard_map/ppermute | solution.py:369
  7.9 4.7 %collective-permute-start.3 = (bf16[40,1024]{1,0:T(8,128)(2,1)}, bf16[40,1024]{1,0:T(8,128)(2,1)S(1)}, u32[]{:S(2)}, u32[]{:S(2)}) collective-permute-start(bf16[40,1024]{1,0:T(8,128)(2,1)} %get-tuple-element.58), channel_id=1, source_target_pairs={{2,0},{3,1},{0,2},{1,3},{6,4},{7,5},{4,6},{5,7},{10,8},{11,9},{8,1... | collective-permute-start | bytes 245768 | tf_op jit(solution)/shard_map/ppermute | solution.py:375
  10.5 10.3 %copy-start.4 = (bf16[4,8,2048]{2,1,0:T(8,128)(2,1)S(1)}, bf16[4,8,2048]{2,1,0:T(8,128)(2,1)}, u32[]{:S(2)}) copy-start(bf16[4,8,2048]{2,1,0:T(8,128)(2,1)} %get-tuple-element.56.refs_4_) | copy-start | bytes 393220
  10.5 8.4 %collective-permute-start.4 = (bf16[1,128,1024]{2,1,0:T(8,128)(2,1)S(1)}, bf16[1,128,1024]{2,1,0:T(8,128)(2,1)S(1)}, u32[]{:S(2)}, u32[]{:S(2)}) collective-permute-start(bf16[1,128,1024]{2,1,0:T(8,128)(2,1)S(1)} %get-tuple-element.60), channel_id=1, source_target_pairs={{2,0},{3,1},{0,2},{1,3},{6,4},{7,5},{4,6},{5,7},{10,8},{11,9},{8,1... | collective-permute-start | bytes 786440 | tf_op jit(solution)/shard_map/ppermute | solution.py:375
  18.9 8.3 %collective-permute-start.6 = (bf16[2048,512]{1,0:T(8,128)(2,1)S(1)}, bf16[2048,512]{1,0:T(8,128)(2,1)S(1)}, u32[]{:S(2)}, u32[]{:S(2)}) collective-permute-start(bf16[2048,512]{1,0:T(8,128)(2,1)S(1)} %copy-done), channel_id=1, source_target_pairs={{0,1},{1,0},{2,3},{3,2},{4,5},{5,4},{6,7},{7,6},{8,9},{9,8},{10,11... | collective-permute-start | bytes 6291464 | tf_op jit(solution)/shard_map/ppermute | solution.py:369
  19.0 10.1 %collective-permute-start.5 = (bf16[8,5,32,128]{3,2,1,0:T(8,128)(2,1)S(1)}, bf16[8,5,32,128]{3,2,1,0:T(8,128)(2,1)S(1)}, u32[]{:S(2)}, u32[]{:S(2)}) collective-permute-start(bf16[8,5,32,128]{3,2,1,0:T(8,128)(2,1)S(1)} %sketch.3), channel_id=1, source_target_pairs={{2,0},{3,1},{0,2},{1,3},{6,4},{7,5},{4,6},{5,7},{10,8},{11,9},{8,1... | collective-permute-start | bytes 983048 | tf_op jit(solution)/shard_map/ppermute | solution.py:375
  28.2 11.4 %copy-start.6 = (f32[1,5,4096]{2,0,1:T(1,128)S(1)}, f32[1,5,4096]{2,0,1:T(1,128)}, u32[]{:S(2)}) copy-start(f32[1,5,4096]{2,0,1:T(1,128)} %param.14) | copy-start | bytes 245764
  28.2 11.5 %copy-start.7 = (f32[1,5,4096]{2,0,1:T(1,128)S(1)}, f32[1,5,4096]{2,0,1:T(1,128)}, u32[]{:S(2)}) copy-start(f32[1,5,4096]{2,0,1:T(1,128)} %param.15) | copy-start | bytes 245764
  29.1 24.0 %copy-start.1 = (bf16[128,8192]{1,0:T(8,128)(2,1)S(1)}, bf16[128,8192]{1,0:T(8,128)(2,1)}, u32[]{:S(2)}) copy-start(bf16[128,8192]{1,0:T(8,128)(2,1)} %hidden_ref.3) | copy-start | bytes 6291460
  29.1 24.0 %copy-start.3 = (f32[8192]{0:T(1024)S(1)}, f32[8192]{0:T(1024)}, u32[]{:S(2)}) copy-start(f32[8192]{0:T(1024)} %param.9) | copy-start | bytes 98308
  29.3 5.8 %collective-permute-start.7 = (bf16[4,5,32,128]{3,2,1,0:T(8,128)(2,1)S(1)}, bf16[4,5,32,128]{3,2,1,0:T(8,128)(2,1)S(1)}, u32[]{:S(2)}, u32[]{:S(2)}) collective-permute-start(bf16[4,5,32,128]{3,2,1,0:T(8,128)(2,1)S(1)} %slice.43), channel_id=1, source_target_pairs={{0,4},{4,0},{8,12},{12,8},{16,20},{20,16},{24,28},{28,24},{1,5},{5... | collective-permute-start | bytes 491528 | tf_op jit(solution)/shard_map/ppermute | solution.py:381
  31.0 22.1 %collective-permute-start.15 = (bf16[3,128,1024]{2,1,0:T(8,128)(2,1)S(1)}, bf16[3,128,1024]{2,1,0:T(8,128)(2,1)S(1)}, u32[]{:S(2)}, u32[]{:S(2)}) collective-permute-start(bf16[3,128,1024]{2,1,0:T(8,128)(2,1)S(1)} %get-tuple-element.72), channel_id=1, source_target_pairs={{2,0},{3,1},{0,2},{1,3},{6,4},{7,5},{4,6},{5,7},{10,8},{11,9},{8,1... | collective-permute-start | bytes 2359304 | tf_op jit(solution)/shard_map/ppermute | solution.py:375
  35.2 5.9 %collective-permute-start.8 = (bf16[5,32,128]{2,1,0:T(8,128)(2,1)S(1)}, bf16[5,32,128]{2,1,0:T(8,128)(2,1)S(1)}, u32[]{:S(2)}, u32[]{:S(2)}) collective-permute-start(bf16[5,32,128]{2,1,0:T(8,128)(2,1)S(1)} %get-tuple-element.95), channel_id=1, source_target_pairs={{0,24},{4,28},{8,16},{12,20},{16,8},{20,12},{24,0},{28,4},{1,25},{... | collective-permute-start | bytes 122888 | tf_op jit(solution)/shard_map/ppermute | solution.py:381
  39.0 4.0 %collective-permute-start.10 = (bf16[5,32,128]{2,1,0:T(8,128)(2,1)S(1)}, bf16[5,32,128]{2,1,0:T(8,128)(2,1)S(1)}, u32[]{:S(2)}, u32[]{:S(2)}) collective-permute-start(bf16[5,32,128]{2,1,0:T(8,128)(2,1)S(1)} %get-tuple-element.96), channel_id=1, source_target_pairs={{0,8},{4,12},{8,0},{12,4},{16,24},{20,28},{24,16},{28,20},{1,9},{5... | collective-permute-start | bytes 122888 | tf_op jit(solution)/shard_map/ppermute | solution.py:381
  39.0 4.9 %collective-permute-start.9 = (bf16[5,32,128]{2,1,0:T(8,128)(2,1)S(1)}, bf16[5,32,128]{2,1,0:T(8,128)(2,1)S(1)}, u32[]{:S(2)}, u32[]{:S(2)}) collective-permute-start(bf16[5,32,128]{2,1,0:T(8,128)(2,1)S(1)} %get-tuple-element.97), channel_id=1, source_target_pairs={{0,16},{4,20},{8,24},{12,28},{16,0},{20,4},{24,8},{28,12},{1,17},{... | collective-permute-start | bytes 122888 | tf_op jit(solution)/shard_map/ppermute | solution.py:381
  44.0 4.1 %collective-permute-start.11 = (bf16[1,5,32,128]{3,2,1,0:T(8,128)(2,1)S(1)}, bf16[1,5,32,128]{3,2,1,0:T(8,128)(2,1)S(1)}, u32[]{:S(2)}, u32[]{:S(2)}) collective-permute-start(bf16[1,5,32,128]{3,2,1,0:T(8,128)(2,1)S(1)} %get-tuple-element.68), channel_id=1, source_target_pairs={{4,0},{0,4},{12,8},{8,12},{20,16},{16,20},{28,24},{24,28},{5,1},{1... | collective-permute-start | bytes 122888 | tf_op jit(solution)/shard_map/ppermute | solution.py:384
  48.0 8.7 %collective-permute-start.14 = (bf16[2,5,32,128]{3,2,1,0:T(8,128)(2,1)S(1)}, bf16[2,5,32,128]{3,2,1,0:T(8,128)(2,1)S(1)}, u32[]{:S(2)}, u32[]{:S(2)}) collective-permute-start(bf16[2,5,32,128]{3,2,1,0:T(8,128)(2,1)S(1)} %constant_dynamic-update-slice_fusion.refs_0_), channel_id=1, source_target_pairs={{24,0},{28,4},{16,8},{20,12},{8,16},{12,20},{0,24},{4,28},{25,1},{... | collective-permute-start | bytes 245768 | tf_op jit(solution)/shard_map/ppermute | solution.py:384
  50.0 6.7 %collective-permute-start.13 = (bf16[2,5,32,128]{3,2,1,0:T(8,128)(2,1)S(1)}, bf16[2,5,32,128]{3,2,1,0:T(8,128)(2,1)S(1)}, u32[]{:S(2)}, u32[]{:S(2)}) collective-permute-start(bf16[2,5,32,128]{3,2,1,0:T(8,128)(2,1)S(1)} %constant_dynamic-update-slice_fusion.refs_0_), channel_id=1, source_target_pairs={{16,0},{20,4},{24,8},{28,12},{0,16},{4,20},{8,24},{12,28},{17,1},{... | collective-permute-start | bytes 245768 | tf_op jit(solution)/shard_map/ppermute | solution.py:384
  51.6 5.3 %collective-permute-start.12 = (bf16[2,5,32,128]{3,2,1,0:T(8,128)(2,1)S(1)}, bf16[2,5,32,128]{3,2,1,0:T(8,128)(2,1)S(1)}, u32[]{:S(2)}, u32[]{:S(2)}) collective-permute-start(bf16[2,5,32,128]{3,2,1,0:T(8,128)(2,1)S(1)} %constant_dynamic-update-slice_fusion.refs_0_), channel_id=1, source_target_pairs={{8,0},{12,4},{0,8},{4,12},{24,16},{28,20},{16,24},{20,28},{9,1},{1... | collective-permute-start | bytes 245768 | tf_op jit(solution)/shard_map/ppermute | solution.py:384

commit v5 on v4

--- a/solution.py
+++ b/solution.py
@@ -394,6 +394,7 @@
     cots, weights = [key_cotangent], [key_weight]
     if pair == 2:
         inputs[1] = across(inputs[1])
+        inputs, cotangent = lax.optimization_barrier((inputs, cotangent))
         cots.append(across(cotangent))
     first_half, *halves = [(other, half) for other in range(pair) for half in range(HALVES)]
     back = range(turns - 1, 0, -1)

time: 64.7 us -> 67.9 us (1.049)
  waiting for transfers between devices: 11.1 us -> 15.4 us
  starting transfers between devices: 22.6 us -> 21.5 us
    ppermute x3, waiting for transfers between devices: 0.36 us -> 2.86 us  [across(): return lax.ppermute(value, 'fsdp', [(i, i ^ 1) for i in range(fsdp_count)])]
    ppermute x5, waiting for transfers between devices: 1.3 us -> 3.2 us  [from_turn(): return lax.ppermute(value, 'fsdp', pairs)]
  transfers between devices with their start and end apart: 16 -> 16, of which waited for: 9 -> 9; matrix products, arithmetic and copies ran while one was open for 1% -> 1% of each run, Pallas kernels for 33% -> 32%
where the time goes in v5:
time: 67.9 us; the launch traced here: 67.8 us
  Pallas kernels  29 us (43%)
  starting transfers between devices  21.5 us (32%)
  waiting for transfers between devices  15.4 us (23%)
  other arithmetic  0.92 us (1%)
  between operations  0.8 us (1%)
    pallas_call x2, Pallas kernels, sketch(): pl.pallas_call(functools.partial(sketch_kernel, scale, count, near, pair,...  12.7 us
    ppermute x5, starting transfers between devices, from_turn(): return lax.ppermute(value, 'fsdp', pairs)  9.23 us
    pallas_call x1, Pallas kernels, unsketch(): pl.pallas_call(functools.partial(unsketch_kernel, groups, share), out_sha...  7.61 us
    ppermute x4, waiting for transfers between devices, to_share(): lax.ppermute(value, 'dp', [(i, partner(i, step, dp_count)) for i in range...  6.67 us
    ppermute x4, starting transfers between devices, to_share(): lax.ppermute(value, 'dp', [(i, partner(i, step, dp_count)) for i in range...  6.01 us
    ppermute x4, starting transfers between devices, from_share(): lax.ppermute(value, 'dp', [(partner(i, step, dp_count), i) for i in range...  6 us
    pallas_call x1, Pallas kernels, front(): pl.pallas_call(functools.partial(front_kernel, wrap, pair, turns), out_sh...  3.66 us
    pallas_call x1, Pallas kernels, backward(): pl.pallas_call(functools.partial(backward_kernel, turns, pair, pieces), o...  3.56 us
  transfers between devices with their start and end apart: 16, of which 9 were waited for; matrix products, arithmetic and copies ran while one was open for 1% of the time, Pallas kernels for 32%

profile of v5, /device:TPU:0, one launch (start us, length us, event | category | flops | bytes accessed | tf_op | source)
XLA Modules:
  0.0 67.8 jit_solution(6352886990384865801)
XLA Ops:
  0.6 0.0 copy-start.2
  0.6 0.0 copy-start
  0.7 3.0 %collective-permute-start = (bf16[128,512]{1,0:T(8,128)(2,1)}, bf16[128,512]{1,0:T(8,128)(2,1)S(1)}, u32[]{:S(2)}, u32[]{:S(2)}) collective-permute-start(bf16[128,512]{1,0:T(8,128)(2,1)} %refs_0_.1), channel_id=1, source_target_pairs={{2,0},{3,1},{0,2},{1,3},{6,4},{7,5},{4,6},{5,7},{10,8},{11,9},{8,1... | collective-permute-start | bytes 393224 | tf_op jit(solution)/shard_map/ppermute | solution.py:375
  3.7 3.7 %codes_and_normed.1 = (bf16[4,8,2048]{2,1,0:T(8,128)(2,1)}, bf16[40,1024]{1,0:T(8,128)(2,1)}, bf16[2,128,2048]{2,1,0:T(8,128)(2,1)}, bf16[2,128,2048]{2,1,0:T(8,128)(2,1)}) custom-call(s32[5,8192]{1,0:T(8,128)} %bucket_ref.1, s32[5,8192]{1,0:T(8,128)} %sign_ref.1, bf16[128,8192]{1,0:T(8,128)(2,1)} %hidden_ref.3, f32[1,8192]{1,0:T(1,128)} %bitcast.22), custom_call_target="tpu_custom_call" | custom-call | flops 1 | bytes 1 | tf_op jit(solution)/shard_map/codes_and_normed/pallas_call | solution.py:108
  7.3 0.0 copy-start.5
  7.3 0.0 collective-permute-done.refs_1_
  7.4 0.0 collective-permute-start.1
  7.4 2.9 %collective-permute-done.1.refs_1_ = bf16[2,128,2048]{2,1,0:T(8,128)(2,1)S(1)} collective-permute-done((bf16[2,128,2048]{2,1,0:T(8,128)(2,1)}, bf16[2,128,2048]{2,1,0:T(8,128)(2,1)S(1)}, u32[]{:S(2)}, u32[]{:S(2)}) %collective-permute-start.1) | collective-permute-done | bytes 1048608 | tf_op jit(solution)/shard_map/ppermute | solution.py:369
  10.3 0.0 copy-done.2
  10.3 0.1 collective-permute-start.2
  10.4 1.7 %collective-permute-start.3 = (bf16[40,1024]{1,0:T(8,128)(2,1)}, bf16[40,1024]{1,0:T(8,128)(2,1)S(1)}, u32[]{:S(2)}, u32[]{:S(2)}) collective-permute-start(bf16[40,1024]{1,0:T(8,128)(2,1)} %get-tuple-element.64), channel_id=1, source_target_pairs={{2,0},{3,1},{0,2},{1,3},{6,4},{7,5},{4,6},{5,7},{10,8},{11,9},{8,1... | collective-permute-start | bytes 245768 | tf_op jit(solution)/shard_map/ppermute | solution.py:375
  12.2 0.0 copy-done
  12.2 0.5 input_grad.2
  12.6 0.0 copy-start.4
  12.6 0.4 collective-permute-start.4
  13.0 2.3 %collective-permute-done.3.refs_4_ = bf16[40,1024]{1,0:T(8,128)(2,1)S(1)} collective-permute-done((bf16[40,1024]{1,0:T(8,128)(2,1)}, bf16[40,1024]{1,0:T(8,128)(2,1)S(1)}, u32[]{:S(2)}, u32[]{:S(2)}) %collective-permute-start.3) | collective-permute-done | bytes 81952 | tf_op jit(solution)/shard_map/ppermute | solution.py:375
  15.4 0.0 collective-permute-done.2.refs_3_
  15.4 0.0 copy-done.5
  15.4 6.3 %sketch.3 = bf16[8,5,32,128]{3,2,1,0:T(8,128)(2,1)S(1)} custom-call(bf16[2,128,2048]{2,1,0:T(8,128)(2,1)S(1)} %copy-done.5, bf16[2,128,2048]{2,1,0:T(8,128)(2,1)S(1)} %collective-permute-done.1.refs_1_, bf16[128,512]{1,0:T(8,128)(2,1)S(1)} %copy-done.2, bf16[128,512]{1,0:T(8,128)(2,1)S(1)} %collective-permute-done.2.refs_3_, ...), custom_call_target="tpu_custom_call" | custom-call | flops 5368709120 | bytes 2097152 | tf_op jit(solution)/shard_map/sketch/pallas_call | solution.py:184
  21.7 0.0 collective-permute-done.4.refs_1_
  21.7 0.1 collective-permute-start.6
  21.8 2.3 %collective-permute-start.5 = (bf16[8,5,32,128]{3,2,1,0:T(8,128)(2,1)S(1)}, bf16[8,5,32,128]{3,2,1,0:T(8,128)(2,1)S(1)}, u32[]{:S(2)}, u32[]{:S(2)}) collective-permute-start(bf16[8,5,32,128]{3,2,1,0:T(8,128)(2,1)S(1)} %sketch.3), channel_id=1, source_target_pairs={{2,0},{3,1},{0,2},{1,3},{6,4},{7,5},{4,6},{5,7},{10,8},{11,9},{8,1... | collective-permute-start | bytes 983048 | tf_op jit(solution)/shard_map/ppermute | solution.py:375
  24.1 0.0 copy-done.4
  24.1 6.4 %sketch.2 = bf16[8,5,32,128]{3,2,1,0:T(8,128)(2,1)S(1)} custom-call(bf16[2,128,2048]{2,1,0:T(8,128)(2,1)S(1)} %copy-done.5, bf16[2,128,2048]{2,1,0:T(8,128)(2,1)S(1)} %collective-permute-done.1.refs_1_, bf16[128,512]{1,0:T(8,128)(2,1)S(1)} %copy-done.2, bf16[128,512]{1,0:T(8,128)(2,1)S(1)} %collective-permute-done.2.refs_3_, bf16[4,8,2048]{2,1,0:T(8,128)(2,1)S(1)} %copy-done.4), custom_call_target="tpu_custom_call" | custom-call | flops 5368709120 | bytes 2097152 | tf_op jit(solution)/shard_map/sketch/pallas_call | solution.py:184
  30.5 0.0 collective-permute-done.6.refs_3_.refs_4_
  30.5 1.0 %input_grad.3 = (bf16[3,128,1024]{2,1,0:T(8,128)(2,1)S(1)}, bf16[3,128,1024]{2,1,0:T(8,128)(2,1)S(1)}) custom-call(bf16[128,512]{1,0:T(8,128)(2,1)S(1)} %copy-done.2, bf16[128,512]{1,0:T(8,128)(2,1)S(1)} %collective-permute-done.refs_1_, bf16[2048,512]{1,0:T(8,128)(2,1)S(1)} %copy-done, bf16[2048,512]{1,0:T(8,128)(2,1)S(1)} %collective-permute-done.6.refs_3_.refs_4_, ...), custom_call_target="tpu_custom_call" | custom-call | flops 1 | bytes 1 | tf_op jit(solution)/shard_map/input_grad/pallas_call | solution.py:219
  31.6 0.0 copy-start.6
  31.6 0.0 copy-start.7
  31.6 0.8 %collective-permute-done.5 = bf16[8,5,32,128]{3,2,1,0:T(8,128)(2,1)S(1)} collective-permute-done((bf16[8,5,32,128]{3,2,1,0:T(8,128)(2,1)S(1)}, bf16[8,5,32,128]{3,2,1,0:T(8,128)(2,1)S(1)}, u32[]{:S(2)}, u32[]{:S(2)}) %collective-permute-start.5) | collective-permute-done | bytes 327712 | tf_op jit(solution)/shard_map/ppermute | solution.py:375
  32.4 0.0 copy-start.1
  32.4 0.0 copy-start.3
  32.4 0.1 convert_add_fusion
  32.5 1.6 %collective-permute-start.7 = (bf16[4,5,32,128]{3,2,1,0:T(8,128)(2,1)S(1)}, bf16[4,5,32,128]{3,2,1,0:T(8,128)(2,1)S(1)}, u32[]{:S(2)}, u32[]{:S(2)}) collective-permute-start(bf16[4,5,32,128]{3,2,1,0:T(8,128)(2,1)S(1)} %slice.43), channel_id=1, source_target_pairs={{0,4},{4,0},{8,12},{12,8},{16,20},{20,16},{24,28},{28,24},{1,5},{5... | collective-permute-start | bytes 491528 | tf_op jit(solution)/shard_map/ppermute | solution.py:381
  34.1 1.8 %collective-permute-start.15 = (bf16[3,128,1024]{2,1,0:T(8,128)(2,1)S(1)}, bf16[3,128,1024]{2,1,0:T(8,128)(2,1)S(1)}, u32[]{:S(2)}, u32[]{:S(2)}) collective-permute-start(bf16[3,128,1024]{2,1,0:T(8,128)(2,1)S(1)} %get-tuple-element.78), channel_id=1, source_target_pairs={{2,0},{3,1},{0,2},{1,3},{6,4},{7,5},{4,6},{5,7},{10,8},{11,9},{8,1... | collective-permute-start | bytes 2359304 | tf_op jit(solution)/shard_map/ppermute | solution.py:375
  35.9 2.7 %collective-permute-done.7 = bf16[4,5,32,128]{3,2,1,0:T(8,128)(2,1)S(1)} collective-permute-done((bf16[4,5,32,128]{3,2,1,0:T(8,128)(2,1)S(1)}, bf16[4,5,32,128]{3,2,1,0:T(8,128)(2,1)S(1)}, u32[]{:S(2)}, u32[]{:S(2)}) %collective-permute-start.7) | collective-permute-done | bytes 163872 | tf_op jit(solution)/shard_map/ppermute | solution.py:381
  38.6 0.1 fusion.4
  38.6 3.6 %collective-permute-start.8 = (bf16[5,32,128]{2,1,0:T(8,128)(2,1)S(1)}, bf16[5,32,128]{2,1,0:T(8,128)(2,1)S(1)}, u32[]{:S(2)}, u32[]{:S(2)}) collective-permute-start(bf16[5,32,128]{2,1,0:T(8,128)(2,1)S(1)} %get-tuple-element.101), channel_id=1, source_target_pairs={{0,24},{4,28},{8,16},{12,20},{16,8},{20,12},{24,0},{28,4},{1,25},{... | collective-permute-start | bytes 122888 | tf_op jit(solution)/shard_map/ppermute | solution.py:381
  42.3 0.0 collective-permute-start.10
  42.3 0.8 %collective-permute-start.9 = (bf16[5,32,128]{2,1,0:T(8,128)(2,1)S(1)}, bf16[5,32,128]{2,1,0:T(8,128)(2,1)S(1)}, u32[]{:S(2)}, u32[]{:S(2)}) collective-permute-start(bf16[5,32,128]{2,1,0:T(8,128)(2,1)S(1)} %get-tuple-element.103), channel_id=1, source_target_pairs={{0,16},{4,20},{8,24},{12,28},{16,0},{20,4},{24,8},{28,12},{1,17},{... | collective-permute-start | bytes 122888 | tf_op jit(solution)/shard_map/ppermute | solution.py:381
  43.1 0.0 copy-done.6
  43.1 0.1 broadcast_multiply_fusion
  43.2 0.0 copy-done.7
  43.2 1.3 %collective-permute-done.8 = bf16[5,32,128]{2,1,0:T(8,128)(2,1)S(1)} collective-permute-done((bf16[5,32,128]{2,1,0:T(8,128)(2,1)S(1)}, bf16[5,32,128]{2,1,0:T(8,128)(2,1)S(1)}, u32[]{:S(2)}, u32[]{:S(2)}) %collective-permute-start.8) | collective-permute-done | bytes 40992 | tf_op jit(solution)/shard_map/ppermute | solution.py:381
  44.5 1.8 %collective-permute-done.10 = bf16[5,32,128]{2,1,0:T(8,128)(2,1)S(1)} collective-permute-done((bf16[5,32,128]{2,1,0:T(8,128)(2,1)S(1)}, bf16[5,32,128]{2,1,0:T(8,128)(2,1)S(1)}, u32[]{:S(2)}, u32[]{:S(2)}) %collective-permute-start.10) | collective-permute-done | bytes 40992 | tf_op jit(solution)/shard_map/ppermute | solution.py:381
  46.3 0.9 %collective-permute-done.9 = bf16[5,32,128]{2,1,0:T(8,128)(2,1)S(1)} collective-permute-done((bf16[5,32,128]{2,1,0:T(8,128)(2,1)S(1)}, bf16[5,32,128]{2,1,0:T(8,128)(2,1)S(1)}, u32[]{:S(2)}, u32[]{:S(2)}) %collective-permute-start.9) | collective-permute-done | bytes 40992 | tf_op jit(solution)/shard_map/ppermute | solution.py:381
  47.2 1.6 %collective-permute-start.11 = (bf16[1,5,32,128]{3,2,1,0:T(8,128)(2,1)S(1)}, bf16[1,5,32,128]{3,2,1,0:T(8,128)(2,1)S(1)}, u32[]{:S(2)}, u32[]{:S(2)}) collective-permute-start(bf16[1,5,32,128]{3,2,1,0:T(8,128)(2,1)S(1)} %get-tuple-element.74), channel_id=1, source_target_pairs={{4,0},{0,4},{12,8},{8,12},{20,16},{16,20},{28,24},{24,28},{5,1},{1... | collective-permute-start | bytes 122888 | tf_op jit(solution)/shard_map/ppermute | solution.py:384
  48.8 2.5 %collective-permute-done.11 = bf16[1,5,32,128]{3,2,1,0:T(8,128)(2,1)S(1)} collective-permute-done((bf16[1,5,32,128]{3,2,1,0:T(8,128)(2,1)S(1)}, bf16[1,5,32,128]{3,2,1,0:T(8,128)(2,1)S(1)}, u32[]{:S(2)}, u32[]{:S(2)}) %collective-permute-start.11) | collective-permute-done | bytes 40992 | tf_op jit(solution)/shard_map/ppermute | solution.py:384
  51.3 2.0 %collective-permute-start.14 = (bf16[2,5,32,128]{3,2,1,0:T(8,128)(2,1)S(1)}, bf16[2,5,32,128]{3,2,1,0:T(8,128)(2,1)S(1)}, u32[]{:S(2)}, u32[]{:S(2)}) collective-permute-start(bf16[2,5,32,128]{3,2,1,0:T(8,128)(2,1)S(1)} %constant_dynamic-update-slice_fusion.refs_0_), channel_id=1, source_target_pairs={{24,0},{28,4},{16,8},{20,12},{8,16},{12,20},{0,24},{4,28},{25,1},{... | collective-permute-start | bytes 245768 | tf_op jit(solution)/shard_map/ppermute | solution.py:384
  53.3 1.6 %collective-permute-start.13 = (bf16[2,5,32,128]{3,2,1,0:T(8,128)(2,1)S(1)}, bf16[2,5,32,128]{3,2,1,0:T(8,128)(2,1)S(1)}, u32[]{:S(2)}, u32[]{:S(2)}) collective-permute-start(bf16[2,5,32,128]{3,2,1,0:T(8,128)(2,1)S(1)} %constant_dynamic-update-slice_fusion.refs_0_), channel_id=1, source_target_pairs={{16,0},{20,4},{24,8},{28,12},{0,16},{4,20},{8,24},{12,28},{17,1},{... | collective-permute-start | bytes 245768 | tf_op jit(solution)/shard_map/ppermute | solution.py:384
  54.8 0.9 %collective-permute-start.12 = (bf16[2,5,32,128]{3,2,1,0:T(8,128)(2,1)S(1)}, bf16[2,5,32,128]{3,2,1,0:T(8,128)(2,1)S(1)}, u32[]{:S(2)}, u32[]{:S(2)}) collective-permute-start(bf16[2,5,32,128]{3,2,1,0:T(8,128)(2,1)S(1)} %constant_dynamic-update-slice_fusion.refs_0_), channel_id=1, source_target_pairs={{8,0},{12,4},{0,8},{4,12},{24,16},{28,20},{16,24},{20,28},{9,1},{1... | collective-permute-start | bytes 245768 | tf_op jit(solution)/shard_map/ppermute | solution.py:384
  55.7 0.6 multiply_add_fusion
  56.4 0.0 collective-permute-done.15.refs_3_
  56.4 0.0 copy-done.1
  56.4 0.0 copy-done.3
  56.4 3.6 %hidden_grad.1 = bf16[128,8192]{1,0:T(8,128)(2,1)} custom-call(bf16[128,8192]{1,0:T(8,128)(2,1)S(1)} %copy-done.1, f32[1,8192]{1,0:T(1,128)S(1)} %bitcast.23, bf16[1,128,1024]{2,1,0:T(8,128)(2,1)S(1)} %get-tuple-element.75.refs_0_, bf16[1,128,1024]{2,1,0:T(8,128)(2,1)S(1)} %collective-permute-done.4.refs_1_, ...), custom_call_target="tpu_custom_call" | custom-call | flops 1 | bytes 1 | tf_op jit(solution)/shard_map/hidden_grad/pallas_call | solution.py:268
  60.0 0.0 collective-permute-done.14.refs_3_
  60.0 0.0 collective-permute-done.13.refs_2_
  60.0 0.2 collective-permute-done.12.refs_1_
  60.2 7.6 %unsketch.1 = (f32[2048,512]{1,0:T(8,128)}, f32[5,32,128]{2,1,0:T(8,128)}) custom-call(bf16[2,5,32,128]{3,2,1,0:T(8,128)(2,1)S(1)} %constant_dynamic-update-slice_fusion.refs_0_, bf16[2,5,32,128]{3,2,1,0:T(8,128)(2,1)S(1)} %collective-permute-done.12.refs_1_, bf16[2,5,32,128]{3,2,1,0:T(8,128)(2,1)S(1)} %collective-permute-done.13.refs_2_, ...), custom_call_target="tpu_custom_call" | custom-call | flops 1 | bytes 1 | tf_op jit(solution)/shard_map/unsketch/pallas_call | solution.py:331
  (6 shorter events, 0.1 us)
Async XLA Ops:
  0.6 9.7 %copy-start.2 = (bf16[128,512]{1,0:T(8,128)(2,1)S(1)}, bf16[128,512]{1,0:T(8,128)(2,1)}, u32[]{:S(2)}) copy-start(bf16[128,512]{1,0:T(8,128)(2,1)} %refs_0_.1) | copy-start | bytes 393220
  0.6 11.5 %copy-start = (bf16[2048,512]{1,0:T(8,128)(2,1)S(1)}, bf16[2048,512]{1,0:T(8,128)(2,1)}, u32[]{:S(2)}) copy-start(bf16[2048,512]{1,0:T(8,128)(2,1)} %refs_2_.7) | copy-start | bytes 6291460
  0.7 6.7 %collective-permute-start = (bf16[128,512]{1,0:T(8,128)(2,1)}, bf16[128,512]{1,0:T(8,128)(2,1)S(1)}, u32[]{:S(2)}, u32[]{:S(2)}) collective-permute-start(bf16[128,512]{1,0:T(8,128)(2,1)} %refs_0_.1), channel_id=1, source_target_pairs={{2,0},{3,1},{0,2},{1,3},{6,4},{7,5},{4,6},{5,7},{10,8},{11,9},{8,1... | collective-permute-start | bytes 393224 | tf_op jit(solution)/shard_map/ppermute | solution.py:375
  7.3 8.0 %copy-start.5 = (bf16[2,128,2048]{2,1,0:T(8,128)(2,1)S(1)}, bf16[2,128,2048]{2,1,0:T(8,128)(2,1)}, u32[]{:S(2)}) copy-start(bf16[2,128,2048]{2,1,0:T(8,128)(2,1)} %get-tuple-element.59.refs_0_) | copy-start | bytes 3145732
  7.4 2.9 %collective-permute-start.1 = (bf16[2,128,2048]{2,1,0:T(8,128)(2,1)}, bf16[2,128,2048]{2,1,0:T(8,128)(2,1)S(1)}, u32[]{:S(2)}, u32[]{:S(2)}) collective-permute-start(bf16[2,128,2048]{2,1,0:T(8,128)(2,1)} %get-tuple-element.51), channel_id=1, source_target_pairs={{0,1},{1,0},{2,3},{3,2},{4,5},{5,4},{6,7},{7,6},{8,9},{9,8},{10,11... | collective-permute-start | bytes 3145736 | tf_op jit(solution)/shard_map/ppermute | solution.py:369
  10.3 5.1 %collective-permute-start.2 = (bf16[128,512]{1,0:T(8,128)(2,1)S(1)}, bf16[128,512]{1,0:T(8,128)(2,1)S(1)}, u32[]{:S(2)}, u32[]{:S(2)}) collective-permute-start(bf16[128,512]{1,0:T(8,128)(2,1)S(1)} %copy-done.2), channel_id=1, source_target_pairs={{0,1},{1,0},{2,3},{3,2},{4,5},{5,4},{6,7},{7,6},{8,9},{9,8},{10,11... | collective-permute-start | bytes 393224 | tf_op jit(solution)/shard_map/ppermute | solution.py:369
  10.4 4.9 %collective-permute-start.3 = (bf16[40,1024]{1,0:T(8,128)(2,1)}, bf16[40,1024]{1,0:T(8,128)(2,1)S(1)}, u32[]{:S(2)}, u32[]{:S(2)}) collective-permute-start(bf16[40,1024]{1,0:T(8,128)(2,1)} %get-tuple-element.64), channel_id=1, source_target_pairs={{2,0},{3,1},{0,2},{1,3},{6,4},{7,5},{4,6},{5,7},{10,8},{11,9},{8,1... | collective-permute-start | bytes 245768 | tf_op jit(solution)/shard_map/ppermute | solution.py:375
  12.6 11.5 %copy-start.4 = (bf16[4,8,2048]{2,1,0:T(8,128)(2,1)S(1)}, bf16[4,8,2048]{2,1,0:T(8,128)(2,1)}, u32[]{:S(2)}) copy-start(bf16[4,8,2048]{2,1,0:T(8,128)(2,1)} %get-tuple-element.62.refs_4_) | copy-start | bytes 393220
  12.6 9.0 %collective-permute-start.4 = (bf16[1,128,1024]{2,1,0:T(8,128)(2,1)S(1)}, bf16[1,128,1024]{2,1,0:T(8,128)(2,1)S(1)}, u32[]{:S(2)}, u32[]{:S(2)}) collective-permute-start(bf16[1,128,1024]{2,1,0:T(8,128)(2,1)S(1)} %get-tuple-element.66), channel_id=1, source_target_pairs={{2,0},{3,1},{0,2},{1,3},{6,4},{7,5},{4,6},{5,7},{10,8},{11,9},{8,1... | collective-permute-start | bytes 786440 | tf_op jit(solution)/shard_map/ppermute | solution.py:375
  21.7 8.8 %collective-permute-start.6 = (bf16[2048,512]{1,0:T(8,128)(2,1)S(1)}, bf16[2048,512]{1,0:T(8,128)(2,1)S(1)}, u32[]{:S(2)}, u32[]{:S(2)}) collective-permute-start(bf16[2048,512]{1,0:T(8,128)(2,1)S(1)} %copy-done), channel_id=1, source_target_pairs={{0,1},{1,0},{2,3},{3,2},{4,5},{5,4},{6,7},{7,6},{8,9},{9,8},{10,11... | collective-permute-start | bytes 6291464 | tf_op jit(solution)/shard_map/ppermute | solution.py:369
  21.8 10.6 %collective-permute-start.5 = (bf16[8,5,32,128]{3,2,1,0:T(8,128)(2,1)S(1)}, bf16[8,5,32,128]{3,2,1,0:T(8,128)(2,1)S(1)}, u32[]{:S(2)}, u32[]{:S(2)}) collective-permute-start(bf16[8,5,32,128]{3,2,1,0:T(8,128)(2,1)S(1)} %sketch.3), channel_id=1, source_target_pairs={{2,0},{3,1},{0,2},{1,3},{6,4},{7,5},{4,6},{5,7},{10,8},{11,9},{8,1... | collective-permute-start | bytes 983048 | tf_op jit(solution)/shard_map/ppermute | solution.py:375
  31.6 11.5 %copy-start.6 = (f32[1,5,4096]{2,0,1:T(1,128)S(1)}, f32[1,5,4096]{2,0,1:T(1,128)}, u32[]{:S(2)}) copy-start(f32[1,5,4096]{2,0,1:T(1,128)} %param.14) | copy-start | bytes 245764
  31.6 11.6 %copy-start.7 = (f32[1,5,4096]{2,0,1:T(1,128)S(1)}, f32[1,5,4096]{2,0,1:T(1,128)}, u32[]{:S(2)}) copy-start(f32[1,5,4096]{2,0,1:T(1,128)} %param.15) | copy-start | bytes 245764
  32.4 24.0 %copy-start.1 = (bf16[128,8192]{1,0:T(8,128)(2,1)S(1)}, bf16[128,8192]{1,0:T(8,128)(2,1)}, u32[]{:S(2)}) copy-start(bf16[128,8192]{1,0:T(8,128)(2,1)} %hidden_ref.3) | copy-start | bytes 6291460
  32.4 24.0 %copy-start.3 = (f32[8192]{0:T(1024)S(1)}, f32[8192]{0:T(1024)}, u32[]{:S(2)}) copy-start(f32[8192]{0:T(1024)} %param.9) | copy-start | bytes 98308
  32.5 6.0 %collective-permute-start.7 = (bf16[4,5,32,128]{3,2,1,0:T(8,128)(2,1)S(1)}, bf16[4,5,32,128]{3,2,1,0:T(8,128)(2,1)S(1)}, u32[]{:S(2)}, u32[]{:S(2)}) collective-permute-start(bf16[4,5,32,128]{3,2,1,0:T(8,128)(2,1)S(1)} %slice.43), channel_id=1, source_target_pairs={{0,4},{4,0},{8,12},{12,8},{16,20},{20,16},{24,28},{28,24},{1,5},{5... | collective-permute-start | bytes 491528 | tf_op jit(solution)/shard_map/ppermute | solution.py:381
  34.1 22.3 %collective-permute-start.15 = (bf16[3,128,1024]{2,1,0:T(8,128)(2,1)S(1)}, bf16[3,128,1024]{2,1,0:T(8,128)(2,1)S(1)}, u32[]{:S(2)}, u32[]{:S(2)}) collective-permute-start(bf16[3,128,1024]{2,1,0:T(8,128)(2,1)S(1)} %get-tuple-element.78), channel_id=1, source_target_pairs={{2,0},{3,1},{0,2},{1,3},{6,4},{7,5},{4,6},{5,7},{10,8},{11,9},{8,1... | collective-permute-start | bytes 2359304 | tf_op jit(solution)/shard_map/ppermute | solution.py:375
  38.6 5.9 %collective-permute-start.8 = (bf16[5,32,128]{2,1,0:T(8,128)(2,1)S(1)}, bf16[5,32,128]{2,1,0:T(8,128)(2,1)S(1)}, u32[]{:S(2)}, u32[]{:S(2)}) collective-permute-start(bf16[5,32,128]{2,1,0:T(8,128)(2,1)S(1)} %get-tuple-element.101), channel_id=1, source_target_pairs={{0,24},{4,28},{8,16},{12,20},{16,8},{20,12},{24,0},{28,4},{1,25},{... | collective-permute-start | bytes 122888 | tf_op jit(solution)/shard_map/ppermute | solution.py:381
  42.3 4.0 %collective-permute-start.10 = (bf16[5,32,128]{2,1,0:T(8,128)(2,1)S(1)}, bf16[5,32,128]{2,1,0:T(8,128)(2,1)S(1)}, u32[]{:S(2)}, u32[]{:S(2)}) collective-permute-start(bf16[5,32,128]{2,1,0:T(8,128)(2,1)S(1)} %get-tuple-element.102), channel_id=1, source_target_pairs={{0,8},{4,12},{8,0},{12,4},{16,24},{20,28},{24,16},{28,20},{1,9},{5... | collective-permute-start | bytes 122888 | tf_op jit(solution)/shard_map/ppermute | solution.py:381
  42.3 4.9 %collective-permute-start.9 = (bf16[5,32,128]{2,1,0:T(8,128)(2,1)S(1)}, bf16[5,32,128]{2,1,0:T(8,128)(2,1)S(1)}, u32[]{:S(2)}, u32[]{:S(2)}) collective-permute-start(bf16[5,32,128]{2,1,0:T(8,128)(2,1)S(1)} %get-tuple-element.103), channel_id=1, source_target_pairs={{0,16},{4,20},{8,24},{12,28},{16,0},{20,4},{24,8},{28,12},{1,17},{... | collective-permute-start | bytes 122888 | tf_op jit(solution)/shard_map/ppermute | solution.py:381
  47.2 4.1 %collective-permute-start.11 = (bf16[1,5,32,128]{3,2,1,0:T(8,128)(2,1)S(1)}, bf16[1,5,32,128]{3,2,1,0:T(8,128)(2,1)S(1)}, u32[]{:S(2)}, u32[]{:S(2)}) collective-permute-start(bf16[1,5,32,128]{3,2,1,0:T(8,128)(2,1)S(1)} %get-tuple-element.74), channel_id=1, source_target_pairs={{4,0},{0,4},{12,8},{8,12},{20,16},{16,20},{28,24},{24,28},{5,1},{1... | collective-permute-start | bytes 122888 | tf_op jit(solution)/shard_map/ppermute | solution.py:384
  51.3 8.7 %collective-permute-start.14 = (bf16[2,5,32,128]{3,2,1,0:T(8,128)(2,1)S(1)}, bf16[2,5,32,128]{3,2,1,0:T(8,128)(2,1)S(1)}, u32[]{:S(2)}, u32[]{:S(2)}) collective-permute-start(bf16[2,5,32,128]{3,2,1,0:T(8,128)(2,1)S(1)} %constant_dynamic-update-slice_fusion.refs_0_), channel_id=1, source_target_pairs={{24,0},{28,4},{16,8},{20,12},{8,16},{12,20},{0,24},{4,28},{25,1},{... | collective-permute-start | bytes 245768 | tf_op jit(solution)/shard_map/ppermute | solution.py:384
  53.3 6.7 %collective-permute-start.13 = (bf16[2,5,32,128]{3,2,1,0:T(8,128)(2,1)S(1)}, bf16[2,5,32,128]{3,2,1,0:T(8,128)(2,1)S(1)}, u32[]{:S(2)}, u32[]{:S(2)}) collective-permute-start(bf16[2,5,32,128]{3,2,1,0:T(8,128)(2,1)S(1)} %constant_dynamic-update-slice_fusion.refs_0_), channel_id=1, source_target_pairs={{16,0},{20,4},{24,8},{28,12},{0,16},{4,20},{8,24},{12,28},{17,1},{... | collective-permute-start | bytes 245768 | tf_op jit(solution)/shard_map/ppermute | solution.py:384
  54.8 5.3 %collective-permute-start.12 = (bf16[2,5,32,128]{3,2,1,0:T(8,128)(2,1)S(1)}, bf16[2,5,32,128]{3,2,1,0:T(8,128)(2,1)S(1)}, u32[]{:S(2)}, u32[]{:S(2)}) collective-permute-start(bf16[2,5,32,128]{3,2,1,0:T(8,128)(2,1)S(1)} %constant_dynamic-update-slice_fusion.refs_0_), channel_id=1, source_target_pairs={{8,0},{12,4},{0,8},{4,12},{24,16},{28,20},{16,24},{20,28},{9,1},{1... | collective-permute-start | bytes 245768 | tf_op jit(solution)/shard_map/ppermute | solution.py:384
